TPU v7x, 32 devices: a whole 2x2x4 slice. The times are simulated.
32 devices in a mesh: slot: 4 (over y, x), mp: 4 (over z), dp: 2 (over core).
Axes of the slice: x: 2, y: 2, z: 4, core: 2. Of those that a mesh axis runs over, the one named last changes fastest.
Arguments:
- byte_ids: int32 [2, 4096, 8], P(None, 'dp'), may hold values from 0 to 255
- item_ids: int32 [2, 2, 2048], P(None, 'dp'), may hold values from 0 to 4, never falling along the last dimension, each value on 1 to 1024 neighbouring positions
- loss_mask: int32 [2, 4096, 8], P(None, 'dp'), may hold values from 0 to 1, as said below
- attend_in: float32 [1024, 3, 1024], P(('slot', 'dp'), None, 'mp'), may hold values from -0.1875 to 0.1875
- expand_in: float32 [1024, 4096], P(('slot', 'dp'), 'mp'), may hold values from -0.1875 to 0.1875
- attend_out: float32 [1024, 1024], P('mp', ('slot', 'dp')), may hold values from -0.75 to 0.75
- expand_out: float32 [4096, 1024], P('mp', ('slot', 'dp')), may hold values from -0.09375 to 0.09375
- slot_table: float32 [8, 256, 128], P('slot'), may hold values from -6 to 6
- local_pack: float32 [3475456], P(('slot', 'mp', 'dp')), as said below
- moment_attend_in: float32 [1024, 3, 1024], P(('slot', 'dp'), None, 'mp'), may hold values from -3.8146973e-05 to 3.8146973e-05
- moment_expand_in: float32 [1024, 4096], P(('slot', 'dp'), 'mp'), may hold values from -3.8146973e-05 to 3.8146973e-05
- moment_attend_out: float32 [1024, 1024], P('mp', ('slot', 'dp')), may hold values from -3.8146973e-05 to 3.8146973e-05
- moment_expand_out: float32 [4096, 1024], P('mp', ('slot', 'dp')), may hold values from -3.8146973e-05 to 3.8146973e-05
- moment_slot_table: float32 [8, 256, 128], P('slot'), may hold values from -3.8146973e-05 to 3.8146973e-05
- moment_local_pack: float32 [3475456], P(('slot', 'mp', 'dp')), may hold values from -3.8146973e-05 to 3.8146973e-05
- average_attend_in: float32 [1024, 3, 1024], P(('slot', 'dp'), None, 'mp'), may hold values from -0.1875 to 0.1875
- average_expand_in: float32 [1024, 4096], P(('slot', 'dp'), 'mp'), may hold values from -0.1875 to 0.1875
- average_attend_out: float32 [1024, 1024], P('mp', ('slot', 'dp')), may hold values from -0.75 to 0.75
- average_expand_out: float32 [4096, 1024], P('mp', ('slot', 'dp')), may hold values from -0.09375 to 0.09375
- average_slot_table: float32 [8, 256, 128], P('slot'), may hold values from -6 to 6
- average_local_pack: float32 [3475456], P(('slot', 'mp', 'dp')), as said below
Outputs:
- loss_sum: float32 [], replicated
- mask_count: float32 [], replicated
- clip_norm: float32 [], replicated
- next_attend_in: float32 [1024, 3, 1024], P(('slot', 'dp'), None, 'mp')
- next_moment_attend_in: float32 [1024, 3, 1024], P(('slot', 'dp'), None, 'mp')
- next_average_attend_in: float32 [1024, 3, 1024], P(('slot', 'dp'), None, 'mp')
- next_expand_in: float32 [1024, 4096], P(('slot', 'dp'), 'mp')
- next_moment_expand_in: float32 [1024, 4096], P(('slot', 'dp'), 'mp')
- next_average_expand_in: float32 [1024, 4096], P(('slot', 'dp'), 'mp')
- next_attend_out: float32 [1024, 1024], P('mp', ('slot', 'dp'))
- next_moment_attend_out: float32 [1024, 1024], P('mp', ('slot', 'dp'))
- next_average_attend_out: float32 [1024, 1024], P('mp', ('slot', 'dp'))
- next_expand_out: float32 [4096, 1024], P('mp', ('slot', 'dp'))
- next_moment_expand_out: float32 [4096, 1024], P('mp', ('slot', 'dp'))
- next_average_expand_out: float32 [4096, 1024], P('mp', ('slot', 'dp'))
- next_slot_table: float32 [8, 256, 128], P('slot')
- next_moment_slot_table: float32 [8, 256, 128], P('slot')
- next_average_slot_table: float32 [8, 256, 128], P('slot')
- next_local_pack: float32 [3475456], P(('slot', 'mp', 'dp'))
- next_moment_local_pack: float32 [3475456], P(('slot', 'mp', 'dp'))
- next_average_local_pack: float32 [3475456], P(('slot', 'mp', 'dp'))
Inputs may be any that keep to these rules, and one draw needn't show every extreme that they name: local_pack holds the byte layer weights of fan-in scale and gains near 1, laid end to end as the steps list them. average_local_pack is laid out as local_pack. loss_mask holds 0 and 1 only.
All inputs are finite; a program needn't handle non-finite values.
Results may differ from a plain program's by a relative error of at most 0.012.
Values may be sent and summed in bfloat16 or wider, within the bound.
A program may use at most 256 MiB of HBM per device.

v0:
```python
import jax
import jax.numpy as jnp
from jax import lax
from jax.sharding import PartitionSpec as P

D = 1024
LD = 512
LH = 8
LFF = 2048
VOCAB = 256
SLOTS = 8
HEADDIM = 64
LHEADDIM = 64
GSLOT = 128


epsilon = 1e-06
clip_max = 0.01
momentum_keep = 0.9
average_keep = 0.9
rate_dense = 3000.0
rate_table = 60000.0
rate_project = 15000.0
masked_score = -1e30


def product(left, right):
    return jnp.dot(left, right, preferred_element_type=jnp.float32)


def gram_product(left, right):
    return lax.dot_general(
        left, right, (((0,), (0,)), ((), ())), preferred_element_type=jnp.float32
    )


def back_product(left, right):
    return lax.dot_general(
        left, right, (((1,), (1,)), ((), ())), preferred_element_type=jnp.float32
    )


def gelu_tanh(values):
    return jax.nn.gelu(values, approximate=True)


def gelu_back(values, gradient):
    return jax.vjp(gelu_tanh, values)[1](gradient)[0]


def norm_forward(values, gain):
    factor = lax.rsqrt(jnp.mean(values * values, axis=-1, keepdims=True) + epsilon)
    scaled = values * factor
    return (scaled * gain, scaled, factor)


def norm_backward(scaled, factor, gain, gradient):
    inner = gradient * gain
    return factor * (inner - scaled * jnp.mean(inner * scaled, axis=-1, keepdims=True))


def split_pack(packed):
    layouts = (
        (LD, 3 * LD),
        (LD, LFF),
        (LD, LD),
        (LFF, LD),
        (LD, VOCAB),
        (VOCAB, LD),
        (GSLOT, LD),
        (D + 2 * LD,),
    )
    pieces = []
    offset = 0
    for layout in layouts:
        length = 1
        for extent in layout:
            length = length * extent
        pieces.append(packed[offset : offset + length].reshape(layout))
        offset = offset + length
    return pieces


def masked_scores(query, key_all, allowed, heads_local):
    query_heads = query.reshape(query.shape[0], heads_local, HEADDIM)
    key_heads = key_all.reshape(key_all.shape[0], heads_local, HEADDIM)
    scores = jnp.einsum(
        "qhd,khd->hqk", query_heads, key_heads, preferred_element_type=jnp.float32
    ) * HEADDIM ** (-0.5)
    return jnp.where(allowed[None], scores, masked_score)


def local_layer(middle, own_ids, weighting, params, vocab_ids):
    local_in, local_up, local_out, local_down, head, embed, bridge, gain_local, gain_final = params
    patches = own_ids.shape[0]
    byte_rows = patches * SLOTS
    inputs = middle.astype(jnp.bfloat16).reshape(byte_rows, GSLOT)
    previous = jnp.concatenate(
        [jnp.zeros((patches, 1), jnp.int32), own_ids[:, :-1]], axis=1
    ).reshape(-1)
    leading = jnp.tile(jnp.arange(SLOTS) > 0, patches)
    lookup = ((previous[:, None] == vocab_ids[None, :]) & leading[:, None]).astype(jnp.bfloat16)
    start_sum = product(inputs, bridge) + product(lookup, embed)
    normed, scaled, factor = norm_forward(start_sum, gain_local)
    hidden = normed.astype(jnp.bfloat16)
    projected = product(hidden, local_in).astype(jnp.bfloat16)

    def heads_of(block):
        return block.reshape(patches, SLOTS, LH, LHEADDIM)

    query = heads_of(projected[:, :LD])
    key_heads = heads_of(projected[:, LD : 2 * LD])
    value_heads = heads_of(projected[:, 2 * LD :])
    scale = LHEADDIM ** (-0.5)
    causal = jnp.arange(SLOTS)[:, None] >= jnp.arange(SLOTS)[None, :]
    scores = jnp.where(
        causal,
        jnp.einsum("pqhd,pkhd->phqk", query, key_heads, preferred_element_type=jnp.float32) * scale,
        masked_score,
    )
    probs = jax.nn.softmax(scores, axis=-1)
    probs_low = probs.astype(jnp.bfloat16)
    attended = (
        jnp.einsum("phqk,pkhd->pqhd", probs_low, value_heads, preferred_element_type=jnp.float32)
        .reshape(byte_rows, LD)
        .astype(jnp.bfloat16)
    )
    expanded = product(hidden, local_up)
    active = gelu_tanh(expanded).astype(jnp.bfloat16)
    after = start_sum + product(attended, local_out) + product(active, local_down)
    normed_final, scaled_final, factor_final = norm_forward(after, gain_final)
    final = normed_final.astype(jnp.bfloat16)
    logits = product(final, head)
    target_hot = (own_ids.reshape(-1)[:, None] == vocab_ids[None, :]).astype(jnp.float32)
    top = jnp.max(logits, axis=-1, keepdims=True)
    log_total = top + jnp.log(jnp.sum(jnp.exp(logits - top), axis=-1, keepdims=True))
    loss_part = jnp.sum(weighting * (log_total[:, 0] - jnp.sum(logits * target_hot, axis=-1)))
    logits_grad = ((jnp.exp(logits - log_total) - target_hot) * weighting[:, None]).astype(
        jnp.bfloat16
    )
    grad_head = gram_product(final, logits_grad)
    final_grad = back_product(logits_grad, head)
    gain_final_grad = jnp.sum(final_grad * scaled_final, axis=0)
    after_grad = norm_backward(scaled_final, factor_final, gain_final, final_grad)
    branch_grad = after_grad.astype(jnp.bfloat16)
    grad_out = gram_product(attended, branch_grad)
    grad_down = gram_product(active, branch_grad)
    attended_grad = heads_of(back_product(branch_grad, local_out).astype(jnp.bfloat16))
    expanded_grad = gelu_back(expanded, back_product(branch_grad, local_down)).astype(jnp.bfloat16)
    grad_up = gram_product(hidden, expanded_grad)
    probs_grad = jnp.einsum(
        "pqhd,pkhd->phqk", attended_grad, value_heads, preferred_element_type=jnp.float32
    )
    score_grad = (
        probs * (probs_grad - jnp.sum(probs * probs_grad, axis=-1, keepdims=True))
    ).astype(jnp.bfloat16)
    query_grad = (
        jnp.einsum("phqk,pkhd->pqhd", score_grad, key_heads, preferred_element_type=jnp.float32)
        * scale
    )
    key_grad = (
        jnp.einsum("phqk,pqhd->pkhd", score_grad, query, preferred_element_type=jnp.float32) * scale
    )
    value_grad = jnp.einsum(
        "phqk,pqhd->pkhd", probs_low, attended_grad, preferred_element_type=jnp.float32
    )
    projected_grad = jnp.concatenate(
        [
            query_grad.reshape(byte_rows, LD),
            key_grad.reshape(byte_rows, LD),
            value_grad.reshape(byte_rows, LD),
        ],
        axis=1,
    ).astype(jnp.bfloat16)
    grad_in = gram_product(hidden, projected_grad)
    hidden_grad = back_product(projected_grad, local_in) + back_product(expanded_grad, local_up)
    gain_local_grad = jnp.sum(hidden_grad * scaled, axis=0)
    start_grad = (after_grad + norm_backward(scaled, factor, gain_local, hidden_grad)).astype(
        jnp.bfloat16
    )
    grad_embed = gram_product(lookup, start_grad)
    grad_bridge = gram_product(inputs, start_grad)
    input_grad = back_product(start_grad, bridge).reshape(patches, D)
    matrices = (grad_in, grad_up, grad_out, grad_down, grad_head, grad_embed, grad_bridge)
    return (loss_part, matrices, (gain_local_grad, gain_final_grad), input_grad)


def update(weight, moment, average, gradient, factor, rate):
    step_grad = factor * gradient
    moment_next = momentum_keep * moment + step_grad
    weight_next = weight - rate * (step_grad + momentum_keep * moment_next)
    average_next = average_keep * average + (1.0 - average_keep) * weight_next
    return (weight_next, moment_next, average_next)


def local(
    byte_ids,
    item_ids,
    loss_mask,
    attend_in,
    expand_in,
    attend_out,
    expand_out,
    slot_table,
    local_pack,
    moment_attend_in,
    moment_expand_in,
    moment_attend_out,
    moment_expand_out,
    moment_slot_table,
    moment_local_pack,
    average_attend_in,
    average_expand_in,
    average_attend_out,
    average_expand_out,
    average_slot_table,
    average_local_pack,
):
    mask_count = lax.psum(jnp.sum(loss_mask.astype(jnp.float32)), "dp")
    full_in, full_expand, full_out, full_shrink = (
        lax.all_gather(attend_in.astype(jnp.bfloat16), ("slot", "dp"), axis=0, tiled=True),
        lax.all_gather(expand_in.astype(jnp.bfloat16), ("slot", "dp"), axis=0, tiled=True),
        lax.all_gather(attend_out.astype(jnp.bfloat16), ("slot", "dp"), axis=1, tiled=True),
        lax.all_gather(expand_out.astype(jnp.bfloat16), ("slot", "dp"), axis=1, tiled=True),
    )
    unpacked = split_pack(
        lax.all_gather(local_pack.astype(jnp.bfloat16), ("slot", "mp", "dp"), axis=0, tiled=True)
    )
    gains = unpacked[7].astype(jnp.float32)
    gain_global = gains[:D]
    local_params = tuple(unpacked[:7]) + (gains[D : D + LD], gains[D + LD :])
    slot_index = lax.axis_index("slot")
    mp_index = lax.axis_index("mp")
    dp_index = lax.axis_index("dp")
    group_rows = byte_ids.shape[1]
    slot_rows = group_rows // lax.axis_size("slot")
    local_rows = slot_rows // lax.axis_size("mp")
    slot_share = slot_table.shape[0]
    local_width = full_in.shape[2]
    heads_local = local_width // HEADDIM
    full_in_flat = full_in.reshape(D, 3 * local_width)
    table_low = slot_table.astype(jnp.bfloat16)
    vocab_ids = jnp.arange(VOCAB)
    positions = jnp.arange(group_rows)
    summed_global = None
    summed_local = None
    summed_table = None
    loss_sum = jnp.float32(0.0)
    for micro_index in range(byte_ids.shape[0]):
        group_ids = byte_ids[micro_index]
        group_items = item_ids[micro_index, 0]
        prev_patch = jnp.concatenate([jnp.zeros((1, SLOTS), jnp.int32), group_ids[:-1]], axis=0)
        earlier = jnp.concatenate([group_items[:1], group_items[:-1]])
        keep_rows = (positions > 0) & (group_items == earlier)
        slot_start = slot_index * slot_rows
        own_prev = lax.dynamic_slice_in_dim(prev_patch, slot_index * slot_share, slot_share, 1)
        lookup = ((own_prev[:, :, None] == vocab_ids) & keep_rows[:, None, None]).astype(
            jnp.bfloat16
        )
        embedded = jnp.einsum("pjv,jvg->pjg", lookup, table_low, preferred_element_type=jnp.float32)
        embedded = embedded.astype(jnp.bfloat16).reshape(group_rows, slot_share * GSLOT)
        start_rows = lax.all_to_all(
            embedded, "slot", split_axis=0, concat_axis=1, tiled=True
        ).astype(jnp.float32)
        normed, scaled, factor = norm_forward(start_rows, gain_global)
        hidden = normed.astype(jnp.bfloat16)
        projected = product(hidden, full_in_flat).astype(jnp.bfloat16)
        query = projected[:, :local_width]
        key_all, value_all = (
            lax.all_gather(projected[:, local_width : 2 * local_width], "slot", axis=0, tiled=True),
            lax.all_gather(projected[:, 2 * local_width :], "slot", axis=0, tiled=True),
        )
        own_items = lax.dynamic_slice_in_dim(group_items, slot_start, slot_rows, 0)
        own_positions = slot_start + jnp.arange(slot_rows)
        allowed = (own_items[:, None] == group_items[None, :]) & (
            positions[None, :] <= own_positions[:, None]
        )
        scores = masked_scores(query, key_all, allowed, heads_local)
        top = jnp.max(scores, axis=-1, keepdims=True)
        log_total = top + jnp.log(jnp.sum(jnp.exp(scores - top), axis=-1, keepdims=True))
        probs = jnp.exp(scores - log_total)
        value_heads = value_all.reshape(group_rows, heads_local, HEADDIM)
        attended = (
            jnp.einsum(
                "hqk,khd->qhd",
                probs.astype(jnp.bfloat16),
                value_heads,
                preferred_element_type=jnp.float32,
            )
            .reshape(slot_rows, local_width)
            .astype(jnp.bfloat16)
        )
        expanded = product(hidden, full_expand)
        active = gelu_tanh(expanded).astype(jnp.bfloat16)
        branch = lax.psum_scatter(
            product(attended, full_out) + product(active, full_shrink),
            "mp",
            scatter_dimension=0,
            tiled=True,
        )
        middle = lax.dynamic_slice_in_dim(start_rows, mp_index * local_rows, local_rows, 0) + branch
        local_start = slot_start + mp_index * local_rows
        own_ids = lax.dynamic_slice_in_dim(group_ids, local_start, local_rows, 0)
        own_mask = lax.dynamic_slice_in_dim(loss_mask[micro_index], local_start, local_rows, 0)
        weighting = own_mask.reshape(-1).astype(jnp.float32) / mask_count
        loss_part, matrices, local_gains, input_grad = local_layer(
            middle, own_ids, weighting, local_params, vocab_ids
        )
        loss_sum = loss_sum + loss_part
        back_rows = lax.all_gather(
            input_grad.astype(jnp.bfloat16), "mp", axis=0, tiled=True
        ).astype(input_grad.dtype)
        branch_grad = back_rows.astype(jnp.bfloat16)
        grad_out = gram_product(attended, branch_grad)
        grad_shrink = gram_product(active, branch_grad)
        attended_grad = (
            back_product(branch_grad, full_out)
            .astype(jnp.bfloat16)
            .reshape(slot_rows, heads_local, HEADDIM)
        )
        expanded_grad = gelu_back(expanded, back_product(branch_grad, full_shrink)).astype(
            jnp.bfloat16
        )
        grad_expand = gram_product(hidden, expanded_grad)
        probs = jnp.exp(masked_scores(query, key_all, allowed, heads_local) - log_total)
        probs_grad = jnp.einsum(
            "qhd,khd->hqk", attended_grad, value_heads, preferred_element_type=jnp.float32
        )
        score_grad = (
            probs * (probs_grad - jnp.sum(probs * probs_grad, axis=-1, keepdims=True))
        ).astype(jnp.bfloat16)
        scale = HEADDIM ** (-0.5)
        query_grad = (
            jnp.einsum(
                "hqk,khd->qhd",
                score_grad,
                key_all.reshape(group_rows, heads_local, HEADDIM),
                preferred_element_type=jnp.float32,
            )
            * scale
        )
        key_terms = (
            jnp.einsum(
                "hqk,qhd->khd",
                score_grad,
                query.reshape(slot_rows, heads_local, HEADDIM),
                preferred_element_type=jnp.float32,
            )
            * scale
        )
        value_terms = jnp.einsum(
            "hqk,qhd->khd",
            probs.astype(jnp.bfloat16),
            attended_grad,
            preferred_element_type=jnp.float32,
        )
        key_grad, value_grad = (
            lax.psum_scatter(
                key_terms.reshape(group_rows, local_width).astype(jnp.bfloat16),
                "slot",
                scatter_dimension=0,
                tiled=True,
            ).astype(jnp.float32),
            lax.psum_scatter(
                value_terms.reshape(group_rows, local_width).astype(jnp.bfloat16),
                "slot",
                scatter_dimension=0,
                tiled=True,
            ).astype(jnp.float32),
        )
        projected_grad = jnp.concatenate(
            [query_grad.reshape(slot_rows, local_width), key_grad, value_grad], axis=1
        ).astype(jnp.bfloat16)
        grad_in = gram_product(hidden, projected_grad).reshape(D, 3, local_width)
        hidden_grad = back_product(projected_grad, full_in_flat) + back_product(
            expanded_grad, full_expand
        )
        gain_global_grad = jnp.sum(hidden_grad * scaled, axis=0)
        hidden_sum = lax.psum(hidden_grad.astype(jnp.bfloat16), "mp").astype(jnp.float32)
        start_grad = (back_rows + norm_backward(scaled, factor, gain_global, hidden_sum)).astype(
            jnp.bfloat16
        )
        returned = lax.all_to_all(start_grad, "slot", split_axis=1, concat_axis=0, tiled=True)
        table_grad = jnp.einsum(
            "pjv,pjg->jvg",
            lookup,
            returned.reshape(group_rows, slot_share, GSLOT),
            preferred_element_type=jnp.float32,
        )
        local_flat = jnp.concatenate(
            [matrix.reshape(-1) for matrix in matrices]
            + [gain_global_grad, local_gains[0], local_gains[1]]
        )
        global_terms = (grad_in, grad_expand, grad_out, grad_shrink)
        if summed_global is None:
            summed_global = tuple(global_terms)
            summed_local = local_flat
            summed_table = table_grad
        else:
            summed_global = tuple(
                (total + term for total, term in zip(summed_global, global_terms))
            )
            summed_local = summed_local + local_flat
            summed_table = summed_table + table_grad
    summed_global = (
        lax.psum_scatter(summed_global[0], ("slot", "dp"), scatter_dimension=0, tiled=True),
        lax.psum_scatter(summed_global[1], ("slot", "dp"), scatter_dimension=0, tiled=True),
        lax.psum_scatter(summed_global[2], ("slot", "dp"), scatter_dimension=1, tiled=True),
        lax.psum_scatter(summed_global[3], ("slot", "dp"), scatter_dimension=1, tiled=True),
    )
    summed_local = lax.psum_scatter(
        summed_local, ("slot", "mp", "dp"), scatter_dimension=0, tiled=True
    )
    table_total = lax.psum(summed_table.astype(jnp.bfloat16), "dp").astype(jnp.float32)
    owner = ((mp_index == 0) & (dp_index == 0)).astype(jnp.float32)
    squares = jnp.sum(summed_local * summed_local) + owner * jnp.sum(table_total * table_total)
    for gradient in summed_global:
        squares = squares + jnp.sum(gradient * gradient)
    total_squares, loss_value = lax.psum((squares, loss_sum), ("slot", "mp", "dp"))
    clip_norm = jnp.sqrt(total_squares)
    factor = clip_max / jnp.maximum(clip_norm, clip_max)
    in_next = update(
        attend_in, moment_attend_in, average_attend_in, summed_global[0], factor, rate_dense
    )
    up_next = update(
        expand_in, moment_expand_in, average_expand_in, summed_global[1], factor, rate_dense
    )
    out_next = update(
        attend_out, moment_attend_out, average_attend_out, summed_global[2], factor, rate_project
    )
    down_next = update(
        expand_out, moment_expand_out, average_expand_out, summed_global[3], factor, rate_dense
    )
    table_next = update(
        slot_table, moment_slot_table, average_slot_table, table_total, factor, rate_table
    )
    pack_next = update(
        local_pack, moment_local_pack, average_local_pack, summed_local, factor, rate_dense
    )
    return (
        loss_value * mask_count,
        mask_count,
        clip_norm,
        in_next[0],
        in_next[1],
        in_next[2],
        up_next[0],
        up_next[1],
        up_next[2],
        out_next[0],
        out_next[1],
        out_next[2],
        down_next[0],
        down_next[1],
        down_next[2],
        table_next[0],
        table_next[1],
        table_next[2],
        pack_next[0],
        pack_next[1],
        pack_next[2],
    )


def solution(mesh):
    placed = (
        P(None, "dp", None),
        P(None, "dp", None),
        P(None, "dp", None),
        P(("slot", "dp"), None, "mp"),
        P(("slot", "dp"), "mp"),
        P("mp", ("slot", "dp")),
        P("mp", ("slot", "dp")),
        P("slot", None, None),
        P(("slot", "mp", "dp")),
        P(("slot", "dp"), None, "mp"),
        P(("slot", "dp"), "mp"),
        P("mp", ("slot", "dp")),
        P("mp", ("slot", "dp")),
        P("slot", None, None),
        P(("slot", "mp", "dp")),
        P(("slot", "dp"), None, "mp"),
        P(("slot", "dp"), "mp"),
        P("mp", ("slot", "dp")),
        P("mp", ("slot", "dp")),
        P("slot", None, None),
        P(("slot", "mp", "dp")),
    )
    return jax.shard_map(
        local,
        mesh=mesh,
        in_specs=placed,
        out_specs=(
            P(),
            P(),
            P(),
            P(("slot", "dp"), None, "mp"),
            P(("slot", "dp"), None, "mp"),
            P(("slot", "dp"), None, "mp"),
            P(("slot", "dp"), "mp"),
            P(("slot", "dp"), "mp"),
            P(("slot", "dp"), "mp"),
            P("mp", ("slot", "dp")),
            P("mp", ("slot", "dp")),
            P("mp", ("slot", "dp")),
            P("mp", ("slot", "dp")),
            P("mp", ("slot", "dp")),
            P("mp", ("slot", "dp")),
            P("slot", None, None),
            P("slot", None, None),
            P("slot", None, None),
            P(("slot", "mp", "dp")),
            P(("slot", "mp", "dp")),
            P(("slot", "mp", "dp")),
        ),
        check_vma=False,
    )
```

profile of v0, /device:TPU:0, one launch (start us, length us, event | category | flops | bytes accessed | tf_op | source)
XLA Modules:
  0.0 1349.6 jit_solution(1075547487112552282)
XLA Ops:
  23.0 8.7 copy.222
  40.8 8.7 copy.206
  51.1 9.7 all-to-all-done.1
  64.6 19.3 %all-to-all-done = bf16[4,512,256]{2,1,0:T(8,128)(2,1)S(1)} async-done(((bf16[4,512,256]{2,1,0:T(8,128)(2,1)}), bf16[4,512,256]{2,1,0:T(8,128)(2,1)S(1)}, u32[]{:S(2)}, u32[]{:S(2)}) %all-to-all-start) | async-done | bytes 1048608 | tf_op jit(solution)/shard_map/all_to_all | solution.py:262
  84.2 112.3 %all-reduce.15.cloned.1.call-done = bf16[3475456]{0:T(1024)(128)(2,1)} async-done(((bf16[3475456]{0:T(1024)(128)(2,1)}), bf16[3475456]{0:T(1024)(128)(2,1)}) %all-reduce.15.cloned.1.call-update) | async-done | bytes 6950928
  225.3 11.2 all_gather.37
  275.9 8.7 convolution_convert_fusion.13
  297.9 19.7 %all-gather.20.cloned.1.call-done = bf16[2048,256]{1,0:T(8,128)(2,1)} async-done(((bf16[512,256]{1,0:T(8,128)(2,1)}), bf16[2048,256]{1,0:T(8,128)(2,1)}) %all-gather.20.cloned.1.call-update) | async-done | bytes 1048592 | tf_op jit(solution)/shard_map/all_gather | solution.py:271
  362.6 17.8 %reduce-scatter.13.cloned.1.call-done = f32[128,1024]{1,0:T(8,128)} async-done(((f32[512,1024]{1,0:T(8,128)}), f32[128,1024]{1,0:T(8,128)}) %reduce-scatter.13.cloned.1.call-update) | async-done | bytes 524304 | tf_op jit(solution)/shard_map/reduce_scatter | solution.py:295
  421.5 15.2 %fusion.195 = (f32[128,8,8]{2,1,0:T(8,128)S(1)}, f32[128,8,8,8]{2,3,1,0:T(8,128)S(1)}) fusion(f32[128,8,8,8]{2,3,1,0:T(8,128)S(1)} %fusion.91, pred[8,8]{0,1:T(8,128)(4,1)S(1)} %copy-done.232), kind=kOutput, calls=%fused_computation.388 | output fusion | flops 393223 | bytes 557120 | tf_op jit(solution)/shard_map/sub | solution.py:121
  441.5 6.9 fusion.176
  487.3 7.3 fusion.175
  525.4 11.5 fusion.19
  537.4 8.8 fusion.12
  596.5 6.0 fusion.204
  661.9 5.7 convolution_bitcast_fusion
  689.0 15.9 %multiply_reduce_fusion.1 = (f32[4,512]{1,0:T(4,128)}, f32[4,512,2048]{2,1,0:T(8,128)}) fusion(f32[4,512,2048]{2,1,0:T(8,128)} %copy-done, f32[4,512]{1,0:T(4,128)S(1)} %copy-done.188, pred[512,2048]{1,0:T(8,128)(4,1)S(1)} %copy-done.23, bf16[512,4,64]{0,2,1:T(8,128)(2,1)} %bitcast.351, bf16[2048,4,64]{0,2,1:T(8,128)(2,1)} %bitcast.318), kind=kOutput, calls=%fused_computation.5 | convolution fusion | flops 557840384 | bytes 35930112 | tf_op jit(solution)/shard_map/qhd,khd->hqk/dot_general | solution.py:326
  706.0 8.3 multiply_convert_fusion.1
  719.7 11.6 convolution_convert_fusion.3
  731.4 12.9 multiply_reduce_fusion
  744.4 12.3 multiply_convert_fusion
  772.6 5.8 convolution_convert_fusion.2
  806.6 30.5 %reduce-scatter.21.cloned.1.call-done = bf16[512,256]{0,1:T(8,128)(2,1)} async-done(((bf16[2048,256]{0,1:T(8,128)(2,1)}), bf16[512,256]{0,1:T(8,128)(2,1)}) %reduce-scatter.21.cloned.1.call-update) | async-done | bytes 262160 | tf_op jit(solution)/shard_map/reduce_scatter | solution.py:364
  848.7 80.5 %all-reduce.19.cloned.1.call-done = (bf16[512,1024]{1,0:T(8,128)(2,1)}, bf16[512,1024]{1,0:T(8,128)(2,1)}) async-done(((bf16[512,1024]{1,0:T(8,128)(2,1)}, bf16[512,1024]{1,0:T(8,128)(2,1)}), (bf16[512,1024]{1,0:T(8,128)(2,1)}, bf16[512,1024]{1,0:T(8,128)(2,1)})) %all-reduce.19.cloned.1.call-update) | async-done | bytes 2097168 | tf_op jit(solution)/shard_map/psum | solution.py:379
  948.2 7.3 all-to-all-done.2
  959.9 6.0 convolution_bitcast_fusion.2
  982.3 6.4 convolution_add_fusion
  1024.2 15.4 %add.396 = f32[3475456]{0:T(1024)} add(f32[3475456]{0:T(1024)} %constant_dynamic-update-slice_fusion.8, f32[3475456]{0:T(1024)} %constant_dynamic-update-slice_fusion.9) | non-fusion elementwise | flops 3475456 | bytes 41705472 | tf_op jit(solution)/shard_map/add | solution.py:403
  1046.7 48.4 %reduce-scatter.25.cloned.1.call-done = f32[128,1024]{1,0:T(8,128)} async-done(((f32[1024,1024]{1,0:T(8,128)}), f32[128,1024]{1,0:T(8,128)}) %reduce-scatter.25.cloned.1.call-update) | async-done | bytes 524304 | tf_op jit(solution)/shard_map/reduce_scatter | solution.py:407
  1096.8 60.6 %reduce-scatter.23.cloned.1.call-done = f32[128,3,256]{2,0,1:T(8,128)} async-done(((f32[1024,3,256]{2,0,1:T(8,128)}), f32[128,3,256]{2,0,1:T(8,128)}) %reduce-scatter.23.cloned.1.call-update) | async-done | bytes 393232 | tf_op jit(solution)/shard_map/reduce_scatter | solution.py:406
  1159.1 125.6 %all-reduce.17.cloned.1.call-done = f32[3475456]{0:T(1024)} async-done(((f32[3475456]{0:T(1024)}), f32[3475456]{0:T(1024)}) %all-reduce.17.cloned.1.call-update) | async-done | bytes 13901840
  1289.8 39.4 %all-reduce.6 = (f32[]{:T(128)}, f32[]{:T(128)}) all-reduce(f32[]{:T(128)S(6)} %add.389, f32[]{:T(128)S(6)} %add.408), channel_id=1, replica_groups=mesh['slot'=4,'mp'=4,'dp'=2] {'slot','mp','dp'}, use_global_device_ids=true, to_apply=%region_26.27 | all-reduce | flops 2 | bytes 16 | tf_op jit(solution)/shard_map/psum | solution.py:419
  (853 shorter events, 556.4 us)
Async XLA Ops:
  8.0 188.5 %all-reduce.15.cloned.1.call-start = ((), (), s32[]{:S(2)}) async-start(), calls=%async_computation.34 | async-start | bytes 13901824
  16.9 183.3 %all-gather.10.cloned.1.call-start = ((), (), s32[]{:S(2)}) async-start(), calls=%async_computation.14 | async-start | bytes 1769472 | tf_op jit(solution)/shard_map/all_gather | solution.py:221
  18.6 232.8 %all-gather.16.cloned.1.call-start = ((), (), s32[]{:S(2)}) async-start(), calls=%async_computation.17 | async-start | bytes 2359296 | tf_op jit(solution)/shard_map/all_gather | solution.py:222
  19.4 236.3 %all-gather.18.cloned.1.call-start = ((), (), s32[]{:S(2)}) async-start(), calls=%async_computation.18 | async-start | bytes 2359296 | tf_op jit(solution)/shard_map/all_gather | solution.py:224
  33.2 27.5 %all-to-all-start.1 = ((bf16[4,512,256]{2,1,0:T(8,128)(2,1)}), bf16[4,512,256]{2,1,0:T(8,128)(2,1)S(1)}, u32[]{:S(2)}, u32[]{:S(2)}) async-start(bf16[4,512,256]{2,1,0:T(8,128)(2,1)} %all_to_all.46), calls=%async_computation.2 | async-start | bytes 2097152 | tf_op jit(solution)/shard_map/all_to_all | solution.py:262
  60.7 23.2 %all-to-all-start = ((bf16[4,512,256]{2,1,0:T(8,128)(2,1)}), bf16[4,512,256]{2,1,0:T(8,128)(2,1)S(1)}, u32[]{:S(2)}, u32[]{:S(2)}) async-start(bf16[4,512,256]{2,1,0:T(8,128)(2,1)} %all_to_all.44), calls=%async_computation | async-start | bytes 2097152 | tf_op jit(solution)/shard_map/all_to_all | solution.py:262
  64.3 196.4 %all-gather.14.cloned.1.call-start = ((), (), s32[]{:S(2)}) async-start(), calls=%async_computation.16 | async-start | bytes 1310720 | tf_op jit(solution)/shard_map/all_gather | solution.py:270
  203.9 69.8 %all-gather.12.cloned.1.call-start = ((), (), s32[]{:S(2)}) async-start(), calls=%async_computation.15 | async-start | bytes 1310720 | tf_op jit(solution)/shard_map/all_gather | solution.py:271
  204.6 91.0 %all-gather.22.cloned.1.call-start = ((), (), s32[]{:S(2)}) async-start(), calls=%async_computation.21 | async-start | bytes 1310720 | tf_op jit(solution)/shard_map/all_gather | solution.py:270
  213.9 103.8 %all-gather.20.cloned.1.call-start = ((), (), s32[]{:S(2)}) async-start(), calls=%async_computation.20 | async-start | bytes 1310720 | tf_op jit(solution)/shard_map/all_gather | solution.py:271
  246.9 110.2 %reduce-scatter.11.cloned.1.call-start = ((), (), s32[]{:S(2)}) async-start(), calls=%async_computation.19 | async-start | bytes 2621440 | tf_op jit(solution)/shard_map/reduce_scatter | solution.py:295
  287.2 93.2 %reduce-scatter.13.cloned.1.call-start = ((), (), s32[]{:S(2)}) async-start(), calls=%async_computation.22 | async-start | bytes 2621440 | tf_op jit(solution)/shard_map/reduce_scatter | solution.py:295
  336.4 350.1 %all-gather.24.cloned.1.call-start = ((), (), s32[]{:S(2)}) async-start(), calls=%async_computation.23 | async-start | bytes 1310720 | tf_op jit(solution)/shard_map/all_gather | solution.py:310
  648.3 69.7 %all-gather.26.cloned.1.call-start = ((), (), s32[]{:S(2)}) async-start(), calls=%async_computation.26 | async-start | bytes 1310720 | tf_op jit(solution)/shard_map/all_gather | solution.py:310
  678.6 118.2 %reduce-scatter.15.cloned.1.call-start = ((), (), s32[]{:S(2)}) async-start(), calls=%async_computation.24 | async-start | bytes 1310720 | tf_op jit(solution)/shard_map/reduce_scatter | solution.py:358
  717.9 78.9 %reduce-scatter.17.cloned.1.call-start = ((), (), s32[]{:S(2)}) async-start(), calls=%async_computation.25 | async-start | bytes 1310720 | tf_op jit(solution)/shard_map/reduce_scatter | solution.py:364
  744.3 62.3 %reduce-scatter.19.cloned.1.call-start = ((), (), s32[]{:S(2)}) async-start(), calls=%async_computation.27 | async-start | bytes 1310720 | tf_op jit(solution)/shard_map/reduce_scatter | solution.py:358
  760.4 76.7 %reduce-scatter.21.cloned.1.call-start = ((), (), s32[]{:S(2)}) async-start(), calls=%async_computation.28 | async-start | bytes 1310720 | tf_op jit(solution)/shard_map/reduce_scatter | solution.py:364
  778.4 150.8 %all-reduce.19.cloned.1.call-start = ((), (), s32[]{:S(2)}) async-start(), calls=%async_computation.36 | async-start | bytes 4194304 | tf_op jit(solution)/shard_map/psum | solution.py:379
  937.3 18.2 %all-to-all-start.2 = ((bf16[512,4,256]{2,0,1:T(8,128)(2,1)}), bf16[512,4,256]{2,0,1:T(8,128)(2,1)}, u32[]{:S(2)}, u32[]{:S(2)}) async-start(bf16[512,4,256]{2,0,1:T(8,128)(2,1)} %bitcast.322), calls=%async_computation.8 | async-start | bytes 2097152 | tf_op jit(solution)/shard_map/all_to_all | solution.py:383
  941.6 99.5 %reduce-scatter.27.cloned.1.call-start = ((), (), s32[]{:S(2)}) async-start(), calls=%async_computation.32 | async-start | bytes 1179648 | tf_op jit(solution)/shard_map/reduce_scatter | solution.py:408
  955.6 20.3 %all-to-all-start.3 = ((bf16[512,4,256]{2,0,1:T(8,128)(2,1)}), bf16[512,4,256]{2,0,1:T(8,128)(2,1)}, u32[]{:S(2)}, u32[]{:S(2)}) async-start(bf16[512,4,256]{2,0,1:T(8,128)(2,1)} %bitcast.323), calls=%async_computation.9 | async-start | bytes 2097152 | tf_op jit(solution)/shard_map/all_to_all | solution.py:383
  959.8 82.8 %all-reduce.13.cloned.1.call-start = ((), (), s32[]{:S(2)}) async-start(), calls=%async_computation.29 | async-start | bytes 262144 | tf_op jit(solution)/shard_map/psum | solution.py:414
  982.1 62.8 %reduce-scatter.29.cloned.1.call-start = ((), (), s32[]{:S(2)}) async-start(), calls=%async_computation.33 | async-start | bytes 4718592 | tf_op jit(solution)/shard_map/reduce_scatter | solution.py:409
  988.7 106.3 %reduce-scatter.25.cloned.1.call-start = ((), (), s32[]{:S(2)}) async-start(), calls=%async_computation.31 | async-start | bytes 4718592 | tf_op jit(solution)/shard_map/reduce_scatter | solution.py:407
  1004.6 152.8 %reduce-scatter.23.cloned.1.call-start = ((), (), s32[]{:S(2)}) async-start(), calls=%async_computation.30 | async-start | bytes 3538944 | tf_op jit(solution)/shard_map/reduce_scatter | solution.py:406
  1012.6 272.2 %all-reduce.17.cloned.1.call-start = ((), (), s32[]{:S(2)}) async-start(), calls=%async_computation.35 | async-start | bytes 27803648
  1039.6 291.6 %copy-start.117 = (f32[108608]{0:T(1024)S(1)}, f32[108608]{0:T(1024)}, u32[]{:S(2)}) copy-start(f32[108608]{0:T(1024)} %param.29) | copy-start | bytes 1303300
  1039.6 291.6 %copy-start.158 = (f32[108608]{0:T(1024)S(1)}, f32[108608]{0:T(1024)}, u32[]{:S(2)}) copy-start(f32[108608]{0:T(1024)} %param.41) | copy-start | bytes 1303300
  1039.6 291.6 %copy-start.159 = (f32[108608]{0:T(1024)S(1)}, f32[108608]{0:T(1024)}, u32[]{:S(2)}) copy-start(f32[108608]{0:T(1024)} %param.35) | copy-start | bytes 1303300
  1046.7 287.1 %copy-start.168 = (f32[2,256,128]{2,1,0:T(8,128)S(1)}, f32[2,256,128]{2,1,0:T(8,128)}, u32[]{:S(2)}) copy-start(f32[2,256,128]{2,1,0:T(8,128)} %param.40) | copy-start | bytes 786436
  1046.7 287.1 %copy-start.169 = (f32[2,256,128]{2,1,0:T(8,128)S(1)}, f32[2,256,128]{2,1,0:T(8,128)}, u32[]{:S(2)}) copy-start(f32[2,256,128]{2,1,0:T(8,128)} %param.34) | copy-start | bytes 786436
  (248 other events, 3794.8 us)
Sparse Core Ops, SparseCore 0:
  16.9 179.5 all-reduce.14
  287.3 43.0 reduce-scatter.10
  336.5 43.8 reduce-scatter.12
  648.4 27.2 all-gather.23
  678.7 27.3 all-gather.25
  842.1 87.0 all-reduce.18
  982.2 16.2 all-reduce.12
  1039.7 245.0 all-reduce.16
Sparse Core Ops, SparseCore 1:
  19.9 42.0 all-gather.9
  64.5 29.6 all-gather.15
  96.7 28.3 all-gather.17
  203.9 26.1 all-gather.13
  232.7 27.1 all-gather.11
  262.4 26.4 all-gather.21
  291.1 26.4 all-gather.19
  718.0 27.2 reduce-scatter.14
  748.0 27.7 reduce-scatter.16
  778.9 27.7 reduce-scatter.18
  809.4 27.7 reduce-scatter.20
  946.0 38.7 reduce-scatter.26
  988.8 50.4 reduce-scatter.28
  1043.0 52.0 reduce-scatter.24
  1098.4 58.9 reduce-scatter.22
where the time goes:
time: 1360 us; the launch traced here: 1350 us
  waiting for transfers between devices  539 us (40%)
  matrix products  316 us (23%)
  local copies, waits for them, and re-layouts  273 us (20%)
  other arithmetic  120 us (9%)
  blocking collectives  53.6 us (4%)
  between operations  28.9 us (2%)
  starting transfers between devices  19.2 us (1%)
    unnamed x25, waiting for transfers between devices  238 us
    unnamed x543, local copies, waits for them, and re-layouts  98.6 us
    psum x1, waiting for transfers between devices, local(): lax.psum(hidden_grad.astype(jnp.bfloat16), 'mp').astype(jnp.float32)  80.5 us
    dot_general x20, matrix products, back_product(): lax.dot_general(left, right, (((1,), (1,)), ((), ())), preferred_element_...  71.5 us
    dot_general x22, matrix products, product(): return jnp.dot(left, right, preferred_element_type=jnp.float32)  64.6 us
    reduce_scatter x1, waiting for transfers between devices, local(): lax.psum_scatter(summed_global[0], ('slot', 'dp'), scatter_dimension=0, t...  60.6 us
    dot_general x22, matrix products, gram_product(): lax.dot_general(left, right, (((0,), (0,)), ((), ())), preferred_element_...  55.2 us
    reduce_scatter x1, waiting for transfers between devices, local(): lax.psum_scatter(summed_global[1], ('slot', 'dp'), scatter_dimension=0, t...  48.4 us
  transfers between devices with their start and end apart: 27, of which 13 were waited for; matrix products, arithmetic and copies ran while one was open for 29% of the time, Pallas kernels for 0%

commit v1 on v0

v1 whole, which is shorter than its diff:
```python
import functools

import jax
import jax.numpy as jnp
from jax import lax
from jax.experimental import pallas as pl
from jax.experimental.pallas import tpu as pltpu
from jax.sharding import PartitionSpec as P

D = 1024
LD = 512
LH = 8
LFF = 2048
VOCAB = 256
SLOTS = 8
HEADDIM = 64
LHEADDIM = 64
GSLOT = 128
BLK = 256
F32 = jnp.float32
BF16 = jnp.bfloat16
MESH = pl.DeviceIdType.MESH

longest_item = 1024


epsilon = 1e-06
clip_max = 0.01
momentum_keep = 0.9
average_keep = 0.9
rate_dense = 3000.0
rate_table = 60000.0
rate_project = 15000.0
masked_score = -1e30


def product(left, right):
    return jnp.dot(left, right, preferred_element_type=jnp.float32)


def gram_product(left, right):
    return lax.dot_general(
        left, right, (((0,), (0,)), ((), ())), preferred_element_type=jnp.float32
    )


def back_product(left, right):
    return lax.dot_general(
        left, right, (((1,), (1,)), ((), ())), preferred_element_type=jnp.float32
    )


def gelu_tanh(values):
    return jax.nn.gelu(values, approximate=True)


def gelu_back(values, gradient):
    return jax.vjp(gelu_tanh, values)[1](gradient)[0]


def norm_forward(values, gain):
    factor = lax.rsqrt(jnp.mean(values * values, axis=-1, keepdims=True) + epsilon)
    scaled = values * factor
    return (scaled * gain, scaled, factor)


def norm_backward(scaled, factor, gain, gradient):
    inner = gradient * gain
    return factor * (inner - scaled * jnp.mean(inner * scaled, axis=-1, keepdims=True))


def split_pack(packed):
    layouts = (
        (LD, 3 * LD),
        (LD, LFF),
        (LD, LD),
        (LFF, LD),
        (LD, VOCAB),
        (VOCAB, LD),
        (GSLOT, LD),
        (D + 2 * LD,),
    )
    pieces = []
    offset = 0
    for layout in layouts:
        length = 1
        for extent in layout:
            length = length * extent
        pieces.append(packed[offset : offset + length].reshape(layout))
        offset = offset + length
    return pieces


def mm(a, b):
    return lax.dot_general(a, b, (((1,), (0,)), ((), ())), preferred_element_type=F32)


def mm_tn(a, b):
    return lax.dot_general(a, b, (((0,), (0,)), ((), ())), preferred_element_type=F32)


def mm_nt(a, b):
    return lax.dot_general(a, b, (((1,), (1,)), ((), ())), preferred_element_type=F32)


def stack_heads(x):
    lane = lax.broadcasted_iota(jnp.int32, x.shape, 1)
    zero = jnp.zeros_like(x)
    return jnp.concatenate([jnp.where(lane < 64, x, zero), jnp.where(lane < 64, zero, x)], axis=0)


def window_fill(rows, width, own_ref, earlier, keys, values_t, values, keys_t):
    for place, ref in enumerate(earlier):
        at = (len(earlier) - 1 - place) * rows
        if keys is not None:
            keys[at : at + rows, :] = ref[:, :width]
        if values is not None:
            values[at : at + rows, :] = ref[:, width:]
        if values_t is not None:
            values_t[:, at : at + rows] = jnp.transpose(ref[:, width:])
        if keys_t is not None:
            keys_t[:, at : at + rows] = jnp.transpose(ref[:, :width])
    at = len(earlier) * rows
    if keys is not None:
        keys[at : at + rows, :] = own_ref[:, width : 2 * width]
    if values is not None:
        values[at : at + rows, :] = own_ref[:, 2 * width :]
    if values_t is not None:
        values_t[:, at : at + rows] = jnp.transpose(own_ref[:, 2 * width :])
    if keys_t is not None:
        keys_t[:, at : at + rows] = jnp.transpose(own_ref[:, width : 2 * width])


def fwd_kernel(rows, width, count, low_ref, start_ref, own_ref, *rest):
    earlier, (att_ref, lse_ref, keys, values_t) = rest[:count], rest[count:]
    window_fill(rows, width, own_ref, earlier, keys, values_t, None, None)
    base = count * rows
    key_iota = lax.broadcasted_iota(jnp.int32, (BLK, 2 * BLK), 0)
    q_iota = lax.broadcasted_iota(jnp.int32, (1, 2 * BLK), 1) % BLK
    pairs = width // 128
    for qt in range(rows // BLK):
        q_pos = q_iota + (base + qt * BLK)
        start = start_ref[qt]
        start = jnp.concatenate([start, start], axis=1)
        for pair in range(pairs):
            cs = slice(pair * 128, pair * 128 + 128)
            qs = stack_heads(own_ref[qt * BLK : (qt + 1) * BLK, cs] * jnp.asarray(0.125, BF16))

            def block(i, carry):
                top, total, acc = carry
                kb = base // BLK + qt - i
                at = pl.ds(pl.multiple_of(kb * BLK, BLK), BLK)
                s = mm_nt(keys[at, cs], qs)
                pos = key_iota + kb * BLK
                s = jnp.where((pos >= start) & (pos <= q_pos), s, masked_score)
                new = jnp.maximum(top, jnp.max(s, axis=0, keepdims=True))
                p = jnp.exp(s - new)
                alpha = jnp.exp(top - new)
                total = total * alpha + jnp.sum(p, axis=0, keepdims=True)
                acc = acc * alpha + mm(values_t[cs, at], p.astype(BF16))
                return new, total, acc

            init = (
                jnp.full((1, 2 * BLK), masked_score, F32),
                jnp.zeros((1, 2 * BLK), F32),
                jnp.zeros((128, 2 * BLK), F32),
            )
            top, total, acc = lax.fori_loop(0, base // BLK + qt + 1 - low_ref[qt], block, init)
            acc = acc * (1.0 / total)
            sub = lax.broadcasted_iota(jnp.int32, (128, BLK), 0)
            both = jnp.where(sub < 64, acc[:, :BLK], acc[:, BLK:])
            att_ref[qt * BLK : (qt + 1) * BLK, cs] = jnp.transpose(both).astype(BF16)
            lse_ref[qt * pairs + pair] = top + jnp.log(total)


def bwd_kernel(rows, width, count, low_ref, start_ref, own_ref, *rest):
    earlier = rest[:count]
    att_ref, attg_ref, lse_ref = rest[count : count + 3]
    dq_ref, dkv_refs = rest[count + 3], rest[count + 4 : 2 * count + 5]
    keys, values, keys_t, dkeys, dvalues = rest[2 * count + 5 :]
    window_fill(rows, width, own_ref, earlier, keys, None, values, keys_t)
    base = count * rows
    dkeys[...] = jnp.zeros_like(dkeys)
    dvalues[...] = jnp.zeros_like(dvalues)
    key_iota = lax.broadcasted_iota(jnp.int32, (BLK, 2 * BLK), 0)
    q_iota = lax.broadcasted_iota(jnp.int32, (1, 2 * BLK), 1) % BLK
    pairs = width // 128
    for qt in range(rows // BLK):
        q_pos = q_iota + (base + qt * BLK)
        start = start_ref[qt]
        start = jnp.concatenate([start, start], axis=1)
        rq = slice(qt * BLK, (qt + 1) * BLK)
        for pair in range(pairs):
            cs = slice(pair * 128, pair * 128 + 128)
            qs = stack_heads(own_ref[rq, cs] * jnp.asarray(0.125, BF16))
            das = stack_heads(attg_ref[rq, cs])
            att = att_ref[rq, cs]
            both = jnp.concatenate([att, att], axis=0).astype(F32) * das.astype(F32)
            delta = jnp.sum(jnp.transpose(both), axis=0, keepdims=True)
            lse = lse_ref[qt * pairs + pair]

            def block(i, acc):
                kb = base // BLK + qt - i
                at = pl.ds(pl.multiple_of(kb * BLK, BLK), BLK)
                s = mm_nt(keys[at, cs], qs)
                pos = key_iota + kb * BLK
                p = jnp.where((pos >= start) & (pos <= q_pos), jnp.exp(s - lse), 0.0)
                dp = mm_nt(values[at, cs], das)
                ds = (p * (dp - delta)).astype(BF16)
                dkeys[at, cs] += mm(ds, qs)
                dvalues[at, cs] += mm(p.astype(BF16), das)
                return acc + mm(keys_t[cs, at], ds)

            acc = lax.fori_loop(
                0, base // BLK + qt + 1 - low_ref[qt], block, jnp.zeros((128, 2 * BLK), F32)
            )
            sub = lax.broadcasted_iota(jnp.int32, (128, BLK), 0)
            both = jnp.where(sub < 64, acc[:, :BLK], acc[:, BLK:]) * 0.125
            dq_ref[rq, cs] = jnp.transpose(both).astype(BF16)
    for place in range(count + 1):
        at = (count - place) * rows
        dkv_refs[place][:, :width] = dkeys[at : at + rows, :].astype(BF16)
        dkv_refs[place][:, width:] = dvalues[at : at + rows, :].astype(BF16)


def specs(n):
    return [pl.BlockSpec(memory_space=pltpu.SMEM)] + [pl.BlockSpec(memory_space=pltpu.VMEM)] * n


def attention_fwd(low, start, own, earlier):
    rows, width = own.shape[0], own.shape[1] // 3
    count = len(earlier)
    span = (count + 1) * rows
    units = rows // BLK * (width // 128)
    return pl.pallas_call(
        functools.partial(fwd_kernel, rows, width, count),
        out_shape=[
            jax.ShapeDtypeStruct((rows, width), BF16),
            jax.ShapeDtypeStruct((units, 1, 2 * BLK), F32),
        ],
        in_specs=specs(2 + count),
        out_specs=[pl.BlockSpec(memory_space=pltpu.VMEM)] * 2,
        scratch_shapes=[pltpu.VMEM((span, width), BF16), pltpu.VMEM((width, span), BF16)],
        compiler_params=pltpu.CompilerParams(vmem_limit_bytes=32 * 2**20),
        name="patch_attention",
    )(low, start, own, *earlier)


def attention_bwd(low, start, own, earlier, attended, attended_grad, lse):
    rows, width = own.shape[0], own.shape[1] // 3
    count = len(earlier)
    span = (count + 1) * rows
    out = pl.pallas_call(
        functools.partial(bwd_kernel, rows, width, count),
        out_shape=[jax.ShapeDtypeStruct((rows, width), BF16)]
        + [jax.ShapeDtypeStruct((rows, 2 * width), BF16)] * (count + 1),
        in_specs=specs(5 + count),
        out_specs=[pl.BlockSpec(memory_space=pltpu.VMEM)] * (count + 2),
        scratch_shapes=[
            pltpu.VMEM((span, width), BF16),
            pltpu.VMEM((span, width), BF16),
            pltpu.VMEM((width, span), BF16),
            pltpu.VMEM((span, width), F32),
            pltpu.VMEM((span, width), F32),
        ],
        compiler_params=pltpu.CompilerParams(vmem_limit_bytes=32 * 2**20),
        name="patch_attention_back",
    )(low, start, own, *earlier, attended, attended_grad, lse)
    return out[0], out[1:]


def gelu_pair(x):
    c = 0.7978845608028654
    x2 = x * x
    t = jnp.tanh(c * (x + 0.044715 * (x2 * x)))
    half = 0.5 * (1.0 + t)
    slope = half + (0.5 * c) * x * (1.0 - t * t) * (1.0 + (3 * 0.044715) * x2)
    return x * half, slope


def byte_kernel(
    rows, tile, with_base,
    inputs_ref, ids_ref, weight_ref, w_in, w_up, w_out, w_down, w_head, w_embed, w_bridge, gains_ref,
    *rest,
):
    if with_base:
        base, rest = rest[:9], rest[9:]
    else:
        base = None
    (g_in, g_up, g_out, g_down, g_head, g_embed, g_bridge, g_gain, loss_ref, inputg_ref,
     hid, proj, probs, att, act, slope, fin, lgrad, bgrad, egrad, attg, projg, sgrad, startv) = rest
    steps = rows // tile
    blocks = tile // 128
    g_gain_local = gains_ref[0:1, :]
    g_gain_final = gains_ref[1:2, :]
    lane = lax.broadcasted_iota(jnp.int32, (128, 128), 1)
    first = (lane < 64)
    r_i = lax.broadcasted_iota(jnp.int32, (256, 128), 0) % 128
    c_i = lax.broadcasted_iota(jnp.int32, (256, 128), 1)
    allowed = (r_i // SLOTS == c_i // SLOTS) & (c_i <= r_i)
    vocab_ids = lax.broadcasted_iota(jnp.int32, (tile, VOCAB), 1)
    zero_low = jnp.zeros((128, 128), BF16)

    def stack(x):
        return jnp.concatenate([jnp.where(first, x, zero_low), jnp.where(first, zero_low, x)], axis=0)

    def norm(v):
        factor = lax.rsqrt(jnp.mean(v * v, axis=-1, keepdims=True) + epsilon)
        return v * factor, factor

    def step(t, carry):
        loss, gl, gf = carry
        at = pl.ds(pl.multiple_of(t * tile, tile), tile)
        inputs = inputs_ref[at, :]
        prev = ids_ref[at, 0:1]
        own = ids_ref[at, 1:2]
        weighting = weight_ref[at, :]
        lookup = jnp.where(prev == vocab_ids, 1.0, 0.0).astype(BF16)
        start = mm(inputs, w_bridge[...]) + mm(lookup, w_embed[...])
        startv[...] = start
        scaled, factor = norm(start)
        hidden = (scaled * g_gain_local).astype(BF16)
        hid[at, :] = hidden
        for c in range(3):
            proj[:, c * LD : (c + 1) * LD] = mm(hidden, w_in[:, c * LD : (c + 1) * LD]).astype(BF16)

        def attend(b, _):
            ra = pl.ds(pl.multiple_of(b * 128, 128), 128)
            for pair in range(4):
                cs = slice(pair * 128, pair * 128 + 128)
                qs = stack(proj[ra, cs] * jnp.asarray(0.125, BF16))
                kp = proj[ra, LD + pair * 128 : LD + pair * 128 + 128]
                vp = proj[ra, 2 * LD + pair * 128 : 2 * LD + pair * 128 + 128]
                s = jnp.where(allowed, mm_nt(qs, kp), masked_score)
                e = jnp.exp(s - jnp.max(s, axis=-1, keepdims=True))
                p = e * (1.0 / jnp.sum(e, axis=-1, keepdims=True))
                probs[b * 4 + pair] = p
                pl_ = p.astype(BF16)
                wide = jnp.concatenate([pl_[:128], pl_[128:]], axis=1)
                att[pl.ds(pl.multiple_of(t * tile + b * 128, 128), 128), cs] = mm(wide, stack(vp)).astype(BF16)
            return 0

        lax.fori_loop(0, blocks, attend, 0)
        attended = att[at, :]
        after = start + mm(attended, w_out[...])
        for c in range(4):
            cs = slice(c * 512, c * 512 + 512)
            a, s = gelu_pair(mm(hidden, w_up[:, cs]))
            a = a.astype(BF16)
            act[at, cs] = a
            slope[:, cs] = s
            after = after + mm(a, w_down[cs, :])
        scaled_f, factor_f = norm(after)
        final = (scaled_f * g_gain_final).astype(BF16)
        fin[at, :] = final
        logits = mm(final, w_head[...])
        hot = jnp.where(own == vocab_ids, 1.0, 0.0)
        top = jnp.max(logits, axis=-1, keepdims=True)
        log_total = top + jnp.log(jnp.sum(jnp.exp(logits - top), axis=-1, keepdims=True))
        loss = loss + jnp.sum(
            weighting * (log_total - jnp.sum(logits * hot, axis=-1, keepdims=True)), axis=0, keepdims=True
        )
        lg = ((jnp.exp(logits - log_total) - hot) * weighting).astype(BF16)
        lgrad[at, :] = lg
        fg = mm_nt(lg, w_head[...])
        gf = gf + jnp.sum(fg * scaled_f, axis=0, keepdims=True)
        inner = fg * g_gain_final
        after_grad = factor_f * (inner - scaled_f * jnp.mean(inner * scaled_f, axis=-1, keepdims=True))
        bg = after_grad.astype(BF16)
        bgrad[at, :] = bg
        attg[...] = mm_nt(bg, w_out[...]).astype(BF16)
        hg = None
        for c in range(4):
            cs = slice(c * 512, c * 512 + 512)
            eg = (slope[:, cs] * mm_nt(bg, w_down[cs, :])).astype(BF16)
            egrad[at, cs] = eg
            term = mm_nt(eg, w_up[:, cs])
            hg = term if hg is None else hg + term

        def attend_back(b, _):
            ra = pl.ds(pl.multiple_of(b * 128, 128), 128)
            rg = pl.ds(pl.multiple_of(t * tile + b * 128, 128), 128)
            for pair in range(4):
                cs = slice(pair * 128, pair * 128 + 128)
                qs = stack(proj[ra, cs] * jnp.asarray(0.125, BF16))
                kp = proj[ra, LD + pair * 128 : LD + pair * 128 + 128]
                vp = proj[ra, 2 * LD + pair * 128 : 2 * LD + pair * 128 + 128]
                das = stack(attg[ra, cs])
                p = probs[b * 4 + pair]
                dp = mm_nt(das, vp)
                ds = (p * (dp - jnp.sum(p * dp, axis=-1, keepdims=True))).astype(BF16)
                wide = jnp.concatenate([ds[:128], ds[128:]], axis=1)
                projg[rg, cs] = (mm(wide, stack(kp)) * 0.125).astype(BF16)
                projg[rg, LD + pair * 128 : LD + pair * 128 + 128] = mm_tn(ds, qs).astype(BF16)
                projg[rg, 2 * LD + pair * 128 : 2 * LD + pair * 128 + 128] = mm_tn(p.astype(BF16), das).astype(BF16)
            return 0

        lax.fori_loop(0, blocks, attend_back, 0)
        for c in range(3):
            hg = hg + mm_nt(projg[at, c * LD : (c + 1) * LD], w_in[:, c * LD : (c + 1) * LD])
        start = startv[...]
        scaled, factor = norm(start)
        gl = gl + jnp.sum(hg * scaled, axis=0, keepdims=True)
        inner = hg * g_gain_local
        sg = (after_grad + factor * (inner - scaled * jnp.mean(inner * scaled, axis=-1, keepdims=True))).astype(BF16)
        sgrad[at, :] = sg
        inputg_ref[at, :] = mm_nt(sg, w_bridge[...]).astype(BF16)
        return loss, gl, gf

    init = (jnp.zeros((1, 1), F32), jnp.zeros((1, LD), F32), jnp.zeros((1, LD), F32))
    loss, gl, gf = lax.fori_loop(0, steps, step, init)

    def put(ref, index, value, which):
        if base is not None:
            value = value + base[which][index].astype(F32)
        ref[index] = value.astype(ref.dtype)

    every = slice(None)
    if base is not None:
        loss = loss + base[8][...]
        gl = gl + base[7][0:1, :]
        gf = gf + base[7][1:2, :]
    loss_ref[...] = loss
    g_gain[0:1, :] = gl
    g_gain[1:2, :] = gf
    hidden_t = jnp.transpose(hid[...])
    for c in range(3):
        cs = slice(c * 512, c * 512 + 512)
        put(g_in, (every, cs), mm(hidden_t, projg[:, cs]), 0)
    for c in range(4):
        cs = slice(c * 512, c * 512 + 512)
        put(g_up, (every, cs), mm(hidden_t, egrad[:, cs]), 1)
    put(g_out, (every, every), mm_tn(att[...], bgrad[...]), 2)
    for c in range(4):
        cs = slice(c * 512, c * 512 + 512)
        put(g_down, (cs, every), mm_tn(act[:, cs], bgrad[...]), 3)
    put(g_head, (every, every), mm_tn(fin[...], lgrad[...]), 4)
    lookup_all = jnp.where(
        ids_ref[:, 0:1] == lax.broadcasted_iota(jnp.int32, (rows, VOCAB), 1), 1.0, 0.0
    ).astype(BF16)
    put(g_embed, (every, every), mm_tn(lookup_all, sgrad[...]), 5)
    put(g_bridge, (every, every), mm_tn(inputs_ref[...], sgrad[...]), 6)


def byte_layer(inputs, ids, weighting, weights, gains, base=None, tile=256):
    rows = inputs.shape[0]
    shapes = [(LD, 3 * LD), (LD, LFF), (LD, LD), (LFF, LD), (LD, VOCAB), (VOCAB, LD), (GSLOT, LD)]
    out_shape = [jax.ShapeDtypeStruct(s, BF16) for s in shapes] + [
        jax.ShapeDtypeStruct((2, LD), F32), jax.ShapeDtypeStruct((1, 1), F32),
        jax.ShapeDtypeStruct((rows, GSLOT), BF16)]
    args = [inputs, ids, weighting, *weights, gains] + (list(base) if base is not None else [])
    vm = pl.BlockSpec(memory_space=pltpu.VMEM)
    return pl.pallas_call(
        functools.partial(byte_kernel, rows, tile, base is not None),
        out_shape=out_shape,
        in_specs=[vm] * len(args),
        out_specs=[vm] * len(out_shape),
        scratch_shapes=[
            pltpu.VMEM((rows, LD), BF16),
            pltpu.VMEM((tile, 3 * LD), BF16),
            pltpu.VMEM((tile // 128 * 4, 256, 128), F32),
            pltpu.VMEM((rows, LD), BF16),
            pltpu.VMEM((rows, LFF), BF16),
            pltpu.VMEM((tile, LFF), F32),
            pltpu.VMEM((rows, LD), BF16),
            pltpu.VMEM((rows, VOCAB), BF16),
            pltpu.VMEM((rows, LD), BF16),
            pltpu.VMEM((rows, LFF), BF16),
            pltpu.VMEM((tile, LD), BF16),
            pltpu.VMEM((rows, 3 * LD), BF16),
            pltpu.VMEM((rows, LD), BF16),
            pltpu.VMEM((tile, LD), F32),
        ],
        compiler_params=pltpu.CompilerParams(vmem_limit_bytes=60 * 2**20),
        name="byte_layer",
    )(*args)


def other(index, offset, size):
    return index ^ offset if size & (size - 1) == 0 else lax.rem(index + offset, size)


def origin(index, offset, size):
    return index ^ offset if size & (size - 1) == 0 else lax.rem(index + size - offset, size)


def place_of(ref, by_column, extent, index):
    at = pl.ds(pl.multiple_of(index * extent, extent), extent)
    return ref.at[:, at] if by_column else ref.at[at, :]


def remote(src, dst, send, recv, device):
    return pltpu.make_async_remote_copy(
        src_ref=src, dst_ref=dst, send_sem=send, recv_sem=recv, device_id=device, device_id_type=MESH
    )


def greet(devices):
    barrier = pltpu.get_barrier_semaphore()
    for device in devices:
        pl.semaphore_signal(barrier, inc=1, device_id=device, device_id_type=MESH)
    pl.semaphore_wait(barrier, len(devices))


def group_peers(slots, groups):
    s, m, d = lax.axis_index("slot"), lax.axis_index("mp"), lax.axis_index("dp")
    across = [(other(s, j, slots), m, d) for j in range(1, slots)]
    beside = [(s, m, other(d, k, groups)) for k in range(1, groups)]
    return across, beside


def stack_peers(stacks):
    s, m, d = lax.axis_index("slot"), lax.axis_index("mp"), lax.axis_index("dp")
    return [(s, other(m, j, stacks), d) for j in range(1, stacks)]


def gather_kernel(sizes, columns, *refs):
    slots, stacks, groups = sizes
    count = len(columns)
    shards, tail = refs[:count], refs[count]
    outs, gain_out = refs[count + 1 : 2 * count + 1], refs[2 * count + 1]
    (tail_z, tail_s, tail_d, own_sem, xs, xr, cs, cr, zs, zr, ts, tr, ds, dr, gs) = refs[2 * count + 2 :]
    s, d = lax.axis_index("slot"), lax.axis_index("dp")
    across, beside = group_peers(slots, groups)
    above = stack_peers(stacks)
    greet(across + beside + above)

    def place(w, slot, group):
        extent = shards[w].shape[1 if columns[w] else 0]
        return place_of(outs[w], columns[w], extent, slot * groups + group)

    pending = []
    tail_copies = [
        remote(tail, tail_z.at[j], zs.at[j], zr.at[j], above[j - 1]) for j in range(1, stacks)
    ]
    own_tail = pltpu.make_async_copy(tail, tail_z.at[0], gs.at[0])
    own_tail.start()
    for copy in tail_copies:
        copy.start()
    sends = {}
    for w in range(count):
        for j in range(1, slots):
            copy = remote(shards[w], place(w, s, d), xs.at[w, j], xr.at[w, j], across[j - 1])
            copy.start()
            sends[w, j] = copy
        for k in range(1, groups):
            copy = remote(shards[w], place(w, s, d), cs.at[w, 0, k], cr.at[w, 0, k], beside[k - 1])
            copy.start()
            pending.append(copy)
        copy = pltpu.make_async_copy(shards[w], place(w, s, d), own_sem.at[w])
        copy.start()
        sends[w, 0] = copy

    m = lax.axis_index("mp")
    own_tail.wait()
    for copy in tail_copies:
        copy.wait()
    chosen = tail_z[0]
    for j in range(1, stacks):
        chosen = jnp.where(origin(m, j, stacks) == stacks - 1, tail_z[j], chosen)
    tail_s[0] = chosen
    step = [remote(tail_s.at[0], tail_s.at[j], ts.at[j], tr.at[j], across[j - 1]) for j in range(1, slots)]
    for copy in step:
        copy.start()
    for copy in step:
        copy.wait()
    chosen = tail_s[0]
    for j in range(1, slots):
        chosen = jnp.where(origin(s, j, slots) == slots - 1, tail_s[j], chosen)
    tail_d[0] = chosen
    step = [remote(tail_d.at[0], tail_d.at[k], ds.at[k], dr.at[k], beside[k - 1]) for k in range(1, groups)]
    for copy in step:
        copy.start()
    for copy in step:
        copy.wait()
    chosen = tail_d[0]
    for k in range(1, groups):
        chosen = jnp.where(origin(d, k, groups) == groups - 1, tail_d[k], chosen)
    gain_out[...] = chosen.astype(F32)

    for w in range(count):
        for j in range(1, slots):
            here = place(w, origin(s, j, slots), d)
            remote(here, here, xs.at[w, j], xr.at[w, j], across[j - 1]).wait_recv()
            for k in range(1, groups):
                copy = remote(here, here, cs.at[w, j, k], cr.at[w, j, k], beside[k - 1])
                copy.start()
                pending.append(copy)
    for w in range(count):
        sends[w, 0].wait()
        for j in range(1, slots):
            sends[w, j].wait_send()
    for copy in pending:
        copy.wait()


def gather_weights(shards, columns, tail):
    sizes = tuple(lax.axis_size(axis) for axis in ("slot", "mp", "dp"))
    slots, stacks, groups = sizes
    count = len(shards)
    parts = slots * groups
    shapes = [
        (v.shape[0], v.shape[1] * parts) if c else (v.shape[0] * parts, v.shape[1])
        for v, c in zip(shards, columns)
    ]
    anywhere = pl.BlockSpec(memory_space=pl.ANY)
    dma = pltpu.SemaphoreType.DMA
    return pl.pallas_call(
        functools.partial(gather_kernel, sizes, columns),
        out_shape=[jax.ShapeDtypeStruct(shape, BF16) for shape in shapes]
        + [jax.ShapeDtypeStruct(tail.shape, F32)],
        in_specs=[anywhere] * (count + 1),
        out_specs=[anywhere] * count + [pl.BlockSpec(memory_space=pltpu.VMEM)],
        scratch_shapes=[
            pltpu.VMEM((stacks,) + tail.shape, BF16),
            pltpu.VMEM((slots,) + tail.shape, BF16),
            pltpu.VMEM((groups,) + tail.shape, BF16),
            dma((count,)),
            dma((count, slots)), dma((count, slots)),
            dma((count, slots, groups)), dma((count, slots, groups)),
            dma((stacks,)), dma((stacks,)),
            dma((slots,)), dma((slots,)),
            dma((groups,)), dma((groups,)),
            dma((1,)),
        ],
        compiler_params=pltpu.CompilerParams(collective_id=1, has_side_effects=True),
        name="gather_weights",
    )(*shards, tail)


def scatter_kernel(sizes, columns, extents, *refs):
    slots, stacks, groups = sizes
    count = len(columns)
    partials, outs = refs[:count], refs[count : 2 * count]
    rest = refs[2 * count :]
    from_core, stage, from_slot = rest[:count], rest[count : 2 * count], rest[2 * count : 3 * count]
    from_z, own_c, from_c, cs, cr, xs, xr, zs, zr, ts, tr = rest[3 * count :]
    s, m, d = lax.axis_index("slot"), lax.axis_index("mp"), lax.axis_index("dp")
    across, beside = group_peers(slots, groups)
    above = stack_peers(stacks)
    greet(across + beside + above)
    order = (count - 1,) + tuple(range(count - 1))

    def part(w, slot, group):
        return place_of(partials[w], columns[w], extents[w], slot * groups + group)

    first = {}
    for w in order:
        for j in tuple(range(1, slots)) + (0,):
            t = other(s, j, slots)
            for k in range(1, groups):
                copy = remote(
                    part(w, t, other(d, k, groups)), from_core[w].at[j, k - 1],
                    cs.at[w, j, k], cr.at[w, j, k], beside[k - 1],
                )
                copy.start()
                first[w, j, k] = copy
    second = {}
    for w in order:
        for j in tuple(range(1, slots)) + (0,):
            t = other(s, j, slots)
            for k in range(1, groups):
                first[w, j, k].wait_recv()
            total = part(w, t, d)[...].astype(F32)
            for k in range(1, groups):
                total = total + from_core[w][j, k - 1].astype(F32)
            if j:
                stage[w][j] = total.astype(BF16)
                copy = remote(stage[w].at[j], from_slot[w].at[j], xs.at[w, j], xr.at[w, j], across[j - 1])
                copy.start()
                second[w, j] = copy
            else:
                outs[w][: total.shape[0]] = total
    for w in order:
        for j in range(1, slots):
            second[w, j].wait_recv()
        total = outs[w][: from_slot[w].shape[1]]
        for j in range(1, slots):
            total = total + from_slot[w][j].astype(F32)
        outs[w][: total.shape[0]] = total
        if w == order[0]:
            from_z[m] = total.astype(BF16)
            third = [
                remote(from_z.at[m], from_z.at[m], zs.at[j], zr.at[j], above[j - 1])
                for j in range(1, stacks)
            ]
            for copy in third:
                copy.start()
    w = order[0]
    size = from_slot[w].shape[1]
    for copy in third:
        copy.wait()
    total = from_z[0].astype(F32)
    for j in range(1, stacks):
        total = total + from_z[j].astype(F32)
    own_c[...] = total.astype(BF16)
    fourth = [remote(own_c, from_c.at[k], ts.at[k], tr.at[k], beside[k - 1]) for k in range(1, groups)]
    for copy in fourth:
        copy.start()
    outs[w][pl.ds(pl.multiple_of(d * size, size), size), :] = own_c[...].astype(F32)
    for k in range(1, groups):
        fourth[k - 1].wait()
        outs[w][pl.ds(pl.multiple_of(origin(d, k, groups) * size, size), size), :] = from_c[k].astype(F32)
    for copy in first.values():
        copy.wait_send()
    for copy in second.values():
        copy.wait_send()


def scatter_grads(partials, columns):
    sizes = tuple(lax.axis_size(axis) for axis in ("slot", "mp", "dp"))
    slots, stacks, groups = sizes
    count = len(partials)
    parts = slots * groups
    blocks = [
        (v.shape[0], v.shape[1] // parts) if c else (v.shape[0] // parts, v.shape[1])
        for v, c in zip(partials, columns)
    ]
    extents = tuple(b[1] if c else b[0] for b, c in zip(blocks, columns))
    shapes = blocks[:-1] + [(blocks[-1][0] * groups, blocks[-1][1])]
    vm = pl.BlockSpec(memory_space=pltpu.VMEM)
    dma = pltpu.SemaphoreType.DMA
    last = blocks[-1]
    return pl.pallas_call(
        functools.partial(scatter_kernel, sizes, columns, extents),
        out_shape=[jax.ShapeDtypeStruct(shape, F32) for shape in shapes],
        in_specs=[vm] * count,
        out_specs=[vm] * count,
        scratch_shapes=[pltpu.VMEM((slots, groups - 1) + b, BF16) for b in blocks]
        + [pltpu.VMEM((slots,) + b, BF16) for b in blocks]
        + [pltpu.VMEM((slots,) + b, BF16) for b in blocks]
        + [
            pltpu.VMEM((stacks,) + last, BF16),
            pltpu.VMEM(last, BF16), pltpu.VMEM((groups,) + last, BF16),
            dma((count, slots, groups)), dma((count, slots, groups)),
            dma((count, slots)), dma((count, slots)),
            dma((stacks,)), dma((stacks,)),
            dma((groups,)), dma((groups,)),
        ],
        compiler_params=pltpu.CompilerParams(
            collective_id=2, has_side_effects=True, vmem_limit_bytes=48 * 2**20
        ),
        name="scatter_grads",
    )(*partials)


def total_kernel(sizes, value, out, held_z, held_s, held_d, zs, zr, xs, xr, cs, cr):
    slots, stacks, groups = sizes
    across, beside = group_peers(slots, groups)
    above = stack_peers(stacks)
    greet(across + beside + above)
    total = value[...]
    for axis, peers, held, send, recv in (
        ("mp", above, held_z, zs, zr), ("slot", across, held_s, xs, xr), ("dp", beside, held_d, cs, cr)
    ):
        index = lax.axis_index(axis)
        held[index] = total
        copies = [
            remote(held.at[index], held.at[index], send.at[j], recv.at[j], peer)
            for j, peer in enumerate(peers)
        ]
        for copy in copies:
            copy.start()
        for copy in copies:
            copy.wait()
        total = held[0]
        for j in range(1, len(peers) + 1):
            total = total + held[j]
    out[...] = total


def total_of(value):
    sizes = tuple(lax.axis_size(axis) for axis in ("slot", "mp", "dp"))
    slots, stacks, groups = sizes
    vm = pl.BlockSpec(memory_space=pltpu.VMEM)
    dma = pltpu.SemaphoreType.DMA
    return pl.pallas_call(
        functools.partial(total_kernel, sizes),
        out_shape=jax.ShapeDtypeStruct(value.shape, F32),
        in_specs=[vm],
        out_specs=vm,
        scratch_shapes=[pltpu.VMEM((size,) + value.shape, F32) for size in (stacks, slots, groups)]
        + [dma((size,)) for size in (stacks, stacks, slots, slots, groups, groups)],
        compiler_params=pltpu.CompilerParams(collective_id=3, has_side_effects=True),
        name="total_of",
    )(value)


def pieces_of(size):
    return max(step for step in range(16, 129, 16) if size % step == 0)


def pack_layout():
    layout = []
    offset = 0
    for height, breadth in (
        (LD, 3 * LD), (LD, LFF), (LD, LD), (LFF, LD), (LD, VOCAB), (VOCAB, LD), (GSLOT, LD)
    ):
        layout.append((offset, height, breadth // 128))
        offset += height * breadth // 128
    return layout, offset


def unpack_kernel(share, rows, count, blocks_ref, *refs):
    outs, flat = refs[:-1], refs[-1]
    chunk = pieces_of(rows)
    flat[0:8, :] = jnp.zeros((8, 128), F32)

    def block(b, _):
        top = lax.div(b * share, 128)
        held = flat[pl.ds(top, 1), :]
        for i in range(0, rows, chunk):
            source = pl.ds(pl.multiple_of(b * rows, 16) + i, chunk)
            flat[pl.ds(top + i, chunk), :] = blocks_ref[source, :].astype(F32)
        flat[pl.ds(top, 1), :] = flat[pl.ds(top, 1), :] + held
        return 0

    lax.fori_loop(0, count, block, 0)
    layout, _ = pack_layout()
    for out, (offset, height, breadth) in zip(outs, layout):
        def part(i, _, out=out, offset=offset, breadth=breadth):
            for c in range(breadth):
                values = flat[pl.ds(offset + i * (128 * breadth) + c, 128, stride=breadth), :]
                out[pl.ds(pl.multiple_of(i * 128, 128), 128), c * 128 : (c + 1) * 128] = values.astype(BF16)
            return 0
        lax.fori_loop(0, height // 128, part, 0)


def unpack(blocks, share):
    rows = block_rows(share)
    count = blocks.shape[0] // rows
    layout, used = pack_layout()
    vm = pl.BlockSpec(memory_space=pltpu.VMEM)
    return pl.pallas_call(
        functools.partial(unpack_kernel, share, rows, count),
        out_shape=[jax.ShapeDtypeStruct((h, b * 128), BF16) for _, h, b in layout],
        in_specs=[vm],
        out_specs=[vm] * len(layout),
        scratch_shapes=[pltpu.VMEM((share * count // 128 + rows + 8, 128), F32)],
        compiler_params=pltpu.CompilerParams(vmem_limit_bytes=48 * 2**20),
        name="unpack",
    )(blocks)


def pack_kernel(share, rows, count, *refs):
    matrices, out, flat = refs[:-2], refs[-2], refs[-1]
    chunk = pieces_of(rows)
    layout, used = pack_layout()
    for matrix, (offset, height, breadth) in zip(matrices, layout):
        def part(i, _, matrix=matrix, offset=offset, breadth=breadth):
            for c in range(breadth):
                values = matrix[pl.ds(pl.multiple_of(i * 128, 128), 128), c * 128 : (c + 1) * 128]
                flat[pl.ds(offset + i * (128 * breadth) + c, 128, stride=breadth), :] = values.astype(F32)
            return 0
        lax.fori_loop(0, height // 128, part, 0)
    spare = flat.shape[0] - used
    flat[used:, :] = jnp.zeros((spare, 128), F32)

    def block(b, _):
        top = lax.div(b * share, 128)
        for i in range(0, rows, chunk):
            target = pl.ds(pl.multiple_of(b * rows, 16) + i, chunk)
            out[target, :] = flat[pl.ds(top + i, chunk), :].astype(BF16)
        return 0

    lax.fori_loop(0, count, block, 0)


def pack(matrices, share):
    rows = block_rows(share)
    layout, used = pack_layout()
    total = used + (D + 2 * LD) // 128
    count = total * 128 // share
    vm = pl.BlockSpec(memory_space=pltpu.VMEM)
    return pl.pallas_call(
        functools.partial(pack_kernel, share, rows, count),
        out_shape=jax.ShapeDtypeStruct((count * rows, 128), BF16),
        in_specs=[vm] * len(layout),
        out_specs=vm,
        scratch_shapes=[pltpu.VMEM((total + rows + 8, 128), F32)],
        compiler_params=pltpu.CompilerParams(vmem_limit_bytes=48 * 2**20),
        name="pack",
    )(*matrices)


def partner(index, offset, size):
    return index ^ offset if size & (size - 1) == 0 else (index + offset) % size


def swap(value, axis, offset):
    size = lax.axis_size(axis)
    if size & (size - 1) == 0:
        pairs = [(i, i ^ offset) for i in range(size)]
    else:
        pairs = [(i, (i + offset) % size) for i in range(size)]
    return lax.ppermute(value, axis, pairs)


def source(index, offset, size):
    return index ^ offset if size & (size - 1) == 0 else (index + size - offset) % size


def scatter_rows(partial, axis):
    size = lax.axis_size(axis)
    index = lax.axis_index(axis)
    share = partial.shape[0] // size
    pieces = []
    for offset in range(1, size):
        block = lax.dynamic_slice_in_dim(partial, partner(index, offset, size) * share, share, 0)
        pieces.append(swap(block.astype(BF16), axis, offset))
    total = lax.dynamic_slice_in_dim(partial, index * share, share, 0).astype(F32)
    for piece in pieces:
        total = total + piece.astype(F32)
    return total


def gather_rows(block, axis):
    size = lax.axis_size(axis)
    index = lax.axis_index(axis)
    share = block.shape[0]
    whole = jnp.zeros((size * share,) + block.shape[1:], block.dtype)
    whole = lax.dynamic_update_slice_in_dim(whole, block, index * share, 0)
    for offset in range(1, size):
        whole = lax.dynamic_update_slice_in_dim(
            whole, swap(block, axis, offset), source(index, offset, size) * share, 0
        )
    return whole


def shift_chunks(value, distance, forward):
    size = lax.axis_size("slot")
    if forward:
        pairs = [(i, i + distance) for i in range(size - distance)]
    else:
        pairs = [(i + distance, i) for i in range(size - distance)]
    return lax.ppermute(value, "slot", pairs)


def update(weight, moment, average, gradient, factor, rate):
    step_grad = factor * gradient
    moment_next = momentum_keep * moment + step_grad
    weight_next = weight - rate * (step_grad + momentum_keep * moment_next)
    average_next = average_keep * average + (1.0 - average_keep) * weight_next
    return (weight_next, moment_next, average_next)


def block_rows(share):
    return -(-(-(-share // 128) + 1) // 16) * 16


def gather_pack(local_pack):
    share = local_pack.shape[0]
    index = lax.axis_index(("slot", "mp", "dp"))
    offset = lax.rem(index * share, 128)
    rows = block_rows(share)
    block = lax.dynamic_update_slice_in_dim(
        jnp.zeros((rows * 128,), BF16), local_pack.astype(BF16), offset, 0
    )
    return lax.all_gather(block.reshape(rows, 128), ("slot", "mp", "dp"), axis=0, tiled=True)


def scatter_pack(blocks, share):
    own = lax.psum_scatter(blocks, ("slot", "mp", "dp"), scatter_dimension=0, tiled=True)
    index = lax.axis_index(("slot", "mp", "dp"))
    offset = lax.rem(index * share, 128)
    return lax.dynamic_slice_in_dim(own.reshape(-1), offset, share, 0).astype(F32)


def local(
    byte_ids, item_ids, loss_mask,
    attend_in, expand_in, attend_out, expand_out, slot_table, local_pack,
    moment_attend_in, moment_expand_in, moment_attend_out, moment_expand_out,
    moment_slot_table, moment_local_pack,
    average_attend_in, average_expand_in, average_attend_out, average_expand_out,
    average_slot_table, average_local_pack,
):
    slot_size, mp_size = lax.axis_size("slot"), lax.axis_size("mp")
    slot_index, mp_index, dp_index = (
        lax.axis_index("slot"), lax.axis_index("mp"), lax.axis_index("dp"),
    )
    mask_count = lax.psum(jnp.sum(loss_mask.astype(F32)), "dp")
    part = attend_in.shape[0]
    width = attend_in.shape[2]
    piece = slot_table.shape[0] * VOCAB // lax.axis_size("dp")
    table_shard = lax.dynamic_slice_in_dim(
        slot_table.reshape(-1, GSLOT), dp_index * piece, piece, 0
    ).astype(BF16)
    tail = local_pack[-(D + 2 * LD) :].astype(BF16).reshape(-1, 128)
    pack_whole = gather_pack(local_pack)
    shards = [table_shard, attend_in.astype(BF16).reshape(part, 3 * width), expand_in.astype(BF16)]
    late = [attend_out.astype(BF16), expand_out.astype(BF16)]
    wide = attend_out.shape[1] % 128 == 0
    if wide:
        table, full_in_flat, full_expand, full_out, full_shrink, gains = gather_weights(
            shards + late, (False, False, False, True, True), tail
        )
    else:
        table, full_in_flat, full_expand, gains = gather_weights(shards, (False, False, False), tail)
        full_out, full_shrink = (
            lax.all_gather(v, ("slot", "dp"), axis=1, tiled=True) for v in late
        )
    table = table.reshape(SLOTS, VOCAB, GSLOT)
    gains = gains.reshape(-1)
    gain_global = gains[:D]
    local_gains = gains[D:].reshape(2, LD)
    unpacked = unpack(pack_whole, local_pack.shape[0])
    group_rows = byte_ids.shape[1]
    rows = group_rows // slot_size
    local_rows = rows // mp_size
    vocab_ids = jnp.arange(VOCAB)
    reach = min(slot_size - 1, -(-(longest_item - 1) // rows))
    micros = []
    for micro in range(byte_ids.shape[0]):
        forward = micro % 2 == 0
        chunk = slot_index if forward else slot_size - 1 - slot_index
        group_ids = byte_ids[micro]
        items = item_ids[micro, 0]
        begin = chunk * rows
        previous = jnp.concatenate([jnp.full((1, SLOTS), -1, jnp.int32), group_ids[:-1]], axis=0)
        earlier_item = jnp.concatenate([items[:1], items[:-1]])
        previous = jnp.where((items == earlier_item)[:, None], previous, -1)
        own_previous = lax.dynamic_slice_in_dim(previous, begin, rows, 0)
        own_items = lax.dynamic_slice_in_dim(items, begin, rows, 0)
        first = jnp.sum((items[None, :] < own_items[:, None]).astype(jnp.int32), axis=1)
        first = jnp.maximum(first - (chunk - reach) * rows, 0)
        lookup = (own_previous[:, :, None] == vocab_ids).astype(BF16)
        start_rows = (
            jnp.einsum("pjv,jvg->pjg", lookup, table, preferred_element_type=F32)
            .astype(BF16).reshape(rows, D).astype(F32)
        )
        normed, scaled, factor = norm_forward(start_rows, gain_global)
        hidden = normed.astype(BF16)
        projected = product(hidden, full_in_flat).astype(BF16)
        own_kv = projected[:, width:]
        earlier = [shift_chunks(own_kv, d, forward) for d in range(1, reach + 1)]
        expanded = product(hidden, full_expand)
        active = gelu_tanh(expanded).astype(BF16)
        begin_local = begin + mp_index * local_rows
        micros.append(dict(
            forward=forward, group_ids=group_ids, begin_local=begin_local, start_rows=start_rows,
            hidden=hidden, projected=projected, earlier=earlier,
            expanded=expanded, active=active, low=first[::BLK] // BLK,
            first=first.reshape(-1, 1, BLK), own_previous=own_previous, mask=loss_mask[micro],
        ))
    for m in micros:
        m["attended"], m["lse"] = attention_fwd(m["low"], m["first"], m["projected"], m["earlier"])
        branch = scatter_rows(
            product(m["attended"], full_out) + product(m["active"], full_shrink), "mp"
        )
        m["own_start"] = lax.dynamic_slice_in_dim(
            m["start_rows"], mp_index * local_rows, local_rows, 0
        )
        m["middle"] = m["own_start"] + branch
    base = None
    for m in micros:
        ids = lax.dynamic_slice_in_dim(m["group_ids"], m["begin_local"], local_rows, 0)
        mask = lax.dynamic_slice_in_dim(m["mask"], m["begin_local"], local_rows, 0)
        before = jnp.concatenate([jnp.full((local_rows, 1), -1, jnp.int32), ids[:, :-1]], axis=1)
        weighting = mask.reshape(-1, 1).astype(F32) / mask_count
        out = byte_layer(
            m["middle"].astype(BF16).reshape(-1, GSLOT),
            jnp.stack([before.reshape(-1), ids.reshape(-1)], axis=1),
            weighting, unpacked[:7], local_gains, base,
        )
        base = out[:9]
        m["own_back"] = out[9].reshape(local_rows, D)
        m["branch_grad"] = gather_rows(m["own_back"], "mp")
    matrices, local_gain_grads, loss_sum = base[:7], base[7], base[8][0, 0]
    sums = None
    table_grad = None
    gain_global_grad = None
    for m in micros:
        branch_grad = m["branch_grad"]
        grad_out = gram_product(m["attended"], branch_grad)
        grad_shrink = gram_product(m["active"], branch_grad)
        attended_grad = back_product(branch_grad, full_out).astype(BF16)
        expanded_grad = gelu_back(m["expanded"], back_product(branch_grad, full_shrink)).astype(BF16)
        grad_expand = gram_product(m["hidden"], expanded_grad)
        query_grad, kv_grads = attention_bwd(
            m["low"], m["first"], m["projected"], m["earlier"], m["attended"], attended_grad, m["lse"]
        )
        kv_total = kv_grads[0].astype(F32)
        for d in range(1, reach + 1):
            kv_total = kv_total + shift_chunks(kv_grads[d], d, not m["forward"]).astype(F32)
        projected_grad = jnp.concatenate([query_grad, kv_total.astype(BF16)], axis=1)
        grad_in = gram_product(m["hidden"], projected_grad)
        hidden_grad = scatter_rows(
            back_product(projected_grad, full_in_flat) + back_product(expanded_grad, full_expand), "mp"
        )
        _, scaled, factor = norm_forward(m["own_start"], gain_global)
        gain_term = jnp.sum(hidden_grad * scaled, axis=0)
        start_grad = (
            m["own_back"].astype(F32) + norm_backward(scaled, factor, gain_global, hidden_grad)
        ).astype(BF16)
        own_lookup = lax.dynamic_slice_in_dim(m["own_previous"], mp_index * local_rows, local_rows, 0)
        own_lookup = (own_lookup[:, :, None] == vocab_ids).astype(BF16)
        table_term = jnp.einsum(
            "pjv,pjg->jvg", own_lookup, start_grad.reshape(local_rows, SLOTS, GSLOT),
            preferred_element_type=F32,
        )
        terms = (grad_in, grad_expand, grad_out, grad_shrink)
        if sums is None:
            sums, table_grad, gain_global_grad = terms, table_term, gain_term
        else:
            sums = tuple(a + b for a, b in zip(sums, terms))
            table_grad = table_grad + table_term
            gain_global_grad = gain_global_grad + gain_term
    sums = tuple(s.astype(BF16) for s in sums)
    gain_grads = jnp.concatenate([gain_global_grad, local_gain_grads.reshape(-1)])
    parts = slot_size * lax.axis_size("dp")
    small = jnp.concatenate(
        [
            table_grad.astype(BF16).reshape(parts, -1, GSLOT),
            jnp.broadcast_to(gain_grads.astype(BF16).reshape(1, -1, GSLOT), (parts, 16, GSLOT)),
        ],
        axis=1,
    ).reshape(-1, GSLOT)
    if wide:
        own_in, own_expand, own_out, own_shrink, own_small = scatter_grads(
            [*sums, small], (False, False, True, True, False)
        )
    else:
        own_in, own_expand, own_small = scatter_grads([*sums[:2], small], (False, False, False))
        own_out, own_shrink = (
            lax.psum_scatter(v, ("slot", "dp"), scatter_dimension=1, tiled=True).astype(F32)
            for v in sums[2:]
        )
    own_in = own_in.reshape(attend_in.shape)
    own_small = own_small.reshape(lax.axis_size("dp"), piece + 16, GSLOT)
    own_table = own_small[:, :piece].reshape(slot_table.shape)
    gain_total = own_small[0, piece:].reshape(-1)
    own_pack = scatter_pack(pack(matrices, local_pack.shape[0]), local_pack.shape[0])
    last = (slot_index == slot_size - 1) & (mp_index == mp_size - 1)
    last = last & (dp_index == lax.axis_size("dp") - 1)
    own_pack = jnp.concatenate(
        [own_pack[: -gain_total.shape[0]], jnp.where(last, gain_total, own_pack[-gain_total.shape[0] :])]
    )
    owner = ((mp_index == 0) & (dp_index == 0)).astype(F32)
    squares = jnp.sum(own_pack * own_pack) + owner * jnp.sum(own_table * own_table)
    for gradient in (own_in, own_expand, own_out, own_shrink):
        squares = squares + jnp.sum(gradient * gradient)
    both = total_of(jnp.stack([jnp.full((8, 128), squares), jnp.full((8, 128), loss_sum)]))
    total_squares, loss_value = both[0, 0, 0], both[1, 0, 0]
    clip_norm = jnp.sqrt(total_squares)
    factor = clip_max / jnp.maximum(clip_norm, clip_max)
    results = [loss_value * mask_count, mask_count, clip_norm]
    for weight, moment, average, gradient, rate in (
        (attend_in, moment_attend_in, average_attend_in, own_in, rate_dense),
        (expand_in, moment_expand_in, average_expand_in, own_expand, rate_dense),
        (attend_out, moment_attend_out, average_attend_out, own_out, rate_project),
        (expand_out, moment_expand_out, average_expand_out, own_shrink, rate_dense),
        (slot_table, moment_slot_table, average_slot_table, own_table, rate_table),
        (local_pack, moment_local_pack, average_local_pack, own_pack, rate_dense),
    ):
        results.extend(update(weight, moment, average, gradient, factor, rate))
    return tuple(results)


def solution(mesh):
    placed = (
        P(None, "dp", None),
        P(None, "dp", None),
        P(None, "dp", None),
        P(("slot", "dp"), None, "mp"),
        P(("slot", "dp"), "mp"),
        P("mp", ("slot", "dp")),
        P("mp", ("slot", "dp")),
        P("slot", None, None),
        P(("slot", "mp", "dp")),
        P(("slot", "dp"), None, "mp"),
        P(("slot", "dp"), "mp"),
        P("mp", ("slot", "dp")),
        P("mp", ("slot", "dp")),
        P("slot", None, None),
        P(("slot", "mp", "dp")),
        P(("slot", "dp"), None, "mp"),
        P(("slot", "dp"), "mp"),
        P("mp", ("slot", "dp")),
        P("mp", ("slot", "dp")),
        P("slot", None, None),
        P(("slot", "mp", "dp")),
    )
    return jax.shard_map(
        local,
        mesh=mesh,
        in_specs=placed,
        out_specs=(
            P(),
            P(),
            P(),
            P(("slot", "dp"), None, "mp"),
            P(("slot", "dp"), None, "mp"),
            P(("slot", "dp"), None, "mp"),
            P(("slot", "dp"), "mp"),
            P(("slot", "dp"), "mp"),
            P(("slot", "dp"), "mp"),
            P("mp", ("slot", "dp")),
            P("mp", ("slot", "dp")),
            P("mp", ("slot", "dp")),
            P("mp", ("slot", "dp")),
            P("mp", ("slot", "dp")),
            P("mp", ("slot", "dp")),
            P("slot", None, None),
            P("slot", None, None),
            P("slot", None, None),
            P(("slot", "mp", "dp")),
            P(("slot", "mp", "dp")),
            P(("slot", "mp", "dp")),
        ),
        check_vma=False,
    )
```

time: 1360 us -> 596 us (0.44)
  waiting for transfers between devices: 539 us -> 55.7 us
  Pallas kernels: 0 us -> 292 us
  matrix products: 316 us -> 55 us
  local copies, waits for them, and re-layouts: 273 us -> 78.7 us
  other arithmetic: 120 us -> 33.7 us
  blocking collectives: 53.6 us -> 3.57 us
  starting transfers between devices: 19.2 us -> 46.6 us
    pallas_call x0 -> x11, Pallas kernels: none -> 292 us  [the longest x2 114 us: byte_layer(): pl.pallas_call(functools.partial(byte_kernel, rows, tile, base is not Non...]
    unnamed x25 -> x2, waiting for transfers between devices: 238 us -> 0.03 us
    reduce_scatter x10 -> x1, waiting for transfers between devices: 163 us -> 0.01 us  [scatter_pack(): lax.psum_scatter(blocks, ('slot', 'mp', 'dp'), scatter_dimension=0, tiled...]
    dot_general x28 -> x4, matrix products: 124 us -> 8.26 us  [the longest x2 7.66 us: local(): jnp.einsum('pjv,jvg->pjg', lookup, table, preferred_element_type=F32)]
    psum x2 -> x0, waiting for transfers between devices: 80.5 us -> none  [the longest x1 80.5 us: local(): lax.psum(hidden_grad.astype(jnp.bfloat16), 'mp').astype(jnp.float32)]
    unnamed x543 -> x170, local copies, waits for them, and re-layouts: 98.6 us -> 25.9 us
    reshape x21 -> x6, local copies, waits for them, and re-layouts: 66.7 us -> 7.33 us  [the longest x2 3.58 us: local(): m['own_back'] = out[9].reshape(local_rows, D)]
    dot_general x20 -> x8, matrix products: 71.5 us -> 15.5 us  [back_product(): lax.dot_general(left, right, (((1,), (1,)), ((), ())), preferred_element_...]
  transfers between devices with their start and end apart: 27 -> 28, of which waited for: 13 -> 5; matrix products, arithmetic and copies ran while one was open for 29% -> 21% of each run, Pallas kernels for 0% -> 26%
where the time goes in v1:
time: 596 us; the launch traced here: 589 us
  Pallas kernels  292 us (49%)
  local copies, waits for them, and re-layouts  78.7 us (13%)
  waiting for transfers between devices  55.7 us (9%)
  matrix products  55 us (9%)
  starting transfers between devices  46.6 us (8%)
  other arithmetic  33.7 us (6%)
  between operations  23.8 us (4%)
    pallas_call x2, Pallas kernels, byte_layer(): pl.pallas_call(functools.partial(byte_kernel, rows, tile, base is not Non...  114 us
    pallas_call x1, Pallas kernels, gather_weights(): pl.pallas_call(functools.partial(gather_kernel, sizes, columns), out_shap...  60.7 us
    ppermute x18, waiting for transfers between devices, swap(): return lax.ppermute(value, axis, pairs)  55.6 us
    pallas_call x1, Pallas kernels, scatter_grads(): pl.pallas_call(functools.partial(scatter_kernel, sizes, columns, extents)...  50.3 us
    ppermute x18, starting transfers between devices, swap(): return lax.ppermute(value, axis, pairs)  30.3 us
    unnamed x170, local copies, waits for them, and re-layouts  25.9 us
    pallas_call x2, Pallas kernels, attention_bwd(): pl.pallas_call(functools.partial(bwd_kernel, rows, width, count), out_sha...  18.9 us
    dot_general x8, matrix products, gram_product(): lax.dot_general(left, right, (((0,), (0,)), ((), ())), preferred_element_...  16.5 us
  transfers between devices with their start and end apart: 28, of which 5 were waited for; matrix products, arithmetic and copies ran while one was open for 21% of the time, Pallas kernels for 26%

profile of v1, /device:TPU:0, one launch (start us, length us, event | category | flops | bytes accessed | tf_op | source)
XLA Modules:
  0.0 588.6 jit_solution(1883940064838957435)
XLA Ops:
  17.7 60.7 %gather_weights.1 = (bf16[2048,128]{1,0:T(8,128)(2,1)}, bf16[1024,768]{1,0:T(8,128)(2,1)}, bf16[1024,1024]{1,0:T(8,128)(2,1)}, bf16[256,1024]{1,0:T(8,128)(2,1)}...) custom-call(bf16[256,128]{1,0:T(8,128)(2,1)} %dynamic-slice_convert_fusion.13.refs_0_, bf16[128,768]{1,0:T(8,128)(2,1)} %copy.111.refs_1_, ...), custom_call_target="tpu_custom_call" | custom-call | tf_op jit(solution)/shard_map/gather_weights/pallas_call | solution.py:608
  80.4 3.6 multiply_reduce_fusion
  86.1 4.1 multiply_reduce_fusion.1
  90.1 2.9 copy.113
  100.3 2.9 collective-permute-start.6
  108.3 3.6 psum.7
  116.9 3.3 fusion.54
  122.9 2.8 fusion.45
  125.7 2.8 fusion.44
  129.1 4.4 patch_attention.3
  141.1 11.6 %patch_attention.2 = (bf16[512,256]{1,0:T(8,128)(2,1)S(1)}, f32[4,1,512]{2,1,0:T(1,128)S(1)}) custom-call(s32[2]{0:T(128)S(1)} %and_select_fusion.1.low_ref, s32[2,1,256]{2,1,0:T(1,128)S(1)} %bitcast.104, bf16[512,768]{1,0:T(8,128)(2,1)S(1)} %convolution_convert_fusion.1.own_ref, bf16[512,512]{1,0:T(8,128)(2,1)} %collective-permute-done.rest_0_, ...), custom_call_target="tpu_custom_call" | custom-call | tf_op jit(solution)/shard_map/patch_attention/pallas_call | solution.py:235
  155.4 3.4 collective-permute-start.3
  177.9 4.3 collective-permute-done.3
  185.8 7.9 %unpack.1 = (bf16[512,1536]{1,0:T(8,128)(2,1)S(1)}, bf16[512,2048]{1,0:T(8,128)(2,1)S(1)}, bf16[512,512]{1,0:T(8,128)(2,1)S(1)}, bf16[2048,512]{1,0:T(8,128)(2,1...) custom-call(bf16[27648,128]{1,0:T(8,128)(2,1)} %all-gather.2.cloned.1.call-done.blocks_ref), custom_call_target="tpu_custom_call" | custom-call | tf_op jit(solution)/shard_map/unpack/pallas_call | solution.py:834
  199.1 55.9 %byte_layer.2 = (bf16[512,1536]{1,0:T(8,128)(2,1)}, bf16[512,2048]{1,0:T(8,128)(2,1)}, bf16[512,512]{1,0:T(8,128)(2,1)}, bf16[2048,512]{1,0:T(8,128)(2,1)}, bf16...) custom-call(bf16[1024,128]{1,0:T(8,128)(2,1)} %reshape.314.inputs_re, ...), custom_call_target="tpu_custom_call" | custom-call | tf_op jit(solution)/shard_map/byte_layer/pallas_call | solution.py:453
  255.0 58.2 %byte_layer.3 = (bf16[512,1536]{1,0:T(8,128)(2,1)}, bf16[512,2048]{1,0:T(8,128)(2,1)}, bf16[512,512]{1,0:T(8,128)(2,1)}, bf16[2048,512]{1,0:T(8,128)(2,1)}, bf16...) custom-call(bf16[1024,128]{1,0:T(8,128)(2,1)} %reshape.311.inputs_re, ...), custom_call_target="tpu_custom_call" | custom-call | tf_op jit(solution)/shard_map/byte_layer/pallas_call | solution.py:453
  315.0 5.1 collective-permute-start.15
  340.7 8.4 %pack.1 = bf16[27648,128]{1,0:T(8,128)(2,1)} custom-call(bf16[512,1536]{1,0:T(8,128)(2,1)S(1)} %copy-done.4, bf16[512,2048]{1,0:T(8,128)(2,1)S(1)} %copy-done.3, bf16[512,512]{1,0:T(8,128)(2,1)S(1)} %copy-done.8, bf16[2048,512]{1,0:T(8,128)(2,1)} %get-tuple-element.98.refs_3_, bf16[512,256]{1,0:T(8,128)(2,1)S(1)} %copy-done.9, ...), custom_call_target="tpu_custom_call" | custom-call | tf_op jit(solution)/shard_map/pack/pallas_call | solution.py:875
  358.4 13.4 %patch_attention_back.3 = (bf16[512,256]{1,0:T(8,128)(2,1)S(1)}, bf16[512,512]{1,0:T(8,128)(2,1)S(1)}, bf16[512,512]{1,0:T(8,128)(2,1)S(1)}, bf16[512,512]{1,0:T(8,128)(2,1)S(1)}) custom-call(s32[2]{0:T(128)S(1)} %copy-done.17, s32[2,1,256]{2,1,0:T(1,128)S(1)} %bitcast.105, bf16[512,768]{1,0:T(8,128)(2,1)S(1)} %convolution_convert_fusion.1.own_ref, ...), custom_call_target="tpu_custom_call" | custom-call | tf_op jit(solution)/shard_map/patch_attention_back/pallas_call | solution.py:253
  373.1 3.6 collective-permute-start.19
  382.6 5.5 patch_attention_back.2
  394.8 3.7 fusion.8
  400.2 3.6 fusion.15
  406.6 2.8 fusion.43
  412.0 4.3 add_convert_fusion.refs_3_
  418.9 4.4 collective-permute-start.23
  430.1 14.3 %collective-permute-done.23 = bf16[128,1024]{1,0:T(8,128)(2,1)S(1)} collective-permute-done((bf16[128,1024]{1,0:T(8,128)(2,1)S(1)}, bf16[128,1024]{1,0:T(8,128)(2,1)S(1)}, u32[]{:S(2)}, u32[]{:S(2)}) %collective-permute-start.23) | collective-permute-done | bytes 262176 | tf_op jit(solution)/shard_map/ppermute | solution.py:896
  446.1 5.0 collective-permute-done.24
  451.2 4.6 collective-permute-done.20
  455.8 27.3 %collective-permute-done.21 = bf16[128,1024]{1,0:T(8,128)(2,1)S(1)} collective-permute-done((bf16[128,1024]{1,0:T(8,128)(2,1)S(1)}, bf16[128,1024]{1,0:T(8,128)(2,1)S(1)}, u32[]{:S(2)}, u32[]{:S(2)}) %collective-permute-start.21) | collective-permute-done | bytes 262176 | tf_op jit(solution)/shard_map/ppermute | solution.py:896
  485.1 50.3 %scatter_grads.1 = (f32[128,768]{1,0:T(8,128)S(1)}, f32[128,1024]{1,0:T(8,128)S(1)}, f32[256,128]{1,0:T(8,128)S(1)}, f32[1024,128]{1,0:T(8,128)S(1)}, f32[544,128]{1,0:T(8,128)S(1)}) custom-call(bf16[1024,768]{1,0:T(8,128)(2,1)S(1)} %add_convert_fusion.2.refs_0_, bf16[1024,1024]{1,0:T(8,128)(2,1)} %add_convert_fusion.1.refs_1_, ...), custom_call_target="tpu_custom_call" | custom-call | tf_op jit(solution)/shard_map/scatter_grads/pallas_call | solution.py:724
  546.0 15.2 %total_of.1 = f32[2,8,128]{2,1,0:T(8,128)} custom-call(f32[2,8,128]{2,1,0:T(8,128)} %stack.14.value), custom_call_target="tpu_custom_call" | custom-call | tf_op jit(solution)/shard_map/total_of/pallas_call | solution.py:777
  (350 shorter events, 160.9 us)
Async XLA Ops:
  7.2 178.6 %all-gather.2.cloned.1.call-start = ((), (), s32[]{:S(2)}) async-start(), calls=%async_computation.1 | async-start | bytes 7299072 | tf_op jit(solution)/shard_map/all_gather | solution.py:959
  11.2 528.3 %reduce-scatter.2.cloned.1.call-start = ((), (), s32[]{:S(2)}) async-start(), calls=%async_computation.2 | async-start | bytes 7299072 | tf_op jit(solution)/shard_map/reduce_scatter | solution.py:963
  11.3 67.0 %copy-start.64 = (s32[2,1,2048]{2,1,0:T(1,128)S(1)}, s32[2,1,2048]{2,1,0:T(1,128)}, u32[]{:S(2)}) copy-start(s32[2,1,2048]{2,1,0:T(1,128)} %param.22) | copy-start | bytes 49156
  12.4 67.9 %copy-start.30 = (f32[128,3,256]{0,2,1:T(8,128)}, f32[128,3,256]{0,2,1:T(8,128)S(1)}, u32[]{:S(2)}) copy-start(f32[128,3,256]{0,2,1:T(8,128)S(1)} %copy.110) | copy-start | bytes 1179652
  12.5 67.8 %copy-start.47 = (s32[2,2048,8]{1,2,0:T(8,128)S(1)}, s32[2,2048,8]{1,2,0:T(8,128)}, u32[]{:S(2)}) copy-start(s32[2,2048,8]{1,2,0:T(8,128)} %param.21) | copy-start | bytes 393220
  97.7 31.4 %collective-permute-start.5 = (bf16[512,512]{1,0:T(8,128)(2,1)}, bf16[512,512]{1,0:T(8,128)(2,1)S(1)}, u32[]{:S(2)}, u32[]{:S(2)}) collective-permute-start(bf16[512,512]{1,0:T(8,128)(2,1)} %slice.131), channel_id=1, source_target_pairs={{0,8},{8,16},{16,24},{1,9},{9,17},{17,25},{2,10},{10,18},{18,26},{... | collective-permute-start | bytes 1572872 | tf_op jit(solution)/shard_map/ppermute | solution.py:936
  100.3 28.8 %collective-permute-start.6 = (bf16[512,512]{1,0:T(8,128)(2,1)}, bf16[512,512]{1,0:T(8,128)(2,1)S(1)}, u32[]{:S(2)}, u32[]{:S(2)}) collective-permute-start(bf16[512,512]{1,0:T(8,128)(2,1)} %slice.131), channel_id=1, source_target_pairs={{0,16},{8,24},{1,17},{9,25},{2,18},{10,26},{3,19},{11,27},{4,20},{... | collective-permute-start | bytes 1572872 | tf_op jit(solution)/shard_map/ppermute | solution.py:936
  105.1 36.0 %collective-permute-start = (bf16[512,512]{1,0:T(8,128)(2,1)}, bf16[512,512]{1,0:T(8,128)(2,1)}, u32[]{:S(2)}, u32[]{:S(2)}) collective-permute-start(bf16[512,512]{1,0:T(8,128)(2,1)} %slice.130), channel_id=1, source_target_pairs={{8,0},{16,8},{24,16},{9,1},{17,9},{25,17},{10,2},{18,10},{26,18},{... | collective-permute-start | bytes 1572872 | tf_op jit(solution)/shard_map/ppermute | solution.py:936
  107.1 34.1 %collective-permute-start.1 = (bf16[512,512]{1,0:T(8,128)(2,1)}, bf16[512,512]{1,0:T(8,128)(2,1)}, u32[]{:S(2)}, u32[]{:S(2)}) collective-permute-start(bf16[512,512]{1,0:T(8,128)(2,1)} %slice.130), channel_id=1, source_target_pairs={{16,0},{24,8},{17,1},{25,9},{18,2},{26,10},{19,3},{27,11},{20,4},{... | collective-permute-start | bytes 1572872 | tf_op jit(solution)/shard_map/ppermute | solution.py:936
  136.7 22.1 %collective-permute-start.7 = (bf16[128,1024]{1,0:T(8,128)(2,1)S(1)}, bf16[128,1024]{1,0:T(8,128)(2,1)S(1)}, u32[]{:S(2)}, u32[]{:S(2)}) collective-permute-start(bf16[128,1024]{1,0:T(8,128)(2,1)S(1)} %get-tuple-element.219), channel_id=1, source_target_pairs={{0,2},{2,0},{4,6},{6,4},{1,3},{3,1},{5,7},{7,5},{8,10},{10,8},{12,... | collective-permute-start | bytes 786440 | tf_op jit(solution)/shard_map/ppermute | solution.py:896
  138.1 37.4 %collective-permute-start.8 = (bf16[128,1024]{1,0:T(8,128)(2,1)}, bf16[128,1024]{1,0:T(8,128)(2,1)}, u32[]{:S(2)}, u32[]{:S(2)}) collective-permute-start(bf16[128,1024]{1,0:T(8,128)(2,1)} %get-tuple-element.221), channel_id=1, source_target_pairs={{0,4},{2,6},{4,0},{6,2},{1,5},{3,7},{5,1},{7,3},{8,12},{10,14},{12... | collective-permute-start | bytes 786440 | tf_op jit(solution)/shard_map/ppermute | solution.py:896
  140.6 34.9 %collective-permute-start.9 = (bf16[128,1024]{1,0:T(8,128)(2,1)}, bf16[128,1024]{1,0:T(8,128)(2,1)}, u32[]{:S(2)}, u32[]{:S(2)}) collective-permute-start(bf16[128,1024]{1,0:T(8,128)(2,1)} %get-tuple-element.220), channel_id=1, source_target_pairs={{0,6},{2,4},{4,2},{6,0},{1,7},{3,5},{5,3},{7,1},{8,14},{10,12},{12... | collective-permute-start | bytes 786440 | tf_op jit(solution)/shard_map/ppermute | solution.py:896
  155.0 23.0 %collective-permute-start.2 = (bf16[128,1024]{1,0:T(8,128)(2,1)}, bf16[128,1024]{1,0:T(8,128)(2,1)}, u32[]{:S(2)}, u32[]{:S(2)}) collective-permute-start(bf16[128,1024]{1,0:T(8,128)(2,1)} %get-tuple-element.222), channel_id=1, source_target_pairs={{0,2},{2,0},{4,6},{6,4},{1,3},{3,1},{5,7},{7,5},{8,10},{10,8},{12,... | collective-permute-start | bytes 786440 | tf_op jit(solution)/shard_map/ppermute | solution.py:896
  155.4 26.8 %collective-permute-start.3 = (bf16[128,1024]{1,0:T(8,128)(2,1)}, bf16[128,1024]{1,0:T(8,128)(2,1)}, u32[]{:S(2)}, u32[]{:S(2)}) collective-permute-start(bf16[128,1024]{1,0:T(8,128)(2,1)} %get-tuple-element.224), channel_id=1, source_target_pairs={{0,4},{2,6},{4,0},{6,2},{1,5},{3,7},{5,1},{7,3},{8,12},{10,14},{12... | collective-permute-start | bytes 786440 | tf_op jit(solution)/shard_map/ppermute | solution.py:896
  159.5 22.7 %collective-permute-start.4 = (bf16[128,1024]{1,0:T(8,128)(2,1)}, bf16[128,1024]{1,0:T(8,128)(2,1)}, u32[]{:S(2)}, u32[]{:S(2)}) collective-permute-start(bf16[128,1024]{1,0:T(8,128)(2,1)} %get-tuple-element.223), channel_id=1, source_target_pairs={{0,6},{2,4},{4,2},{6,0},{1,7},{3,5},{5,3},{7,1},{8,14},{10,12},{12... | collective-permute-start | bytes 786440 | tf_op jit(solution)/shard_map/ppermute | solution.py:896
  315.0 34.1 %collective-permute-start.15 = (bf16[128,1024]{1,0:T(8,128)(2,1)}, bf16[128,1024]{1,0:T(8,128)(2,1)}, u32[]{:S(2)}, u32[]{:S(2)}) collective-permute-start(bf16[128,1024]{1,0:T(8,128)(2,1)} %reshape.317), channel_id=1, source_target_pairs={{0,2},{2,0},{4,6},{6,4},{1,3},{3,1},{5,7},{7,5},{8,10},{10,8},{12,... | collective-permute-start | bytes 786440 | tf_op jit(solution)/shard_map/ppermute | solution.py:896
  321.3 31.8 %collective-permute-start.16 = (bf16[128,1024]{1,0:T(8,128)(2,1)}, bf16[128,1024]{1,0:T(8,128)(2,1)}, u32[]{:S(2)}, u32[]{:S(2)}) collective-permute-start(bf16[128,1024]{1,0:T(8,128)(2,1)} %reshape.317), channel_id=1, source_target_pairs={{0,4},{2,6},{4,0},{6,2},{1,5},{3,7},{5,1},{7,3},{8,12},{10,14},{12... | collective-permute-start | bytes 786440 | tf_op jit(solution)/shard_map/ppermute | solution.py:896
  322.4 32.5 %collective-permute-start.17 = (bf16[128,1024]{1,0:T(8,128)(2,1)}, bf16[128,1024]{1,0:T(8,128)(2,1)}, u32[]{:S(2)}, u32[]{:S(2)}) collective-permute-start(bf16[128,1024]{1,0:T(8,128)(2,1)} %reshape.317), channel_id=1, source_target_pairs={{0,6},{2,4},{4,2},{6,0},{1,7},{3,5},{5,3},{7,1},{8,14},{10,12},{12... | collective-permute-start | bytes 786440 | tf_op jit(solution)/shard_map/ppermute | solution.py:896
  325.6 51.1 %collective-permute-start.10 = (bf16[128,1024]{1,0:T(8,128)(2,1)}, bf16[128,1024]{1,0:T(8,128)(2,1)}, u32[]{:S(2)}, u32[]{:S(2)}) collective-permute-start(bf16[128,1024]{1,0:T(8,128)(2,1)} %reshape.316), channel_id=1, source_target_pairs={{0,2},{2,0},{4,6},{6,4},{1,3},{3,1},{5,7},{7,5},{8,10},{10,8},{12,... | collective-permute-start | bytes 786440 | tf_op jit(solution)/shard_map/ppermute | solution.py:896
  326.6 51.8 %collective-permute-start.11 = (bf16[128,1024]{1,0:T(8,128)(2,1)}, bf16[128,1024]{1,0:T(8,128)(2,1)}, u32[]{:S(2)}, u32[]{:S(2)}) collective-permute-start(bf16[128,1024]{1,0:T(8,128)(2,1)} %reshape.316), channel_id=1, source_target_pairs={{0,4},{2,6},{4,0},{6,2},{1,5},{3,7},{5,1},{7,3},{8,12},{10,14},{12... | collective-permute-start | bytes 786440 | tf_op jit(solution)/shard_map/ppermute | solution.py:896
  350.0 30.1 %collective-permute-start.12 = (bf16[128,1024]{1,0:T(8,128)(2,1)S(1)}, bf16[128,1024]{1,0:T(8,128)(2,1)S(1)}, u32[]{:S(2)}, u32[]{:S(2)}) collective-permute-start(bf16[128,1024]{1,0:T(8,128)(2,1)S(1)} %copy-done.34), channel_id=1, source_target_pairs={{0,6},{2,4},{4,2},{6,0},{1,7},{3,5},{5,3},{7,1},{8,14},{10,12},{12... | collective-permute-start | bytes 786440 | tf_op jit(solution)/shard_map/ppermute | solution.py:896
  371.8 44.5 %collective-permute-start.18 = (bf16[512,512]{1,0:T(8,128)(2,1)S(1)}, bf16[512,512]{1,0:T(8,128)(2,1)S(1)}, u32[]{:S(2)}, u32[]{:S(2)}) collective-permute-start(bf16[512,512]{1,0:T(8,128)(2,1)S(1)} %get-tuple-element.112), channel_id=1, source_target_pairs={{0,8},{8,16},{16,24},{1,9},{9,17},{17,25},{2,10},{10,18},{18,26},{... | collective-permute-start | bytes 1572872 | tf_op jit(solution)/shard_map/ppermute | solution.py:936
  373.1 43.2 %collective-permute-start.19 = (bf16[512,512]{1,0:T(8,128)(2,1)S(1)}, bf16[512,512]{1,0:T(8,128)(2,1)S(1)}, u32[]{:S(2)}, u32[]{:S(2)}) collective-permute-start(bf16[512,512]{1,0:T(8,128)(2,1)S(1)} %get-tuple-element.113), channel_id=1, source_target_pairs={{0,16},{8,24},{1,17},{9,25},{2,18},{10,26},{3,19},{11,27},{4,20},{... | collective-permute-start | bytes 1572872 | tf_op jit(solution)/shard_map/ppermute | solution.py:936
  388.1 37.6 %collective-permute-start.13 = (bf16[512,512]{1,0:T(8,128)(2,1)S(1)}, bf16[512,512]{1,0:T(8,128)(2,1)S(1)}, u32[]{:S(2)}, u32[]{:S(2)}) collective-permute-start(bf16[512,512]{1,0:T(8,128)(2,1)S(1)} %get-tuple-element.106), channel_id=1, source_target_pairs={{8,0},{16,8},{24,16},{9,1},{17,9},{25,17},{10,2},{18,10},{26,18},{... | collective-permute-start | bytes 1572872 | tf_op jit(solution)/shard_map/ppermute | solution.py:936
  389.4 36.3 %collective-permute-start.14 = (bf16[512,512]{1,0:T(8,128)(2,1)S(1)}, bf16[512,512]{1,0:T(8,128)(2,1)S(1)}, u32[]{:S(2)}, u32[]{:S(2)}) collective-permute-start(bf16[512,512]{1,0:T(8,128)(2,1)S(1)} %get-tuple-element.107), channel_id=1, source_target_pairs={{16,0},{24,8},{17,1},{25,9},{18,2},{26,10},{19,3},{27,11},{20,4},{... | collective-permute-start | bytes 1572872 | tf_op jit(solution)/shard_map/ppermute | solution.py:936
  418.9 25.5 %collective-permute-start.23 = (bf16[128,1024]{1,0:T(8,128)(2,1)S(1)}, bf16[128,1024]{1,0:T(8,128)(2,1)S(1)}, u32[]{:S(2)}, u32[]{:S(2)}) collective-permute-start(bf16[128,1024]{1,0:T(8,128)(2,1)S(1)} %get-tuple-element.209), channel_id=1, source_target_pairs={{0,2},{2,0},{4,6},{6,4},{1,3},{3,1},{5,7},{7,5},{8,10},{10,8},{12,... | collective-permute-start | bytes 786440 | tf_op jit(solution)/shard_map/ppermute | solution.py:896
  423.2 27.9 %collective-permute-start.24 = (bf16[128,1024]{1,0:T(8,128)(2,1)S(1)}, bf16[128,1024]{1,0:T(8,128)(2,1)S(1)}, u32[]{:S(2)}, u32[]{:S(2)}) collective-permute-start(bf16[128,1024]{1,0:T(8,128)(2,1)S(1)} %get-tuple-element.211), channel_id=1, source_target_pairs={{0,4},{2,6},{4,0},{6,2},{1,5},{3,7},{5,1},{7,3},{8,12},{10,14},{12... | collective-permute-start | bytes 786440 | tf_op jit(solution)/shard_map/ppermute | solution.py:896
  423.3 27.9 %collective-permute-start.25 = (bf16[128,1024]{1,0:T(8,128)(2,1)S(1)}, bf16[128,1024]{1,0:T(8,128)(2,1)S(1)}, u32[]{:S(2)}, u32[]{:S(2)}) collective-permute-start(bf16[128,1024]{1,0:T(8,128)(2,1)S(1)} %get-tuple-element.210), channel_id=1, source_target_pairs={{0,6},{2,4},{4,2},{6,0},{1,7},{3,5},{5,3},{7,1},{8,14},{10,12},{12... | collective-permute-start | bytes 786440 | tf_op jit(solution)/shard_map/ppermute | solution.py:896
  427.0 28.8 %collective-permute-start.20 = (bf16[128,1024]{1,0:T(8,128)(2,1)S(1)}, bf16[128,1024]{1,0:T(8,128)(2,1)S(1)}, u32[]{:S(2)}, u32[]{:S(2)}) collective-permute-start(bf16[128,1024]{1,0:T(8,128)(2,1)S(1)} %get-tuple-element.212), channel_id=1, source_target_pairs={{0,2},{2,0},{4,6},{6,4},{1,3},{3,1},{5,7},{7,5},{8,10},{10,8},{12,... | collective-permute-start | bytes 786440 | tf_op jit(solution)/shard_map/ppermute | solution.py:896
  428.1 55.0 %collective-permute-start.21 = (bf16[128,1024]{1,0:T(8,128)(2,1)S(1)}, bf16[128,1024]{1,0:T(8,128)(2,1)S(1)}, u32[]{:S(2)}, u32[]{:S(2)}) collective-permute-start(bf16[128,1024]{1,0:T(8,128)(2,1)S(1)} %get-tuple-element.214), channel_id=1, source_target_pairs={{0,4},{2,6},{4,0},{6,2},{1,5},{3,7},{5,1},{7,3},{8,12},{10,14},{12... | collective-permute-start | bytes 786440 | tf_op jit(solution)/shard_map/ppermute | solution.py:896
  444.4 38.7 %copy-start.72 = (f32[128]{0:T(128)S(1)}, f32[128]{0:T(128)}, u32[]{:S(2)}) copy-start(f32[128]{0:T(128)} %add_rsqrt_fusion.2) | copy-start | bytes 1540
  444.4 38.7 %collective-permute-start.22 = (bf16[128,1024]{1,0:T(8,128)(2,1)S(1)}, bf16[128,1024]{1,0:T(8,128)(2,1)S(1)}, u32[]{:S(2)}, u32[]{:S(2)}) collective-permute-start(bf16[128,1024]{1,0:T(8,128)(2,1)S(1)} %get-tuple-element.213), channel_id=1, source_target_pairs={{0,6},{2,4},{4,2},{6,0},{1,7},{3,5},{5,3},{7,1},{8,14},{10,12},{12... | collective-permute-start | bytes 786440 | tf_op jit(solution)/shard_map/ppermute | solution.py:896
  (77 other events, 659.8 us)
Sparse Core Ops, SparseCore 0:
  11.6 82.9 all-gather.1
  349.2 155.1 reduce-scatter.1

commit v2 on v1

--- a/solution.py
+++ b/solution.py
@@ -173,11 +173,18 @@
             lse_ref[qt * pairs + pair] = top + jnp.log(total)
 
 
-def bwd_kernel(rows, width, count, low_ref, start_ref, own_ref, *rest):
+def bwd_kernel(rows, width, count, pieces, low_ref, start_ref, own_ref, *rest):
     earlier = rest[:count]
-    att_ref, attg_ref, lse_ref = rest[count : count + 3]
-    dq_ref, dkv_refs = rest[count + 3], rest[count + 4 : 2 * count + 5]
-    keys, values, keys_t, dkeys, dvalues = rest[2 * count + 5 :]
+    att_ref, lse_ref, weight_ref = rest[count : count + 3]
+    rest = rest[count + 3 :]
+    piece_refs, rest = rest[:pieces], rest[pieces:]
+    branch_ref, dq_ref, dkv_refs = rest[0], rest[1], rest[2 : count + 3]
+    keys, values, keys_t, dkeys, dvalues, attg_ref = rest[count + 3 :]
+    place, share = lax.axis_index("mp"), rows // pieces
+    for j in range(pieces):
+        at = pl.ds(pl.multiple_of(origin(place, j, pieces) * share, share), share)
+        branch_ref[at, :] = piece_refs[j][...]
+    attg_ref[...] = mm_nt(branch_ref[...], weight_ref[...]).astype(BF16)
     window_fill(rows, width, own_ref, earlier, keys, None, values, keys_t)
     base = count * rows
     dkeys[...] = jnp.zeros_like(dkeys)
@@ -241,32 +248,82 @@
         in_specs=specs(2 + count),
         out_specs=[pl.BlockSpec(memory_space=pltpu.VMEM)] * 2,
         scratch_shapes=[pltpu.VMEM((span, width), BF16), pltpu.VMEM((width, span), BF16)],
+        cost_estimate=pl.CostEstimate(flops=6 * 10**9, bytes_accessed=20 * 10**6, transcendentals=10**6),
         compiler_params=pltpu.CompilerParams(vmem_limit_bytes=32 * 2**20),
         name="patch_attention",
     )(low, start, own, *earlier)
 
 
-def attention_bwd(low, start, own, earlier, attended, attended_grad, lse):
+def attention_bwd(low, start, own, earlier, attended, lse, weight, pieces):
     rows, width = own.shape[0], own.shape[1] // 3
     count = len(earlier)
     span = (count + 1) * rows
     out = pl.pallas_call(
-        functools.partial(bwd_kernel, rows, width, count),
-        out_shape=[jax.ShapeDtypeStruct((rows, width), BF16)]
+        functools.partial(bwd_kernel, rows, width, count, len(pieces)),
+        out_shape=[jax.ShapeDtypeStruct((rows, pieces[0].shape[1]), BF16), jax.ShapeDtypeStruct((rows, width), BF16)]
         + [jax.ShapeDtypeStruct((rows, 2 * width), BF16)] * (count + 1),
-        in_specs=specs(5 + count),
-        out_specs=[pl.BlockSpec(memory_space=pltpu.VMEM)] * (count + 2),
+        in_specs=specs(5 + count + len(pieces)),
+        out_specs=[pl.BlockSpec(memory_space=pltpu.VMEM)] * (count + 3),
         scratch_shapes=[
             pltpu.VMEM((span, width), BF16),
             pltpu.VMEM((span, width), BF16),
             pltpu.VMEM((width, span), BF16),
             pltpu.VMEM((span, width), F32),
             pltpu.VMEM((span, width), F32),
+            pltpu.VMEM((rows, width), BF16),
         ],
+        cost_estimate=pl.CostEstimate(flops=8 * 10**9, bytes_accessed=25 * 10**6, transcendentals=10**6),
         compiler_params=pltpu.CompilerParams(vmem_limit_bytes=32 * 2**20),
         name="patch_attention_back",
-    )(low, start, own, *earlier, attended, attended_grad, lse)
-    return out[0], out[1:]
+    )(low, start, own, *earlier, attended, lse, weight, *pieces)
+    return out[0], out[1], out[2:]
+
+
+def embed_kernel(width, ids_ref, table_ref, w_ref, gain_ref, start_ref, hidden_ref, proj_ref, kv_ref):
+    rows = ids_ref.shape[0]
+    ids = ids_ref[...].astype(F32)
+    low = lax.broadcasted_iota(jnp.int32, (rows, 128), 1).astype(F32)
+    squares = jnp.zeros((rows, 1), F32)
+    parts = []
+    for j in range(SLOTS):
+        own = jnp.broadcast_to(ids[:, j : j + 1], (rows, 128))
+        hot = jnp.concatenate(
+            [jnp.where(own == low, 1.0, 0.0), jnp.where(own == low + 128.0, 1.0, 0.0)], axis=1
+        ).astype(BF16)
+        part = mm(hot, table_ref[j * VOCAB : (j + 1) * VOCAB, :])
+        parts.append(part)
+        squares = squares + jnp.sum(part * part, axis=-1, keepdims=True)
+    factor = lax.rsqrt(squares * (1.0 / D) + epsilon)
+    for j in range(SLOTS):
+        cs = slice(j * GSLOT, (j + 1) * GSLOT)
+        start_ref[:, cs] = parts[j].astype(BF16)
+        hidden_ref[:, cs] = (parts[j] * factor * gain_ref[:, cs]).astype(BF16)
+    hidden = hidden_ref[...]
+    for c in range(3):
+        cs = slice(c * width, (c + 1) * width)
+        part = mm(hidden, w_ref[:, cs]).astype(BF16)
+        proj_ref[:, cs] = part
+        if c:
+            kv_ref[:, (c - 1) * width : c * width] = part
+
+
+def embed_rows(ids, table, weight, gain):
+    rows, width = ids.shape[0], weight.shape[1] // 3
+    vm = pl.BlockSpec(memory_space=pltpu.VMEM)
+    return pl.pallas_call(
+        functools.partial(embed_kernel, width),
+        out_shape=[
+            jax.ShapeDtypeStruct((rows, D), BF16),
+            jax.ShapeDtypeStruct((rows, D), BF16),
+            jax.ShapeDtypeStruct((rows, 3 * width), BF16),
+            jax.ShapeDtypeStruct((rows, 2 * width), BF16),
+        ],
+        in_specs=[vm] * 4,
+        out_specs=[vm] * 4,
+        cost_estimate=pl.CostEstimate(flops=2 * 10**9, bytes_accessed=6 * 10**6, transcendentals=1000),
+        compiler_params=pltpu.CompilerParams(vmem_limit_bytes=32 * 2**20),
+        name="embed_rows",
+    )(ids, table, weight, gain)
 
 
 def gelu_pair(x):
@@ -280,29 +337,60 @@
 
 def byte_kernel(
     rows, tile, with_base,
-    inputs_ref, ids_ref, weight_ref, w_in, w_up, w_out, w_down, w_head, w_embed, w_bridge, gains_ref,
-    *rest,
+    pieces, start_ref, own_ref, *rest
 ):
+    piece_refs, rest = rest[:pieces], rest[pieces:]
+    ids_ref, mask_ref, count_ref, w_in, w_up, w_out, w_down, w_head, w_embed, w_bridge, gains_ref = rest[:11]
+    rest = rest[11:]
     if with_base:
         base, rest = rest[:9], rest[9:]
     else:
         base = None
     (g_in, g_up, g_out, g_down, g_head, g_embed, g_bridge, g_gain, loss_ref, inputg_ref,
-     hid, proj, probs, att, act, slope, fin, lgrad, bgrad, egrad, attg, projg, sgrad, startv) = rest
+     hid, proj, probs, att, act, slope, fin, lgrad, bgrad, egrad, attg, projg, sgrad, startv, att_t, projg_t,
+     wide_rows, own_ids, prev_ids, weights, inputs_ref) = rest
     steps = rows // tile
     blocks = tile // 128
     g_gain_local = gains_ref[0:1, :]
     g_gain_final = gains_ref[1:2, :]
-    lane = lax.broadcasted_iota(jnp.int32, (128, 128), 1)
-    first = (lane < 64)
-    r_i = lax.broadcasted_iota(jnp.int32, (256, 128), 0) % 128
-    c_i = lax.broadcasted_iota(jnp.int32, (256, 128), 1)
-    allowed = (r_i // SLOTS == c_i // SLOTS) & (c_i <= r_i)
-    vocab_ids = lax.broadcasted_iota(jnp.int32, (tile, VOCAB), 1)
+    first = lax.broadcasted_iota(jnp.int32, (128, 128), 1) < 64
+    lane = lax.broadcasted_iota(jnp.int32, (SLOTS, 256), 1) % 128
+    patch = lane // SLOTS
+    causal = lax.broadcasted_iota(jnp.int32, (SLOTS, 256), 0) <= lane % SLOTS
+    none = jnp.zeros((SLOTS, 256), F32)
+    patches = rows // SLOTS
+    for j in range(SLOTS):
+        cs = slice(j * GSLOT, (j + 1) * GSLOT)
+        at = pl.ds(j, patches, stride=SLOTS)
+        total = own_ref[:, cs] + start_ref[:, cs].astype(F32)
+        for piece in piece_refs:
+            total = total + piece[:, cs].astype(F32)
+        wide_rows[at, :] = total
+        spread = functools.partial(jnp.broadcast_to, shape=(patches, 128))
+        own_ids[at, :] = spread(ids_ref[:, j : j + 1].astype(F32))
+        prev_ids[at, :] = spread(ids_ref[:, j - 1 : j].astype(F32)) if j else jnp.full((patches, 128), -1.0, F32)
+        weights[at, :] = spread(mask_ref[:, j : j + 1].astype(F32) / count_ref[0, 0])
+    inputs_ref[...] = wide_rows[...].astype(BF16)
+
+    def one_hot(ids):
+        low = lax.broadcasted_iota(jnp.int32, ids.shape, 1).astype(F32)
+        return jnp.concatenate(
+            [jnp.where(ids == low, 1.0, 0.0), jnp.where(ids == low + 128.0, 1.0, 0.0)], axis=1
+        )
+
     zero_low = jnp.zeros((128, 128), BF16)
 
     def stack(x):
         return jnp.concatenate([jnp.where(first, x, zero_low), jnp.where(first, zero_low, x)], axis=0)
+
+    def narrow(x):
+        out = x[:SLOTS]
+        for j in range(1, 16):
+            out = jnp.where(patch == j, x[j * SLOTS : (j + 1) * SLOTS], out)
+        return out
+
+    def widen(x):
+        return jnp.concatenate([jnp.where(patch == j, x, none) for j in range(16)], axis=0)
 
     def norm(v):
         factor = lax.rsqrt(jnp.mean(v * v, axis=-1, keepdims=True) + epsilon)
@@ -312,10 +400,8 @@
         loss, gl, gf = carry
         at = pl.ds(pl.multiple_of(t * tile, tile), tile)
         inputs = inputs_ref[at, :]
-        prev = ids_ref[at, 0:1]
-        own = ids_ref[at, 1:2]
-        weighting = weight_ref[at, :]
-        lookup = jnp.where(prev == vocab_ids, 1.0, 0.0).astype(BF16)
+        weighting = weights[at, :]
+        lookup = one_hot(prev_ids[at, :]).astype(BF16)
         start = mm(inputs, w_bridge[...]) + mm(lookup, w_embed[...])
         startv[...] = start
         scaled, factor = norm(start)
@@ -325,42 +411,47 @@
             proj[:, c * LD : (c + 1) * LD] = mm(hidden, w_in[:, c * LD : (c + 1) * LD]).astype(BF16)
 
         def attend(b, _):
-            ra = pl.ds(pl.multiple_of(b * 128, 128), 128)
+            ra = pl.ds(b * 128 if isinstance(b, int) else pl.multiple_of(b * 128, 128), 128)
             for pair in range(4):
                 cs = slice(pair * 128, pair * 128 + 128)
                 qs = stack(proj[ra, cs] * jnp.asarray(0.125, BF16))
                 kp = proj[ra, LD + pair * 128 : LD + pair * 128 + 128]
                 vp = proj[ra, 2 * LD + pair * 128 : 2 * LD + pair * 128 + 128]
-                s = jnp.where(allowed, mm_nt(qs, kp), masked_score)
-                e = jnp.exp(s - jnp.max(s, axis=-1, keepdims=True))
-                p = e * (1.0 / jnp.sum(e, axis=-1, keepdims=True))
+                s = jnp.where(causal, narrow(mm_nt(kp, qs)), masked_score)
+                e = jnp.exp(s - jnp.max(s, axis=0, keepdims=True))
+                p = e * (1.0 / jnp.sum(e, axis=0, keepdims=True))
                 probs[b * 4 + pair] = p
-                pl_ = p.astype(BF16)
-                wide = jnp.concatenate([pl_[:128], pl_[128:]], axis=1)
-                att[pl.ds(pl.multiple_of(t * tile + b * 128, 128), 128), cs] = mm(wide, stack(vp)).astype(BF16)
+                flipped = jnp.transpose(widen(p).astype(BF16))
+                wide = jnp.concatenate([flipped[:128], flipped[128:]], axis=1)
+                att_t[ra, cs] = mm(wide, stack(vp)).astype(BF16)
             return 0
 
-        lax.fori_loop(0, blocks, attend, 0)
-        attended = att[at, :]
+        def two(i, _):
+            attend(2 * i, 0)
+            return attend(2 * i + 1, 0)
+
+        lax.fori_loop(0, blocks // 2, two, 0)
+        attended = att_t[...]
+        att[at, :] = attended
         after = start + mm(attended, w_out[...])
         for c in range(4):
             cs = slice(c * 512, c * 512 + 512)
             a, s = gelu_pair(mm(hidden, w_up[:, cs]))
             a = a.astype(BF16)
             act[at, cs] = a
-            slope[:, cs] = s
+            slope[:, cs] = s.astype(BF16)
             after = after + mm(a, w_down[cs, :])
         scaled_f, factor_f = norm(after)
         final = (scaled_f * g_gain_final).astype(BF16)
         fin[at, :] = final
         logits = mm(final, w_head[...])
-        hot = jnp.where(own == vocab_ids, 1.0, 0.0)
+        hot = one_hot(own_ids[at, :])
         top = jnp.max(logits, axis=-1, keepdims=True)
         log_total = top + jnp.log(jnp.sum(jnp.exp(logits - top), axis=-1, keepdims=True))
         loss = loss + jnp.sum(
-            weighting * (log_total - jnp.sum(logits * hot, axis=-1, keepdims=True)), axis=0, keepdims=True
+            weighting[:, :1] * (log_total - jnp.sum(logits * hot, axis=-1, keepdims=True)), axis=0, keepdims=True
         )
-        lg = ((jnp.exp(logits - log_total) - hot) * weighting).astype(BF16)
+        lg = ((jnp.exp(logits - log_total) - hot) * jnp.concatenate([weighting, weighting], axis=1)).astype(BF16)
         lgrad[at, :] = lg
         fg = mm_nt(lg, w_head[...])
         gf = gf + jnp.sum(fg * scaled_f, axis=0, keepdims=True)
@@ -378,8 +469,7 @@
             hg = term if hg is None else hg + term
 
         def attend_back(b, _):
-            ra = pl.ds(pl.multiple_of(b * 128, 128), 128)
-            rg = pl.ds(pl.multiple_of(t * tile + b * 128, 128), 128)
+            ra = pl.ds(b * 128 if isinstance(b, int) else pl.multiple_of(b * 128, 128), 128)
             for pair in range(4):
                 cs = slice(pair * 128, pair * 128 + 128)
                 qs = stack(proj[ra, cs] * jnp.asarray(0.125, BF16))
@@ -387,28 +477,35 @@
                 vp = proj[ra, 2 * LD + pair * 128 : 2 * LD + pair * 128 + 128]
                 das = stack(attg[ra, cs])
                 p = probs[b * 4 + pair]
-                dp = mm_nt(das, vp)
-                ds = (p * (dp - jnp.sum(p * dp, axis=-1, keepdims=True))).astype(BF16)
-                wide = jnp.concatenate([ds[:128], ds[128:]], axis=1)
-                projg[rg, cs] = (mm(wide, stack(kp)) * 0.125).astype(BF16)
-                projg[rg, LD + pair * 128 : LD + pair * 128 + 128] = mm_tn(ds, qs).astype(BF16)
-                projg[rg, 2 * LD + pair * 128 : 2 * LD + pair * 128 + 128] = mm_tn(p.astype(BF16), das).astype(BF16)
+                dp = narrow(mm_nt(vp, das))
+                ds = widen(p * (dp - jnp.sum(p * dp, axis=0, keepdims=True)))
+                flipped = jnp.transpose(ds.astype(BF16))
+                wide = jnp.concatenate([flipped[:128], flipped[128:]], axis=1)
+                projg_t[ra, cs] = (mm(wide, stack(kp)) * 0.125).astype(BF16)
+                projg_t[ra, LD + pair * 128 : LD + pair * 128 + 128] = mm(ds.astype(BF16), qs).astype(BF16)
+                projg_t[ra, 2 * LD + pair * 128 : 2 * LD + pair * 128 + 128] = mm(widen(p).astype(BF16), das).astype(BF16)
             return 0
 
-        lax.fori_loop(0, blocks, attend_back, 0)
+        for b in range(blocks):
+            attend_back(b, 0)
         for c in range(3):
-            hg = hg + mm_nt(projg[at, c * LD : (c + 1) * LD], w_in[:, c * LD : (c + 1) * LD])
+            own = projg_t[:, c * LD : (c + 1) * LD]
+            projg[at, c * LD : (c + 1) * LD] = own
+            hg = hg + mm_nt(own, w_in[:, c * LD : (c + 1) * LD])
         start = startv[...]
         scaled, factor = norm(start)
         gl = gl + jnp.sum(hg * scaled, axis=0, keepdims=True)
         inner = hg * g_gain_local
         sg = (after_grad + factor * (inner - scaled * jnp.mean(inner * scaled, axis=-1, keepdims=True))).astype(BF16)
         sgrad[at, :] = sg
-        inputg_ref[at, :] = mm_nt(sg, w_bridge[...]).astype(BF16)
+        wide_rows[at, :] = mm_nt(sg, w_bridge[...])
         return loss, gl, gf
 
     init = (jnp.zeros((1, 1), F32), jnp.zeros((1, LD), F32), jnp.zeros((1, LD), F32))
     loss, gl, gf = lax.fori_loop(0, steps, step, init)
+
+    for j in range(SLOTS):
+        inputg_ref[:, j * GSLOT : (j + 1) * GSLOT] = wide_rows[pl.ds(j, patches, stride=SLOTS), :].astype(BF16)
 
     def put(ref, index, value, which):
         if base is not None:
@@ -435,33 +532,34 @@
         cs = slice(c * 512, c * 512 + 512)
         put(g_down, (cs, every), mm_tn(act[:, cs], bgrad[...]), 3)
     put(g_head, (every, every), mm_tn(fin[...], lgrad[...]), 4)
-    lookup_all = jnp.where(
-        ids_ref[:, 0:1] == lax.broadcasted_iota(jnp.int32, (rows, VOCAB), 1), 1.0, 0.0
-    ).astype(BF16)
+    lookup_all = one_hot(prev_ids[...]).astype(BF16)
     put(g_embed, (every, every), mm_tn(lookup_all, sgrad[...]), 5)
     put(g_bridge, (every, every), mm_tn(inputs_ref[...], sgrad[...]), 6)
 
 
-def byte_layer(inputs, ids, weighting, weights, gains, base=None, tile=256):
-    rows = inputs.shape[0]
+def byte_layer(start, own, pieces, ids, mask, count, weights, gains, base=None, tile=512):
+    rows = start.shape[0] * SLOTS
     shapes = [(LD, 3 * LD), (LD, LFF), (LD, LD), (LFF, LD), (LD, VOCAB), (VOCAB, LD), (GSLOT, LD)]
     out_shape = [jax.ShapeDtypeStruct(s, BF16) for s in shapes] + [
         jax.ShapeDtypeStruct((2, LD), F32), jax.ShapeDtypeStruct((1, 1), F32),
-        jax.ShapeDtypeStruct((rows, GSLOT), BF16)]
-    args = [inputs, ids, weighting, *weights, gains] + (list(base) if base is not None else [])
+        jax.ShapeDtypeStruct(start.shape, BF16)]
+    args = [start, own, *pieces, ids, mask, count, *weights, gains] + (list(base) if base is not None else [])
     vm = pl.BlockSpec(memory_space=pltpu.VMEM)
+    in_specs = [vm] * len(args)
+    in_specs[4 + len(pieces)] = pl.BlockSpec(memory_space=pltpu.SMEM)
     return pl.pallas_call(
-        functools.partial(byte_kernel, rows, tile, base is not None),
+        functools.partial(byte_kernel, rows, tile, base is not None, len(pieces)),
         out_shape=out_shape,
-        in_specs=[vm] * len(args),
+        in_specs=in_specs,
         out_specs=[vm] * len(out_shape),
+        cost_estimate=pl.CostEstimate(flops=43 * 10**9, bytes_accessed=150 * 10**6, transcendentals=10**6),
         scratch_shapes=[
             pltpu.VMEM((rows, LD), BF16),
             pltpu.VMEM((tile, 3 * LD), BF16),
-            pltpu.VMEM((tile // 128 * 4, 256, 128), F32),
+            pltpu.VMEM((tile // 128 * 4, SLOTS, 256), F32),
             pltpu.VMEM((rows, LD), BF16),
             pltpu.VMEM((rows, LFF), BF16),
-            pltpu.VMEM((tile, LFF), F32),
+            pltpu.VMEM((tile, LFF), BF16),
             pltpu.VMEM((rows, LD), BF16),
             pltpu.VMEM((rows, VOCAB), BF16),
             pltpu.VMEM((rows, LD), BF16),
@@ -470,8 +568,15 @@
             pltpu.VMEM((rows, 3 * LD), BF16),
             pltpu.VMEM((rows, LD), BF16),
             pltpu.VMEM((tile, LD), F32),
+            pltpu.VMEM((tile, LD), BF16),
+            pltpu.VMEM((tile, 3 * LD), BF16),
+            pltpu.VMEM((rows, GSLOT), F32),
+            pltpu.VMEM((rows, GSLOT), F32),
+            pltpu.VMEM((rows, GSLOT), F32),
+            pltpu.VMEM((rows, GSLOT), F32),
+            pltpu.VMEM((rows, GSLOT), BF16),
         ],
-        compiler_params=pltpu.CompilerParams(vmem_limit_bytes=60 * 2**20),
+        compiler_params=pltpu.CompilerParams(vmem_limit_bytes=61 * 2**20),
         name="byte_layer",
     )(*args)
 
@@ -514,132 +619,166 @@
     return [(s, other(m, j, stacks), d) for j in range(1, stacks)]
 
 
-def gather_kernel(sizes, columns, *refs):
+def gather_kernel(sizes, columns, forwarded, *refs):
     slots, stacks, groups = sizes
     count = len(columns)
-    shards, tail = refs[:count], refs[count]
-    outs, gain_out = refs[count + 1 : 2 * count + 1], refs[2 * count + 1]
-    (tail_z, tail_s, tail_d, own_sem, xs, xr, cs, cr, zs, zr, ts, tr, ds, dr, gs) = refs[2 * count + 2 :]
-    s, d = lax.axis_index("slot"), lax.axis_index("dp")
+    wide, tail, counted = refs[:count], refs[count], refs[count + 1]
+    outs, gain_out, count_out = refs[count + 2 : 2 * count + 2], refs[2 * count + 2], refs[2 * count + 3]
+    shards, rest = refs[2 * count + 4 : 3 * count + 4], refs[3 * count + 4 :]
+    (tail_z, tail_s, tail_d, held_count, own_sem, xs, xr, cs, cr, zs, zr, ts, tr, ds, dr, ns, nr) = rest
+    s, m, d = lax.axis_index("slot"), lax.axis_index("mp"), lax.axis_index("dp")
     across, beside = group_peers(slots, groups)
     above = stack_peers(stacks)
+    for w in range(count):
+        if len(wide[w].shape) == 3:
+            breadth = wide[w].shape[2]
+            for i in range(wide[w].shape[0]):
+                shards[w][:, i * breadth : (i + 1) * breadth] = wide[w][i].astype(BF16)
+        else:
+            shards[w][...] = wide[w][...].astype(BF16)
+    tail_z[m] = tail[...].astype(BF16)
+    held_count[d] = counted[...]
     greet(across + beside + above)
 
-    def place(w, slot, group):
-        extent = shards[w].shape[1 if columns[w] else 0]
-        return place_of(outs[w], columns[w], extent, slot * groups + group)
-
-    pending = []
-    tail_copies = [
-        remote(tail, tail_z.at[j], zs.at[j], zr.at[j], above[j - 1]) for j in range(1, stacks)
+    def place(w, slot, group, half=None):
+        rows, breadth = shards[w].shape
+        index = slot * groups + group
+        if half is None:
+            return place_of(outs[w], columns[w], breadth if columns[w] else rows, index)
+        size = rows // 2
+        if columns[w]:
+            return outs[w].at[pl.ds(half * size, size), pl.ds(pl.multiple_of(index * breadth, breadth), breadth)]
+        return outs[w].at[pl.ds(pl.multiple_of(index * rows + half * size, size), size), :]
+
+    tail_copies = [remote(tail_z.at[m], tail_z.at[m], zs.at[j], zr.at[j], above[j - 1]) for j in range(1, stacks)]
+    tail_copies += [
+        remote(held_count.at[d], held_count.at[d], ns.at[k], nr.at[k], beside[k - 1]) for k in range(1, groups)
     ]
-    own_tail = pltpu.make_async_copy(tail, tail_z.at[0], gs.at[0])
-    own_tail.start()
     for copy in tail_copies:
         copy.start()
-    sends = {}
+    sends, pending = [], []
+    direct = (1, 2) if forwarded else tuple(range(1, slots))
     for w in range(count):
-        for j in range(1, slots):
+        for j in direct:
             copy = remote(shards[w], place(w, s, d), xs.at[w, j], xr.at[w, j], across[j - 1])
             copy.start()
-            sends[w, j] = copy
+            sends.append(copy)
+    for w in range(count):
         for k in range(1, groups):
             copy = remote(shards[w], place(w, s, d), cs.at[w, 0, k], cr.at[w, 0, k], beside[k - 1])
             copy.start()
             pending.append(copy)
         copy = pltpu.make_async_copy(shards[w], place(w, s, d), own_sem.at[w])
         copy.start()
-        sends[w, 0] = copy
-
-    m = lax.axis_index("mp")
-    own_tail.wait()
+        pending.append(copy)
+
     for copy in tail_copies:
         copy.wait()
-    chosen = tail_z[0]
-    for j in range(1, stacks):
-        chosen = jnp.where(origin(m, j, stacks) == stacks - 1, tail_z[j], chosen)
-    tail_s[0] = chosen
-    step = [remote(tail_s.at[0], tail_s.at[j], ts.at[j], tr.at[j], across[j - 1]) for j in range(1, slots)]
+    total = held_count[0]
+    for k in range(1, groups):
+        total = total + held_count[k]
+    count_out[...] = total
+    tail_s[s] = tail_z[stacks - 1]
+    step = [remote(tail_s.at[s], tail_s.at[s], ts.at[j], tr.at[j], across[j - 1]) for j in range(1, slots)]
     for copy in step:
         copy.start()
     for copy in step:
         copy.wait()
-    chosen = tail_s[0]
-    for j in range(1, slots):
-        chosen = jnp.where(origin(s, j, slots) == slots - 1, tail_s[j], chosen)
-    tail_d[0] = chosen
-    step = [remote(tail_d.at[0], tail_d.at[k], ds.at[k], dr.at[k], beside[k - 1]) for k in range(1, groups)]
+    tail_d[d] = tail_s[slots - 1]
+    step = [remote(tail_d.at[d], tail_d.at[d], ds.at[k], dr.at[k], beside[k - 1]) for k in range(1, groups)]
     for copy in step:
         copy.start()
     for copy in step:
         copy.wait()
-    chosen = tail_d[0]
-    for k in range(1, groups):
-        chosen = jnp.where(origin(d, k, groups) == groups - 1, tail_d[k], chosen)
-    gain_out[...] = chosen.astype(F32)
+    gain_out[...] = tail_d[groups - 1].astype(F32)
+
+    def spread(w, j, slot):
+        here = place(w, slot, d)
+        for k in range(1, groups):
+            copy = remote(here, here, cs.at[w, j, k], cr.at[w, j, k], beside[k - 1])
+            copy.start()
+            pending.append(copy)
 
     for w in range(count):
-        for j in range(1, slots):
-            here = place(w, origin(s, j, slots), d)
+        for j in direct:
+            slot = origin(s, j, slots)
+            here = place(w, slot, d)
             remote(here, here, xs.at[w, j], xr.at[w, j], across[j - 1]).wait_recv()
-            for k in range(1, groups):
-                copy = remote(here, here, cs.at[w, j, k], cr.at[w, j, k], beside[k - 1])
+            if forwarded:
+                half = 0 if j == 1 else 1
+                part, index = place(w, slot, d, half), 3 if j == 1 else 0
+                copy = remote(part, part, xs.at[w, index], xr.at[w, index], across[2 - j])
                 copy.start()
-                pending.append(copy)
-    for w in range(count):
-        sends[w, 0].wait()
-        for j in range(1, slots):
-            sends[w, j].wait_send()
+                sends.append(copy)
+            spread(w, j, slot)
+    if forwarded:
+        for w in range(count):
+            slot = s ^ 3
+            for half, index in ((0, 3), (1, 0)):
+                part = place(w, slot, d, half)
+                remote(part, part, xs.at[w, index], xr.at[w, index], across[1 - half]).wait_recv()
+            spread(w, 3, slot)
+    for copy in sends:
+        copy.wait_send()
     for copy in pending:
         copy.wait()
 
 
-def gather_weights(shards, columns, tail):
+def gather_weights(shards, columns, tail, counted):
     sizes = tuple(lax.axis_size(axis) for axis in ("slot", "mp", "dp"))
     slots, stacks, groups = sizes
     count = len(shards)
     parts = slots * groups
+    flats = [(v.shape[1], v.shape[0] * v.shape[2]) if v.ndim == 3 else v.shape for v in shards]
     shapes = [
-        (v.shape[0], v.shape[1] * parts) if c else (v.shape[0] * parts, v.shape[1])
-        for v, c in zip(shards, columns)
+        (v[0], v[1] * parts) if c else (v[0] * parts, v[1]) for v, c in zip(flats, columns)
     ]
+    forwarded = slots == 4 and all(v[0] % 32 == 0 for v in flats)
     anywhere = pl.BlockSpec(memory_space=pl.ANY)
+    vm = pl.BlockSpec(memory_space=pltpu.VMEM)
     dma = pltpu.SemaphoreType.DMA
     return pl.pallas_call(
-        functools.partial(gather_kernel, sizes, columns),
+        functools.partial(gather_kernel, sizes, columns, forwarded),
         out_shape=[jax.ShapeDtypeStruct(shape, BF16) for shape in shapes]
-        + [jax.ShapeDtypeStruct(tail.shape, F32)],
-        in_specs=[anywhere] * (count + 1),
-        out_specs=[anywhere] * count + [pl.BlockSpec(memory_space=pltpu.VMEM)],
-        scratch_shapes=[
+        + [jax.ShapeDtypeStruct(tail.shape, F32), jax.ShapeDtypeStruct(counted.shape, F32)],
+        in_specs=[vm] * (count + 2),
+        out_specs=[anywhere] * count + [vm] * 2,
+        scratch_shapes=[pltpu.VMEM(v, BF16) for v in flats]
+        + [
             pltpu.VMEM((stacks,) + tail.shape, BF16),
             pltpu.VMEM((slots,) + tail.shape, BF16),
             pltpu.VMEM((groups,) + tail.shape, BF16),
+            pltpu.VMEM((groups,) + counted.shape, F32),
             dma((count,)),
             dma((count, slots)), dma((count, slots)),
             dma((count, slots, groups)), dma((count, slots, groups)),
             dma((stacks,)), dma((stacks,)),
             dma((slots,)), dma((slots,)),
             dma((groups,)), dma((groups,)),
-            dma((1,)),
+            dma((groups,)), dma((groups,)),
         ],
-        compiler_params=pltpu.CompilerParams(collective_id=1, has_side_effects=True),
+        compiler_params=pltpu.CompilerParams(
+            collective_id=1, has_side_effects=True, vmem_limit_bytes=24 * 2**20
+        ),
+        cost_estimate=pl.CostEstimate(flops=10**6, bytes_accessed=120 * 10**6, transcendentals=0),
         name="gather_weights",
-    )(*shards, tail)
-
-
-def scatter_kernel(sizes, columns, extents, *refs):
+    )(*shards, tail, counted)
+
+
+def scatter_kernel(sizes, columns, extents, shared, *refs):
     slots, stacks, groups = sizes
     count = len(columns)
     partials, outs = refs[:count], refs[count : 2 * count]
     rest = refs[2 * count :]
     from_core, stage, from_slot = rest[:count], rest[count : 2 * count], rest[2 * count : 3 * count]
-    from_z, own_c, from_c, cs, cr, xs, xr, zs, zr, ts, tr = rest[3 * count :]
+    cs, cr, xs, xr = rest[3 * count : 3 * count + 4]
+    if shared:
+        from_z, own_c, from_c, zs, zr, ts, tr = rest[3 * count + 4 :]
     s, m, d = lax.axis_index("slot"), lax.axis_index("mp"), lax.axis_index("dp")
     across, beside = group_peers(slots, groups)
     above = stack_peers(stacks)
-    greet(across + beside + above)
-    order = (count - 1,) + tuple(range(count - 1))
+    greet(across + beside + above if shared else across + beside)
+    order = tuple(range(count))
 
     def part(w, slot, group):
         return place_of(partials[w], columns[w], extents[w], slot * groups + group)
@@ -678,7 +817,7 @@
         for j in range(1, slots):
             total = total + from_slot[w][j].astype(F32)
         outs[w][: total.shape[0]] = total
-        if w == order[0]:
+        if shared:
             from_z[m] = total.astype(BF16)
             third = [
                 remote(from_z.at[m], from_z.at[m], zs.at[j], zr.at[j], above[j - 1])
@@ -686,28 +825,29 @@
             ]
             for copy in third:
                 copy.start()
-    w = order[0]
-    size = from_slot[w].shape[1]
-    for copy in third:
-        copy.wait()
-    total = from_z[0].astype(F32)
-    for j in range(1, stacks):
-        total = total + from_z[j].astype(F32)
-    own_c[...] = total.astype(BF16)
-    fourth = [remote(own_c, from_c.at[k], ts.at[k], tr.at[k], beside[k - 1]) for k in range(1, groups)]
-    for copy in fourth:
-        copy.start()
-    outs[w][pl.ds(pl.multiple_of(d * size, size), size), :] = own_c[...].astype(F32)
-    for k in range(1, groups):
-        fourth[k - 1].wait()
-        outs[w][pl.ds(pl.multiple_of(origin(d, k, groups) * size, size), size), :] = from_c[k].astype(F32)
+    if shared:
+        w = 0
+        size = from_slot[w].shape[1]
+        for copy in third:
+            copy.wait()
+        total = from_z[0].astype(F32)
+        for j in range(1, stacks):
+            total = total + from_z[j].astype(F32)
+        own_c[...] = total.astype(BF16)
+        fourth = [remote(own_c, from_c.at[k], ts.at[k], tr.at[k], beside[k - 1]) for k in range(1, groups)]
+        for copy in fourth:
+            copy.start()
+        outs[w][pl.ds(pl.multiple_of(d * size, size), size), :] = own_c[...].astype(F32)
+        for k in range(1, groups):
+            fourth[k - 1].wait()
+            outs[w][pl.ds(pl.multiple_of(origin(d, k, groups) * size, size), size), :] = from_c[k].astype(F32)
     for copy in first.values():
         copy.wait_send()
     for copy in second.values():
         copy.wait_send()
 
 
-def scatter_grads(partials, columns):
+def scatter_grads(partials, columns, shared=False):
     sizes = tuple(lax.axis_size(axis) for axis in ("slot", "mp", "dp"))
     slots, stacks, groups = sizes
     count = len(partials)
@@ -717,30 +857,36 @@
         for v, c in zip(partials, columns)
     ]
     extents = tuple(b[1] if c else b[0] for b, c in zip(blocks, columns))
-    shapes = blocks[:-1] + [(blocks[-1][0] * groups, blocks[-1][1])]
+    shapes = [(b[0] * groups, b[1]) for b in blocks] if shared else blocks
     vm = pl.BlockSpec(memory_space=pltpu.VMEM)
     dma = pltpu.SemaphoreType.DMA
     last = blocks[-1]
     return pl.pallas_call(
-        functools.partial(scatter_kernel, sizes, columns, extents),
+        functools.partial(scatter_kernel, sizes, columns, extents, shared),
         out_shape=[jax.ShapeDtypeStruct(shape, F32) for shape in shapes],
         in_specs=[vm] * count,
         out_specs=[vm] * count,
         scratch_shapes=[pltpu.VMEM((slots, groups - 1) + b, BF16) for b in blocks]
         + [pltpu.VMEM((slots,) + b, BF16) for b in blocks]
         + [pltpu.VMEM((slots,) + b, BF16) for b in blocks]
-        + [
-            pltpu.VMEM((stacks,) + last, BF16),
-            pltpu.VMEM(last, BF16), pltpu.VMEM((groups,) + last, BF16),
-            dma((count, slots, groups)), dma((count, slots, groups)),
-            dma((count, slots)), dma((count, slots)),
-            dma((stacks,)), dma((stacks,)),
-            dma((groups,)), dma((groups,)),
-        ],
+        + [dma((count, slots, groups))] * 2
+        + [dma((count, slots))] * 2
+        + (
+            [
+                pltpu.VMEM((stacks,) + last, BF16),
+                pltpu.VMEM(last, BF16), pltpu.VMEM((groups,) + last, BF16),
+                dma((stacks,)), dma((stacks,)), dma((groups,)), dma((groups,)),
+            ]
+            if shared
+            else []
+        ),
         compiler_params=pltpu.CompilerParams(
-            collective_id=2, has_side_effects=True, vmem_limit_bytes=48 * 2**20
+            collective_id=4 if shared else 2, has_side_effects=True, vmem_limit_bytes=48 * 2**20
         ),
-        name="scatter_grads",
+        cost_estimate=pl.CostEstimate(
+            flops=10**6, bytes_accessed=(10 if shared else 120) * 10**6, transcendentals=0
+        ),
+        name="scatter_small" if shared else "scatter_grads",
     )(*partials)
 
 
@@ -900,7 +1046,7 @@
     return index ^ offset if size & (size - 1) == 0 else (index + size - offset) % size
 
 
-def scatter_rows(partial, axis):
+def trade_rows(partial, axis):
     size = lax.axis_size(axis)
     index = lax.axis_index(axis)
     share = partial.shape[0] // size
@@ -908,23 +1054,11 @@
     for offset in range(1, size):
         block = lax.dynamic_slice_in_dim(partial, partner(index, offset, size) * share, share, 0)
         pieces.append(swap(block.astype(BF16), axis, offset))
-    total = lax.dynamic_slice_in_dim(partial, index * share, share, 0).astype(F32)
-    for piece in pieces:
-        total = total + piece.astype(F32)
-    return total
-
-
-def gather_rows(block, axis):
-    size = lax.axis_size(axis)
-    index = lax.axis_index(axis)
-    share = block.shape[0]
-    whole = jnp.zeros((size * share,) + block.shape[1:], block.dtype)
-    whole = lax.dynamic_update_slice_in_dim(whole, block, index * share, 0)
-    for offset in range(1, size):
-        whole = lax.dynamic_update_slice_in_dim(
-            whole, swap(block, axis, offset), source(index, offset, size) * share, 0
-        )
-    return whole
+    return lax.dynamic_slice_in_dim(partial, index * share, share, 0), pieces
+
+
+def share_rows(block, axis):
+    return [block] + [swap(block, axis, offset) for offset in range(1, lax.axis_size(axis))]
 
 
 def shift_chunks(value, distance, forward):
@@ -978,29 +1112,31 @@
     slot_index, mp_index, dp_index = (
         lax.axis_index("slot"), lax.axis_index("mp"), lax.axis_index("dp"),
     )
-    mask_count = lax.psum(jnp.sum(loss_mask.astype(F32)), "dp")
-    part = attend_in.shape[0]
+    counted = jnp.full((8, 128), jnp.sum(loss_mask.astype(F32)))
     width = attend_in.shape[2]
     piece = slot_table.shape[0] * VOCAB // lax.axis_size("dp")
     table_shard = lax.dynamic_slice_in_dim(
         slot_table.reshape(-1, GSLOT), dp_index * piece, piece, 0
-    ).astype(BF16)
-    tail = local_pack[-(D + 2 * LD) :].astype(BF16).reshape(-1, 128)
-    pack_whole = gather_pack(local_pack)
-    shards = [table_shard, attend_in.astype(BF16).reshape(part, 3 * width), expand_in.astype(BF16)]
-    late = [attend_out.astype(BF16), expand_out.astype(BF16)]
+    )
+    tail = local_pack[-(D + 2 * LD) :].reshape(-1, 128)
+    shards = [table_shard, jnp.transpose(attend_in, (1, 0, 2)), expand_in]
+    late = [attend_out, expand_out]
     wide = attend_out.shape[1] % 128 == 0
     if wide:
-        table, full_in_flat, full_expand, full_out, full_shrink, gains = gather_weights(
-            shards + late, (False, False, False, True, True), tail
+        table, full_in_flat, full_expand, full_out, full_shrink, gains, counted = gather_weights(
+            shards + late, (False, False, False, True, True), tail, counted
         )
     else:
-        table, full_in_flat, full_expand, gains = gather_weights(shards, (False, False, False), tail)
+        table, full_in_flat, full_expand, gains, counted = gather_weights(
+            shards, (False, False, False), tail, counted
+        )
         full_out, full_shrink = (
-            lax.all_gather(v, ("slot", "dp"), axis=1, tiled=True) for v in late
+            lax.all_gather(v.astype(BF16), ("slot", "dp"), axis=1, tiled=True) for v in late
         )
-    table = table.reshape(SLOTS, VOCAB, GSLOT)
+    local_pack_later, gains = lax.optimization_barrier((local_pack, gains))
+    pack_whole = gather_pack(local_pack_later)
     gains = gains.reshape(-1)
+    mask_count = counted[0, 0]
     gain_global = gains[:D]
     local_gains = gains[D:].reshape(2, LD)
     unpacked = unpack(pack_whole, local_pack.shape[0])
@@ -1023,15 +1159,9 @@
         own_items = lax.dynamic_slice_in_dim(items, begin, rows, 0)
         first = jnp.sum((items[None, :] < own_items[:, None]).astype(jnp.int32), axis=1)
         first = jnp.maximum(first - (chunk - reach) * rows, 0)
-        lookup = (own_previous[:, :, None] == vocab_ids).astype(BF16)
-        start_rows = (
-            jnp.einsum("pjv,jvg->pjg", lookup, table, preferred_element_type=F32)
-            .astype(BF16).reshape(rows, D).astype(F32)
+        start_rows, hidden, projected, own_kv = embed_rows(
+            own_previous, table, full_in_flat, gain_global[None]
         )
-        normed, scaled, factor = norm_forward(start_rows, gain_global)
-        hidden = normed.astype(BF16)
-        projected = product(hidden, full_in_flat).astype(BF16)
-        own_kv = projected[:, width:]
         earlier = [shift_chunks(own_kv, d, forward) for d in range(1, reach + 1)]
         expanded = product(hidden, full_expand)
         active = gelu_tanh(expanded).astype(BF16)
@@ -1044,50 +1174,73 @@
         ))
     for m in micros:
         m["attended"], m["lse"] = attention_fwd(m["low"], m["first"], m["projected"], m["earlier"])
-        branch = scatter_rows(
+        m["own"], m["pieces"] = trade_rows(
             product(m["attended"], full_out) + product(m["active"], full_shrink), "mp"
         )
         m["own_start"] = lax.dynamic_slice_in_dim(
             m["start_rows"], mp_index * local_rows, local_rows, 0
         )
-        m["middle"] = m["own_start"] + branch
     base = None
     for m in micros:
         ids = lax.dynamic_slice_in_dim(m["group_ids"], m["begin_local"], local_rows, 0)
         mask = lax.dynamic_slice_in_dim(m["mask"], m["begin_local"], local_rows, 0)
-        before = jnp.concatenate([jnp.full((local_rows, 1), -1, jnp.int32), ids[:, :-1]], axis=1)
-        weighting = mask.reshape(-1, 1).astype(F32) / mask_count
         out = byte_layer(
-            m["middle"].astype(BF16).reshape(-1, GSLOT),
-            jnp.stack([before.reshape(-1), ids.reshape(-1)], axis=1),
-            weighting, unpacked[:7], local_gains, base,
+            m["own_start"], m["own"], m["pieces"], ids, mask, mask_count.reshape(1, 1),
+            unpacked[:7], local_gains, base,
         )
         base = out[:9]
-        m["own_back"] = out[9].reshape(local_rows, D)
-        m["branch_grad"] = gather_rows(m["own_back"], "mp")
+        m["own_back"] = out[9]
+        m["branch_pieces"] = share_rows(out[9], "mp")
     matrices, local_gain_grads, loss_sum = base[:7], base[7], base[8][0, 0]
     sums = None
     table_grad = None
     gain_global_grad = None
     for m in micros:
-        branch_grad = m["branch_grad"]
-        grad_out = gram_product(m["attended"], branch_grad)
-        grad_shrink = gram_product(m["active"], branch_grad)
-        attended_grad = back_product(branch_grad, full_out).astype(BF16)
-        expanded_grad = gelu_back(m["expanded"], back_product(branch_grad, full_shrink)).astype(BF16)
-        grad_expand = gram_product(m["hidden"], expanded_grad)
-        query_grad, kv_grads = attention_bwd(
-            m["low"], m["first"], m["projected"], m["earlier"], m["attended"], attended_grad, m["lse"]
+        branch_grad, m["query_grad"], m["kv_grads"] = attention_bwd(
+            m["low"], m["first"], m["projected"], m["earlier"], m["attended"], m["lse"],
+            full_out, m["branch_pieces"],
         )
-        kv_total = kv_grads[0].astype(F32)
-        for d in range(1, reach + 1):
-            kv_total = kv_total + shift_chunks(kv_grads[d], d, not m["forward"]).astype(F32)
-        projected_grad = jnp.concatenate([query_grad, kv_total.astype(BF16)], axis=1)
-        grad_in = gram_product(m["hidden"], projected_grad)
-        hidden_grad = scatter_rows(
-            back_product(projected_grad, full_in_flat) + back_product(expanded_grad, full_expand), "mp"
+        m["branch_grad"] = branch_grad
+        m["returned"] = [
+            shift_chunks(m["kv_grads"][d], d, not m["forward"]) for d in range(1, reach + 1)
+        ]
+        m["expanded_grad"] = gelu_back(
+            m["expanded"], back_product(branch_grad, full_shrink)
+        ).astype(BF16)
+    for m in micros:
+        kv_total = m["kv_grads"][0].astype(F32)
+        for value in m["returned"]:
+            kv_total = kv_total + value.astype(F32)
+        m["projected_grad"] = jnp.concatenate([m["query_grad"], kv_total.astype(BF16)], axis=1)
+        m["partial"] = back_product(m["projected_grad"], full_in_flat) + back_product(
+            m["expanded_grad"], full_expand
         )
-        _, scaled, factor = norm_forward(m["own_start"], gain_global)
+        m["back"] = trade_rows(m["partial"], "mp")
+    sums = None
+    for m in micros:
+        terms = (
+            gram_product(m["hidden"], m["projected_grad"]),
+            gram_product(m["hidden"], m["expanded_grad"]),
+            gram_product(m["attended"], m["branch_grad"]),
+            gram_product(m["active"], m["branch_grad"]),
+        )
+        sums = terms if sums is None else tuple(a + b for a, b in zip(sums, terms))
+    sums = tuple(s.astype(BF16) for s in sums)
+    if wide:
+        sums, _ = lax.optimization_barrier((sums, [m["back"][0] for m in micros]))
+        own_in, own_expand, own_out, own_shrink = scatter_grads(sums, (False, False, True, True))
+    else:
+        own_in, own_expand = scatter_grads(sums[:2], (False, False))
+        own_out, own_shrink = (
+            lax.psum_scatter(v, ("slot", "dp"), scatter_dimension=1, tiled=True).astype(F32)
+            for v in sums[2:]
+        )
+    backs, own_in = lax.optimization_barrier(([m["back"] for m in micros], own_in))
+    table_grad = None
+    for m, (hidden_grad, pieces) in zip(micros, backs):
+        for value in pieces:
+            hidden_grad = hidden_grad + value.astype(F32)
+        _, scaled, factor = norm_forward(m["own_start"].astype(F32), gain_global)
         gain_term = jnp.sum(hidden_grad * scaled, axis=0)
         start_grad = (
             m["own_back"].astype(F32) + norm_backward(scaled, factor, gain_global, hidden_grad)
@@ -1098,14 +1251,11 @@
             "pjv,pjg->jvg", own_lookup, start_grad.reshape(local_rows, SLOTS, GSLOT),
             preferred_element_type=F32,
         )
-        terms = (grad_in, grad_expand, grad_out, grad_shrink)
-        if sums is None:
-            sums, table_grad, gain_global_grad = terms, table_term, gain_term
+        if table_grad is None:
+            table_grad, gain_global_grad = table_term, gain_term
         else:
-            sums = tuple(a + b for a, b in zip(sums, terms))
             table_grad = table_grad + table_term
             gain_global_grad = gain_global_grad + gain_term
-    sums = tuple(s.astype(BF16) for s in sums)
     gain_grads = jnp.concatenate([gain_global_grad, local_gain_grads.reshape(-1)])
     parts = slot_size * lax.axis_size("dp")
     small = jnp.concatenate(
@@ -1115,16 +1265,7 @@
         ],
         axis=1,
     ).reshape(-1, GSLOT)
-    if wide:
-        own_in, own_expand, own_out, own_shrink, own_small = scatter_grads(
-            [*sums, small], (False, False, True, True, False)
-        )
-    else:
-        own_in, own_expand, own_small = scatter_grads([*sums[:2], small], (False, False, False))
-        own_out, own_shrink = (
-            lax.psum_scatter(v, ("slot", "dp"), scatter_dimension=1, tiled=True).astype(F32)
-            for v in sums[2:]
-        )
+    own_small = scatter_grads([small], (False,), True)[0]
     own_in = own_in.reshape(attend_in.shape)
     own_small = own_small.reshape(lax.axis_size("dp"), piece + 16, GSLOT)
     own_table = own_small[:, :piece].reshape(slot_table.shape)

time: 596 us -> 501 us (0.84)
  waiting for transfers between devices: 55.7 us -> 19.9 us
  Pallas kernels: 292 us -> 258 us
  matrix products: 55 us -> 32.6 us
  starting transfers between devices: 46.6 us -> 57.6 us
  local copies, waits for them, and re-layouts: 78.7 us -> 70.8 us
    ppermute x18, waiting for transfers between devices: 55.6 us -> 19.8 us  [swap(): return lax.ppermute(value, axis, pairs)]
    unnamed x170 -> x184, local copies, waits for them, and re-layouts: 25.9 us -> 49.7 us
    pallas_call x2, Pallas kernels: 114 us -> 91.2 us  [byte_layer(): pl.pallas_call(functools.partial(byte_kernel, rows, tile, base is not Non...]
    ppermute x8, starting transfers between devices: 16.3 us -> 30.8 us  [shift_chunks(): return lax.ppermute(value, 'slot', pairs)]
    dynamic_update_slice x8 -> x0, local copies, waits for them, and re-layouts: 11.5 us -> none  [the longest x6 9.13 us: gather_rows(): lax.dynamic_update_slice_in_dim(whole, swap(block, axis, offset), source(...]
    convert_element_type x8 -> x4, local copies, waits for them, and re-layouts: 9.16 us -> 0.49 us  [trade_rows(): pieces.append(swap(block.astype(BF16), axis, offset))]
    dot_general x2 -> x0, matrix products: 7.66 us -> none  [local(): jnp.einsum('pjv,jvg->pjg', lookup, table, preferred_element_type=F32)]
    div x4 -> x0, local copies, waits for them, and re-layouts: 6.47 us -> none  [local(): weighting = mask.reshape(-1, 1).astype(F32) / mask_count]
  transfers between devices with their start and end apart: 28 -> 28, of which waited for: 5 -> 3; matrix products, arithmetic and copies ran while one was open for 21% -> 14% of each run, Pallas kernels for 26% -> 42%
where the time goes in v2:
time: 501 us; the launch traced here: 492 us
  Pallas kernels  258 us (51%)
  local copies, waits for them, and re-layouts  70.8 us (14%)
  starting transfers between devices  57.6 us (11%)
  matrix products  32.6 us (7%)
  other arithmetic  29.7 us (6%)
  between operations  23.6 us (5%)
  waiting for transfers between devices  19.9 us (4%)
    pallas_call x2, Pallas kernels, byte_layer(): pl.pallas_call(functools.partial(byte_kernel, rows, tile, base is not Non...  91.2 us
    pallas_call x2, Pallas kernels, scatter_grads(): pl.pallas_call(functools.partial(scatter_kernel, sizes, columns, extents,...  60 us
    unnamed x184, local copies, waits for them, and re-layouts  49.7 us
    pallas_call x1, Pallas kernels, gather_weights(): pl.pallas_call(functools.partial(gather_kernel, sizes, columns, forwarded...  40.7 us
    ppermute x8, starting transfers between devices, shift_chunks(): return lax.ppermute(value, 'slot', pairs)  30.8 us
    ppermute x18, starting transfers between devices, swap(): return lax.ppermute(value, axis, pairs)  26.7 us
    ppermute x18, waiting for transfers between devices, swap(): return lax.ppermute(value, axis, pairs)  19.8 us
    pallas_call x2, Pallas kernels, attention_bwd(): pl.pallas_call(functools.partial(bwd_kernel, rows, width, count, len(piec...  17.9 us
  transfers between devices with their start and end apart: 28, of which 3 were waited for; matrix products, arithmetic and copies ran while one was open for 14% of the time, Pallas kernels for 42%

profile of v2, /device:TPU:0, one launch (start us, length us, event | category | flops | bytes accessed | tf_op | source)
XLA Modules:
  0.0 492.4 jit_solution(6893968568009775278)
XLA Ops:
  15.2 40.7 %gather_weights.1 = (bf16[2048,128]{1,0:T(8,128)(2,1)S(1)}, bf16[1024,768]{1,0:T(8,128)(2,1)S(1)}, bf16[1024,1024]{1,0:T(8,128)(2,1)S(1)}, bf16[256,1024]{1,0:T(...) custom-call(f32[256,128]{1,0:T(8,128)S(1)} %constant_dynamic-slice_fusion.15.refs_0_, ...), custom_call_target="tpu_custom_call" | custom-call | flops 1000000 | bytes 120000000 | tf_op jit(solution)/shard_map/gather_weights/pallas_call | solution.py:740
  68.5 3.3 embed_rows.3
  73.8 4.2 collective-permute-start.6
  78.0 3.3 collective-permute-start.5
  85.9 3.3 embed_rows.2
  112.3 3.0 fusion.62
  115.3 2.6 fusion.61
  117.9 2.8 fusion.53
  123.3 3.1 fusion.52
  126.5 5.3 %patch_attention.3 = (bf16[512,256]{1,0:T(8,128)(2,1)S(1)}, f32[4,1,512]{2,1,0:T(1,128)S(1)}) custom-call(s32[2]{0:T(128)S(1)} %and_select_fusion.low_ref, s32[2,1,256]{2,1,0:T(1,128)S(1)} %bitcast.90, bf16[512,768]{1,0:T(8,128)(2,1)S(1)} %copy-done.47, bf16[512,512]{1,0:T(8,128)(2,1)} %collective-permute-done.5.rest_0_, ...), custom_call_target="tpu_custom_call" | custom-call | flops 6000000000 | bytes 20000000 | tf_op jit(solution)/shard_map/patch_attention/pallas_call | solution.py:242
  134.5 2.4 collective-permute-start.7
  136.9 9.3 %patch_attention.2 = (bf16[512,256]{1,0:T(8,128)(2,1)S(1)}, f32[4,1,512]{2,1,0:T(1,128)S(1)}) custom-call(s32[2]{0:T(128)S(1)} %and_select_fusion.1.low_ref, s32[2,1,256]{2,1,0:T(1,128)S(1)} %bitcast.88, bf16[512,768]{1,0:T(8,128)(2,1)S(1)} %copy-done.50, bf16[512,512]{1,0:T(8,128)(2,1)} %collective-permute-done.rest_0_, ...), custom_call_target="tpu_custom_call" | custom-call | flops 6000000000 | bytes 20000000 | tf_op jit(solution)/shard_map/patch_attention/pallas_call | solution.py:242
  150.5 7.9 %unpack.1 = (bf16[512,1536]{1,0:T(8,128)(2,1)S(1)}, bf16[512,2048]{1,0:T(8,128)(2,1)S(1)}, bf16[512,512]{1,0:T(8,128)(2,1)S(1)}, bf16[2048,512]{1,0:T(8,128)(2,1...) custom-call(bf16[27648,128]{1,0:T(8,128)(2,1)} %all-gather.2.cloned.1.call-done.blocks_ref), custom_call_target="tpu_custom_call" | custom-call | tf_op jit(solution)/shard_map/unpack/pallas_call | solution.py:980
  163.9 2.4 collective-permute-start.2
  166.3 3.7 collective-permute-done.8.rest_1_
  170.0 44.2 %byte_layer.2 = (bf16[512,1536]{1,0:T(8,128)(2,1)}, bf16[512,2048]{1,0:T(8,128)(2,1)}, bf16[512,512]{1,0:T(8,128)(2,1)}, bf16[2048,512]{1,0:T(8,128)(2,1)}, bf16...) custom-call(bf16[128,1024]{1,0:T(8,128)(2,1)} %get-tuple-element.239, ...), custom_call_target="tpu_custom_call" | custom-call | flops 43000000512 | bytes 150000000 | tf_op jit(solution)/shard_map/byte_layer/pallas_call | solution.py:550
  216.2 2.4 collective-permute-start.10
  219.3 46.9 %byte_layer.3 = (bf16[512,1536]{1,0:T(8,128)(2,1)}, bf16[512,2048]{1,0:T(8,128)(2,1)}, bf16[512,512]{1,0:T(8,128)(2,1)}, bf16[2048,512]{1,0:T(8,128)(2,1)}, bf16...) custom-call(bf16[128,1024]{1,0:T(8,128)(2,1)} %get-tuple-element.241, ...), custom_call_target="tpu_custom_call" | custom-call | flops 43000000512 | bytes 150000000 | tf_op jit(solution)/shard_map/byte_layer/pallas_call | solution.py:550
  275.8 8.4 %pack.1 = bf16[27648,128]{1,0:T(8,128)(2,1)} custom-call(bf16[512,1536]{1,0:T(8,128)(2,1)S(1)} %copy-done.14, bf16[512,2048]{1,0:T(8,128)(2,1)S(1)} %copy-done.11, bf16[512,512]{1,0:T(8,128)(2,1)S(1)} %copy-done.17, bf16[2048,512]{1,0:T(8,128)(2,1)} %get-tuple-element.134.refs_3_, bf16[512,256]{1,0:T(8,128)(2,1)S(1)} %copy-done.20, ...), custom_call_target="tpu_custom_call" | custom-call | tf_op jit(solution)/shard_map/pack/pallas_call | solution.py:1021
  285.3 2.4 collective-permute-start.18
  293.1 6.5 %patch_attention_back.2 = (bf16[512,1024]{1,0:T(8,128)(2,1)S(1)}, bf16[512,256]{1,0:T(8,128)(2,1)S(1)}, bf16[512,512]{1,0:T(8,128)(2,1)S(1)}, bf16[512,512]{1,0:T(8,128)(2,1)S(1)}, bf16[512,512]{1,0:T(8,128)(2,1)S(1)}) custom-call(s32[2]{0:T(128)S(1)} %and_select_fusion.low_ref, s32[2,1,256]{2,1,0:T(1,128)S(1)} %bitcast.91, bf16[512,768]{1,0:T(8,128)(2,1)S(1)} %copy-done.48, ...), custom_call_target="tpu_custom_call" | custom-call | flops 8000000000 | bytes 25000000 | tf_op jit(solution)/shard_map/patch_attention_back/pallas_call | solution.py:261
  302.2 11.4 %patch_attention_back.3 = (bf16[512,1024]{1,0:T(8,128)(2,1)S(1)}, bf16[512,256]{1,0:T(8,128)(2,1)S(1)}, bf16[512,512]{1,0:T(8,128)(2,1)S(1)}, bf16[512,512]{1,0:T(8,128)(2,1)S(1)}, bf16[512,512]{1,0:T(8,128)(2,1)S(1)}) custom-call(s32[2]{0:T(128)S(1)} %and_select_fusion.1.low_ref, s32[2,1,256]{2,1,0:T(1,128)S(1)} %bitcast.89, ...), custom_call_target="tpu_custom_call" | custom-call | flops 8000000000 | bytes 25000000 | tf_op jit(solution)/shard_map/patch_attention_back/pallas_call | solution.py:261
  313.6 4.8 collective-permute-start.21
  318.5 13.1 %collective-permute-start.22 = (bf16[512,512]{1,0:T(8,128)(2,1)S(1)}, bf16[512,512]{1,0:T(8,128)(2,1)S(1)}, u32[]{:S(2)}, u32[]{:S(2)}) collective-permute-start(bf16[512,512]{1,0:T(8,128)(2,1)S(1)} %get-tuple-element.150), channel_id=1, source_target_pairs={{0,16},{8,24},{1,17},{9,25},{2,18},{10,26},{3,19},{11,27},{4,20},{... | collective-permute-start | bytes 1572872 | tf_op jit(solution)/shard_map/ppermute | solution.py:1070
  345.7 3.2 add_convert_fusion.refs_3_
  353.0 2.9 collective-permute-start.15
  361.1 40.3 %scatter_grads.1 = (f32[128,768]{1,0:T(8,128)S(1)}, f32[128,1024]{1,0:T(8,128)S(1)}, f32[256,128]{1,0:T(8,128)S(1)}, f32[1024,128]{1,0:T(8,128)S(1)}) custom-call(bf16[1024,768]{1,0:T(8,128)(2,1)S(1)} %add_convert_fusion.2.refs_0_, bf16[1024,1024]{1,0:T(8,128)(2,1)S(1)} %add_convert_fusion.1.refs_1_, bf16[256,1024]{1,0:T(8,128)(2,1)S(1)} %fusion.14.refs_2_, ...), custom_call_target="tpu_custom_call" | custom-call | flops 1000000 | bytes 120000000 | tf_op jit(solution)/shard_map/scatter_grads/pallas_call | solution.py:864
  402.0 2.9 collective-permute-start.23
  406.4 9.2 %collective-permute-done.24 = bf16[128,1024]{1,0:T(8,128)(2,1)S(1)} collective-permute-done((bf16[128,1024]{1,0:T(8,128)(2,1)S(1)}, bf16[128,1024]{1,0:T(8,128)(2,1)S(1)}, u32[]{:S(2)}, u32[]{:S(2)}) %collective-permute-start.24) | collective-permute-done | bytes 262176 | tf_op jit(solution)/shard_map/ppermute | solution.py:1042
  415.6 6.9 %collective-permute-done.23 = bf16[128,1024]{1,0:T(8,128)(2,1)S(1)} collective-permute-done((bf16[128,1024]{1,0:T(8,128)(2,1)S(1)}, bf16[128,1024]{1,0:T(8,128)(2,1)S(1)}, u32[]{:S(2)}, u32[]{:S(2)}) %collective-permute-start.23) | collective-permute-done | bytes 262176 | tf_op jit(solution)/shard_map/ppermute | solution.py:1042
  424.4 19.8 %scatter_small.1 = f32[544,128]{1,0:T(8,128)S(1)} custom-call(bf16[2176,128]{1,0:T(8,128)(2,1)S(1)} %bitcast.84), custom_call_target="tpu_custom_call" | custom-call | flops 1000000 | bytes 10000000 | tf_op jit(solution)/shard_map/scatter_small/pallas_call | solution.py:864
  452.8 10.8 %total_of.1 = f32[2,8,128]{2,1,0:T(8,128)} custom-call(f32[2,8,128]{2,1,0:T(8,128)} %stack.6.value), custom_call_target="tpu_custom_call" | custom-call | tf_op jit(solution)/shard_map/total_of/pallas_call | solution.py:923
  (331 shorter events, 135.4 us)
Async XLA Ops:
  7.2 143.3 %all-gather.2.cloned.1.call-start = ((), (), s32[]{:S(2)}) async-start(), calls=%async_computation.1 | async-start | bytes 7299072 | tf_op jit(solution)/shard_map/all_gather | solution.py:1093
  62.2 384.0 %reduce-scatter.2.cloned.1.call-start = ((), (), s32[]{:S(2)}) async-start(), calls=%async_computation.2 | async-start | bytes 7299072 | tf_op jit(solution)/shard_map/reduce_scatter | solution.py:1097
  73.8 52.6 %collective-permute-start.6 = (bf16[512,512]{1,0:T(8,128)(2,1)}, bf16[512,512]{1,0:T(8,128)(2,1)}, u32[]{:S(2)}, u32[]{:S(2)}) collective-permute-start(bf16[512,512]{1,0:T(8,128)(2,1)} %get-tuple-element.119), channel_id=1, source_target_pairs={{0,16},{8,24},{1,17},{9,25},{2,18},{10,26},{3,19},{11,27},{4,20},{... | collective-permute-start | bytes 1572872 | tf_op jit(solution)/shard_map/ppermute | solution.py:1070
  78.0 48.5 %collective-permute-start.5 = (bf16[512,512]{1,0:T(8,128)(2,1)}, bf16[512,512]{1,0:T(8,128)(2,1)}, u32[]{:S(2)}, u32[]{:S(2)}) collective-permute-start(bf16[512,512]{1,0:T(8,128)(2,1)} %get-tuple-element.119), channel_id=1, source_target_pairs={{0,8},{8,16},{16,24},{1,9},{9,17},{17,25},{2,10},{10,18},{18,26},{... | collective-permute-start | bytes 1572872 | tf_op jit(solution)/shard_map/ppermute | solution.py:1070
  92.1 44.8 %collective-permute-start.1 = (bf16[512,512]{1,0:T(8,128)(2,1)}, bf16[512,512]{1,0:T(8,128)(2,1)}, u32[]{:S(2)}, u32[]{:S(2)}) collective-permute-start(bf16[512,512]{1,0:T(8,128)(2,1)} %get-tuple-element.102), channel_id=1, source_target_pairs={{16,0},{24,8},{17,1},{25,9},{18,2},{26,10},{19,3},{27,11},{20,4},{... | collective-permute-start | bytes 1572872 | tf_op jit(solution)/shard_map/ppermute | solution.py:1070
  93.5 43.4 %collective-permute-start = (bf16[512,512]{1,0:T(8,128)(2,1)}, bf16[512,512]{1,0:T(8,128)(2,1)}, u32[]{:S(2)}, u32[]{:S(2)}) collective-permute-start(bf16[512,512]{1,0:T(8,128)(2,1)} %get-tuple-element.102), channel_id=1, source_target_pairs={{8,0},{16,8},{24,16},{9,1},{17,9},{25,17},{10,2},{18,10},{26,18},{... | collective-permute-start | bytes 1572872 | tf_op jit(solution)/shard_map/ppermute | solution.py:1070
  132.4 31.4 %collective-permute-start.9 = (bf16[128,1024]{1,0:T(8,128)(2,1)S(1)}, bf16[128,1024]{1,0:T(8,128)(2,1)S(1)}, u32[]{:S(2)}, u32[]{:S(2)}) collective-permute-start(bf16[128,1024]{1,0:T(8,128)(2,1)S(1)} %get-tuple-element.248), channel_id=1, source_target_pairs={{0,6},{2,4},{4,2},{6,0},{1,7},{3,5},{5,3},{7,1},{8,14},{10,12},{12... | collective-permute-start | bytes 786440 | tf_op jit(solution)/shard_map/ppermute | solution.py:1042
  134.4 35.5 %collective-permute-start.8 = (bf16[128,1024]{1,0:T(8,128)(2,1)S(1)}, bf16[128,1024]{1,0:T(8,128)(2,1)}, u32[]{:S(2)}, u32[]{:S(2)}) collective-permute-start(bf16[128,1024]{1,0:T(8,128)(2,1)S(1)} %get-tuple-element.249), channel_id=1, source_target_pairs={{0,4},{2,6},{4,0},{6,2},{1,5},{3,7},{5,1},{7,3},{8,12},{10,14},{12... | collective-permute-start | bytes 786440 | tf_op jit(solution)/shard_map/ppermute | solution.py:1042
  134.5 35.5 %collective-permute-start.7 = (bf16[128,1024]{1,0:T(8,128)(2,1)S(1)}, bf16[128,1024]{1,0:T(8,128)(2,1)}, u32[]{:S(2)}, u32[]{:S(2)}) collective-permute-start(bf16[128,1024]{1,0:T(8,128)(2,1)S(1)} %get-tuple-element.250), channel_id=1, source_target_pairs={{0,2},{2,0},{4,6},{6,4},{1,3},{3,1},{5,7},{7,5},{8,10},{10,8},{12,... | collective-permute-start | bytes 786440 | tf_op jit(solution)/shard_map/ppermute | solution.py:1042
  146.8 69.4 %collective-permute-start.4 = (bf16[128,1024]{1,0:T(8,128)(2,1)S(1)}, bf16[128,1024]{1,0:T(8,128)(2,1)}, u32[]{:S(2)}, u32[]{:S(2)}) collective-permute-start(bf16[128,1024]{1,0:T(8,128)(2,1)S(1)} %get-tuple-element.251), channel_id=1, source_target_pairs={{0,6},{2,4},{4,2},{6,0},{1,7},{3,5},{5,3},{7,1},{8,14},{10,12},{12... | collective-permute-start | bytes 786440 | tf_op jit(solution)/shard_map/ppermute | solution.py:1042
  148.8 69.8 %collective-permute-start.3 = (bf16[128,1024]{1,0:T(8,128)(2,1)S(1)}, bf16[128,1024]{1,0:T(8,128)(2,1)}, u32[]{:S(2)}, u32[]{:S(2)}) collective-permute-start(bf16[128,1024]{1,0:T(8,128)(2,1)S(1)} %get-tuple-element.252), channel_id=1, source_target_pairs={{0,4},{2,6},{4,0},{6,2},{1,5},{3,7},{5,1},{7,3},{8,12},{10,14},{12... | collective-permute-start | bytes 786440 | tf_op jit(solution)/shard_map/ppermute | solution.py:1042
  163.9 54.8 %collective-permute-start.2 = (bf16[128,1024]{1,0:T(8,128)(2,1)S(1)}, bf16[128,1024]{1,0:T(8,128)(2,1)S(1)}, u32[]{:S(2)}, u32[]{:S(2)}) collective-permute-start(bf16[128,1024]{1,0:T(8,128)(2,1)S(1)} %get-tuple-element.253), channel_id=1, source_target_pairs={{0,2},{2,0},{4,6},{6,4},{1,3},{3,1},{5,7},{7,5},{8,10},{10,8},{12,... | collective-permute-start | bytes 786440 | tf_op jit(solution)/shard_map/ppermute | solution.py:1042
  214.2 70.1 %collective-permute-start.12 = (bf16[128,1024]{1,0:T(8,128)(2,1)}, bf16[128,1024]{1,0:T(8,128)(2,1)S(1)}, u32[]{:S(2)}, u32[]{:S(2)}) collective-permute-start(bf16[128,1024]{1,0:T(8,128)(2,1)} %get-tuple-element.138.rest_5_), channel_id=1, source_target_pairs={{0,6},{2,4},{4,2},{6,0},{1,7},{3,5},{5,3},{7,1},{8,14},{10,12},{12... | collective-permute-start | bytes 786440 | tf_op jit(solution)/shard_map/ppermute | solution.py:1042
  216.2 71.5 %collective-permute-start.11 = (bf16[128,1024]{1,0:T(8,128)(2,1)}, bf16[128,1024]{1,0:T(8,128)(2,1)S(1)}, u32[]{:S(2)}, u32[]{:S(2)}) collective-permute-start(bf16[128,1024]{1,0:T(8,128)(2,1)} %get-tuple-element.138.rest_5_), channel_id=1, source_target_pairs={{0,4},{2,6},{4,0},{6,2},{1,5},{3,7},{5,1},{7,3},{8,12},{10,14},{12... | collective-permute-start | bytes 786440 | tf_op jit(solution)/shard_map/ppermute | solution.py:1042
  216.2 72.2 %collective-permute-start.10 = (bf16[128,1024]{1,0:T(8,128)(2,1)}, bf16[128,1024]{1,0:T(8,128)(2,1)S(1)}, u32[]{:S(2)}, u32[]{:S(2)}) collective-permute-start(bf16[128,1024]{1,0:T(8,128)(2,1)} %get-tuple-element.138.rest_5_), channel_id=1, source_target_pairs={{0,2},{2,0},{4,6},{6,4},{1,3},{3,1},{5,7},{7,5},{8,10},{10,8},{12,... | collective-permute-start | bytes 786440 | tf_op jit(solution)/shard_map/ppermute | solution.py:1042
  266.2 35.9 %collective-permute-start.20 = (bf16[128,1024]{1,0:T(8,128)(2,1)}, bf16[128,1024]{1,0:T(8,128)(2,1)}, u32[]{:S(2)}, u32[]{:S(2)}) collective-permute-start(bf16[128,1024]{1,0:T(8,128)(2,1)} %get-tuple-element.146.rest_5_), channel_id=1, source_target_pairs={{0,6},{2,4},{4,2},{6,0},{1,7},{3,5},{5,3},{7,1},{8,14},{10,12},{12... | collective-permute-start | bytes 786440 | tf_op jit(solution)/shard_map/ppermute | solution.py:1042
  268.3 33.9 %collective-permute-start.19 = (bf16[128,1024]{1,0:T(8,128)(2,1)}, bf16[128,1024]{1,0:T(8,128)(2,1)}, u32[]{:S(2)}, u32[]{:S(2)}) collective-permute-start(bf16[128,1024]{1,0:T(8,128)(2,1)} %get-tuple-element.146.rest_5_), channel_id=1, source_target_pairs={{0,4},{2,6},{4,0},{6,2},{1,5},{3,7},{5,1},{7,3},{8,12},{10,14},{12... | collective-permute-start | bytes 786440 | tf_op jit(solution)/shard_map/ppermute | solution.py:1042
  285.3 16.9 %collective-permute-start.18 = (bf16[128,1024]{1,0:T(8,128)(2,1)S(1)}, bf16[128,1024]{1,0:T(8,128)(2,1)S(1)}, u32[]{:S(2)}, u32[]{:S(2)}) collective-permute-start(bf16[128,1024]{1,0:T(8,128)(2,1)S(1)} %copy-done.19), channel_id=1, source_target_pairs={{0,2},{2,0},{4,6},{6,4},{1,3},{3,1},{5,7},{7,5},{8,10},{10,8},{12,... | collective-permute-start | bytes 786440 | tf_op jit(solution)/shard_map/ppermute | solution.py:1042
  299.6 49.3 %collective-permute-start.13 = (bf16[512,512]{1,0:T(8,128)(2,1)S(1)}, bf16[512,512]{1,0:T(8,128)(2,1)S(1)}, u32[]{:S(2)}, u32[]{:S(2)}) collective-permute-start(bf16[512,512]{1,0:T(8,128)(2,1)S(1)} %get-tuple-element.142), channel_id=1, source_target_pairs={{8,0},{16,8},{24,16},{9,1},{17,9},{25,17},{10,2},{18,10},{26,18},{... | collective-permute-start | bytes 1572872 | tf_op jit(solution)/shard_map/ppermute | solution.py:1070
  300.9 48.0 %collective-permute-start.14 = (bf16[512,512]{1,0:T(8,128)(2,1)S(1)}, bf16[512,512]{1,0:T(8,128)(2,1)S(1)}, u32[]{:S(2)}, u32[]{:S(2)}) collective-permute-start(bf16[512,512]{1,0:T(8,128)(2,1)S(1)} %get-tuple-element.143), channel_id=1, source_target_pairs={{16,0},{24,8},{17,1},{25,9},{18,2},{26,10},{19,3},{27,11},{20,4},{... | collective-permute-start | bytes 1572872 | tf_op jit(solution)/shard_map/ppermute | solution.py:1070
  313.6 42.2 %collective-permute-start.21 = (bf16[512,512]{1,0:T(8,128)(2,1)S(1)}, bf16[512,512]{1,0:T(8,128)(2,1)S(1)}, u32[]{:S(2)}, u32[]{:S(2)}) collective-permute-start(bf16[512,512]{1,0:T(8,128)(2,1)S(1)} %get-tuple-element.149), channel_id=1, source_target_pairs={{0,8},{8,16},{16,24},{1,9},{9,17},{17,25},{2,10},{10,18},{18,26},{... | collective-permute-start | bytes 1572872 | tf_op jit(solution)/shard_map/ppermute | solution.py:1070
  318.5 37.4 %collective-permute-start.22 = (bf16[512,512]{1,0:T(8,128)(2,1)S(1)}, bf16[512,512]{1,0:T(8,128)(2,1)S(1)}, u32[]{:S(2)}, u32[]{:S(2)}) collective-permute-start(bf16[512,512]{1,0:T(8,128)(2,1)S(1)} %get-tuple-element.150), channel_id=1, source_target_pairs={{0,16},{8,24},{1,17},{9,25},{2,18},{10,26},{3,19},{11,27},{4,20},{... | collective-permute-start | bytes 1572872 | tf_op jit(solution)/shard_map/ppermute | solution.py:1070
  351.4 50.6 %collective-permute-start.17 = (bf16[128,1024]{1,0:T(8,128)(2,1)S(1)}, bf16[128,1024]{1,0:T(8,128)(2,1)S(1)}, u32[]{:S(2)}, u32[]{:S(2)}) collective-permute-start(bf16[128,1024]{1,0:T(8,128)(2,1)S(1)} %get-tuple-element.245), channel_id=1, source_target_pairs={{0,6},{2,4},{4,2},{6,0},{1,7},{3,5},{5,3},{7,1},{8,14},{10,12},{12... | collective-permute-start | bytes 786440 | tf_op jit(solution)/shard_map/ppermute | solution.py:1042
  352.8 53.5 %collective-permute-start.16 = (bf16[128,1024]{1,0:T(8,128)(2,1)S(1)}, bf16[128,1024]{1,0:T(8,128)(2,1)S(1)}, u32[]{:S(2)}, u32[]{:S(2)}) collective-permute-start(bf16[128,1024]{1,0:T(8,128)(2,1)S(1)} %get-tuple-element.246), channel_id=1, source_target_pairs={{0,4},{2,6},{4,0},{6,2},{1,5},{3,7},{5,1},{7,3},{8,12},{10,14},{12... | collective-permute-start | bytes 786440 | tf_op jit(solution)/shard_map/ppermute | solution.py:1042
  353.0 53.4 %collective-permute-start.15 = (bf16[128,1024]{1,0:T(8,128)(2,1)S(1)}, bf16[128,1024]{1,0:T(8,128)(2,1)S(1)}, u32[]{:S(2)}, u32[]{:S(2)}) collective-permute-start(bf16[128,1024]{1,0:T(8,128)(2,1)S(1)} %get-tuple-element.247), channel_id=1, source_target_pairs={{0,2},{2,0},{4,6},{6,4},{1,3},{3,1},{5,7},{7,5},{8,10},{10,8},{12,... | collective-permute-start | bytes 786440 | tf_op jit(solution)/shard_map/ppermute | solution.py:1042
  357.2 49.1 %collective-permute-start.25 = (bf16[128,1024]{1,0:T(8,128)(2,1)S(1)}, bf16[128,1024]{1,0:T(8,128)(2,1)S(1)}, u32[]{:S(2)}, u32[]{:S(2)}) collective-permute-start(bf16[128,1024]{1,0:T(8,128)(2,1)S(1)} %get-tuple-element.242), channel_id=1, source_target_pairs={{0,6},{2,4},{4,2},{6,0},{1,7},{3,5},{5,3},{7,1},{8,14},{10,12},{12... | collective-permute-start | bytes 786440 | tf_op jit(solution)/shard_map/ppermute | solution.py:1042
  358.7 56.9 %collective-permute-start.24 = (bf16[128,1024]{1,0:T(8,128)(2,1)S(1)}, bf16[128,1024]{1,0:T(8,128)(2,1)S(1)}, u32[]{:S(2)}, u32[]{:S(2)}) collective-permute-start(bf16[128,1024]{1,0:T(8,128)(2,1)S(1)} %get-tuple-element.243), channel_id=1, source_target_pairs={{0,4},{2,6},{4,0},{6,2},{1,5},{3,7},{5,1},{7,3},{8,12},{10,14},{12... | collective-permute-start | bytes 786440 | tf_op jit(solution)/shard_map/ppermute | solution.py:1042
  361.0 61.5 %copy-start.52 = (bf16[128,1024]{1,0:T(8,128)(2,1)S(1)}, bf16[128,1024]{1,0:T(8,128)(2,1)}, u32[]{:S(2)}) copy-start(bf16[128,1024]{1,0:T(8,128)(2,1)} %get-tuple-element.239.start_ref) | copy-start | bytes 786436
  361.0 61.5 %copy-start.53 = (bf16[128,1024]{1,0:T(8,128)(2,1)S(1)}, bf16[128,1024]{1,0:T(8,128)(2,1)}, u32[]{:S(2)}) copy-start(bf16[128,1024]{1,0:T(8,128)(2,1)} %get-tuple-element.241.start_ref) | copy-start | bytes 786436
  361.0 61.5 %copy-start.77 = (f32[1024]{0:T(1024)S(1)}, f32[1024]{0:T(1024)}, u32[]{:S(2)}) copy-start(f32[1024]{0:T(1024)} %get-tuple-element.269) | copy-start | bytes 12292
  361.0 61.5 %copy-start.81 = (f32[128]{0:T(128)S(1)}, f32[128]{0:T(128)}, u32[]{:S(2)}) copy-start(f32[128]{0:T(128)} %add_rsqrt_fusion.1) | copy-start | bytes 1540
  402.0 20.5 %collective-permute-start.23 = (bf16[128,1024]{1,0:T(8,128)(2,1)S(1)}, bf16[128,1024]{1,0:T(8,128)(2,1)S(1)}, u32[]{:S(2)}, u32[]{:S(2)}) collective-permute-start(bf16[128,1024]{1,0:T(8,128)(2,1)S(1)} %get-tuple-element.244), channel_id=1, source_target_pairs={{0,2},{2,0},{4,6},{6,4},{1,3},{3,1},{5,7},{7,5},{8,10},{10,8},{12,... | collective-permute-start | bytes 786440 | tf_op jit(solution)/shard_map/ppermute | solution.py:1042
  (84 other events, 550.6 us)
Sparse Core Ops, SparseCore 0:
  62.4 74.7 all-gather.1
  284.4 159.4 reduce-scatter.1

commit v3 on v2

--- a/solution.py
+++ b/solution.py
@@ -1,4 +1,5 @@
 import functools
+import types
 
 import jax
 import jax.numpy as jnp
@@ -17,9 +18,11 @@
 LHEADDIM = 64
 GSLOT = 128
 BLK = 256
+ITEMS = 5
 F32 = jnp.float32
 BF16 = jnp.bfloat16
 MESH = pl.DeviceIdType.MESH
+SLOT, STACK, CORE = "slot", "mp", "dp"
 
 longest_item = 1024
 
@@ -131,17 +134,38 @@
         keys_t[:, at : at + rows] = jnp.transpose(own_ref[:, width : 2 * width])
 
 
-def fwd_kernel(rows, width, count, low_ref, start_ref, own_ref, *rest):
+def chunk_begin(forward, rows):
+    slot, slots = lax.axis_index(SLOT), lax.axis_size(SLOT)
+    return (slot if forward else slots - 1 - slot) * rows
+
+
+def item_starts(items_ref, micro, begin, rows, reach):
+    items = items_ref[micro]
+    starts = []
+    for qt in range(rows // BLK):
+        own = items_ref[micro, :, pl.ds(pl.multiple_of(begin + qt * BLK, BLK), BLK)]
+        first = jnp.zeros((1, BLK), F32)
+        for value in range(1, ITEMS):
+            ahead = jnp.sum(jnp.where(items < value, 1.0, 0.0), axis=1, keepdims=True)
+            first = jnp.where(own == value, ahead, first)
+        first = jnp.maximum(first - (begin - reach * rows).astype(F32), 0.0)
+        low = lax.div(jnp.min(first).astype(jnp.int32), BLK)
+        first = first.astype(jnp.int32)
+        starts.append((jnp.concatenate([first, first], axis=1), low))
+    return starts
+
+
+def fwd_kernel(rows, width, count, micro, forward, items_ref, own_ref, *rest):
     earlier, (att_ref, lse_ref, keys, values_t) = rest[:count], rest[count:]
     window_fill(rows, width, own_ref, earlier, keys, values_t, None, None)
+    starts = item_starts(items_ref, micro, chunk_begin(forward, rows), rows, count)
     base = count * rows
     key_iota = lax.broadcasted_iota(jnp.int32, (BLK, 2 * BLK), 0)
     q_iota = lax.broadcasted_iota(jnp.int32, (1, 2 * BLK), 1) % BLK
     pairs = width // 128
     for qt in range(rows // BLK):
         q_pos = q_iota + (base + qt * BLK)
-        start = start_ref[qt]
-        start = jnp.concatenate([start, start], axis=1)
+        start, low = starts[qt]
         for pair in range(pairs):
             cs = slice(pair * 128, pair * 128 + 128)
             qs = stack_heads(own_ref[qt * BLK : (qt + 1) * BLK, cs] * jnp.asarray(0.125, BF16))
@@ -165,7 +189,7 @@
                 jnp.zeros((1, 2 * BLK), F32),
                 jnp.zeros((128, 2 * BLK), F32),
             )
-            top, total, acc = lax.fori_loop(0, base // BLK + qt + 1 - low_ref[qt], block, init)
+            top, total, acc = lax.fori_loop(0, base // BLK + qt + 1 - low, block, init)
             acc = acc * (1.0 / total)
             sub = lax.broadcasted_iota(jnp.int32, (128, BLK), 0)
             both = jnp.where(sub < 64, acc[:, :BLK], acc[:, BLK:])
@@ -173,19 +197,20 @@
             lse_ref[qt * pairs + pair] = top + jnp.log(total)
 
 
-def bwd_kernel(rows, width, count, pieces, low_ref, start_ref, own_ref, *rest):
+def bwd_kernel(rows, width, count, pieces, micro, forward, items_ref, own_ref, *rest):
     earlier = rest[:count]
     att_ref, lse_ref, weight_ref = rest[count : count + 3]
     rest = rest[count + 3 :]
     piece_refs, rest = rest[:pieces], rest[pieces:]
     branch_ref, dq_ref, dkv_refs = rest[0], rest[1], rest[2 : count + 3]
     keys, values, keys_t, dkeys, dvalues, attg_ref = rest[count + 3 :]
-    place, share = lax.axis_index("mp"), rows // pieces
+    place, share = lax.axis_index(STACK), rows // pieces
     for j in range(pieces):
         at = pl.ds(pl.multiple_of(origin(place, j, pieces) * share, share), share)
         branch_ref[at, :] = piece_refs[j][...]
     attg_ref[...] = mm_nt(branch_ref[...], weight_ref[...]).astype(BF16)
     window_fill(rows, width, own_ref, earlier, keys, None, values, keys_t)
+    starts = item_starts(items_ref, micro, chunk_begin(forward, rows), rows, count)
     base = count * rows
     dkeys[...] = jnp.zeros_like(dkeys)
     dvalues[...] = jnp.zeros_like(dvalues)
@@ -194,8 +219,7 @@
     pairs = width // 128
     for qt in range(rows // BLK):
         q_pos = q_iota + (base + qt * BLK)
-        start = start_ref[qt]
-        start = jnp.concatenate([start, start], axis=1)
+        start, low = starts[qt]
         rq = slice(qt * BLK, (qt + 1) * BLK)
         for pair in range(pairs):
             cs = slice(pair * 128, pair * 128 + 128)
@@ -219,7 +243,7 @@
                 return acc + mm(keys_t[cs, at], ds)
 
             acc = lax.fori_loop(
-                0, base // BLK + qt + 1 - low_ref[qt], block, jnp.zeros((128, 2 * BLK), F32)
+                0, base // BLK + qt + 1 - low, block, jnp.zeros((128, 2 * BLK), F32)
             )
             sub = lax.broadcasted_iota(jnp.int32, (128, BLK), 0)
             both = jnp.where(sub < 64, acc[:, :BLK], acc[:, BLK:]) * 0.125
@@ -231,16 +255,16 @@
 
 
 def specs(n):
-    return [pl.BlockSpec(memory_space=pltpu.SMEM)] + [pl.BlockSpec(memory_space=pltpu.VMEM)] * n
-
-
-def attention_fwd(low, start, own, earlier):
+    return [pl.BlockSpec(memory_space=pltpu.VMEM)] * n
+
+
+def attention_fwd(items, micro, forward, own, earlier):
     rows, width = own.shape[0], own.shape[1] // 3
     count = len(earlier)
     span = (count + 1) * rows
     units = rows // BLK * (width // 128)
     return pl.pallas_call(
-        functools.partial(fwd_kernel, rows, width, count),
+        functools.partial(fwd_kernel, rows, width, count, micro, forward),
         out_shape=[
             jax.ShapeDtypeStruct((rows, width), BF16),
             jax.ShapeDtypeStruct((units, 1, 2 * BLK), F32),
@@ -251,15 +275,15 @@
         cost_estimate=pl.CostEstimate(flops=6 * 10**9, bytes_accessed=20 * 10**6, transcendentals=10**6),
         compiler_params=pltpu.CompilerParams(vmem_limit_bytes=32 * 2**20),
         name="patch_attention",
-    )(low, start, own, *earlier)
-
-
-def attention_bwd(low, start, own, earlier, attended, lse, weight, pieces):
+    )(items, own, *earlier)
+
+
+def attention_bwd(items, micro, forward, own, earlier, attended, lse, weight, pieces):
     rows, width = own.shape[0], own.shape[1] // 3
     count = len(earlier)
     span = (count + 1) * rows
     out = pl.pallas_call(
-        functools.partial(bwd_kernel, rows, width, count, len(pieces)),
+        functools.partial(bwd_kernel, rows, width, count, len(pieces), micro, forward),
         out_shape=[jax.ShapeDtypeStruct((rows, pieces[0].shape[1]), BF16), jax.ShapeDtypeStruct((rows, width), BF16)]
         + [jax.ShapeDtypeStruct((rows, 2 * width), BF16)] * (count + 1),
         in_specs=specs(5 + count + len(pieces)),
@@ -275,13 +299,28 @@
         cost_estimate=pl.CostEstimate(flops=8 * 10**9, bytes_accessed=25 * 10**6, transcendentals=10**6),
         compiler_params=pltpu.CompilerParams(vmem_limit_bytes=32 * 2**20),
         name="patch_attention_back",
-    )(low, start, own, *earlier, attended, lse, weight, *pieces)
+    )(items, own, *earlier, attended, lse, weight, *pieces)
     return out[0], out[1], out[2:]
 
 
-def embed_kernel(width, ids_ref, table_ref, w_ref, gain_ref, start_ref, hidden_ref, proj_ref, kv_ref):
-    rows = ids_ref.shape[0]
-    ids = ids_ref[...].astype(F32)
+def embed_kernel(
+    width, rows, micro, forward, ids_ref, items_ref, table_ref, w_ref, gain_ref,
+    start_ref, hidden_ref, proj_ref, kv_ref, previous_ref,
+):
+    begin = pl.multiple_of(chunk_begin(forward, rows), 128)
+    edge = pl.multiple_of(jnp.maximum(begin - 128, 0), 128)
+
+    def delayed(ref):
+        own, before = ref[micro, :, pl.ds(begin, rows)], ref[micro, :, pl.ds(edge, 128)]
+        place = lax.broadcasted_iota(jnp.int32, own.shape, 1)
+        return own, jnp.where(place == 0, before[:, 127:128], pltpu.roll(own, 1, axis=1))
+
+    own_items, earlier_items = delayed(items_ref)
+    place = lax.broadcasted_iota(jnp.int32, own_items.shape, 1)
+    keep = (own_items == earlier_items) & ((place > 0) | (begin > 0))
+    ids = jnp.where(keep, delayed(ids_ref)[1], -1).astype(F32)
+    ids = jnp.transpose(ids)
+    previous_ref[...] = ids.astype(jnp.int32)
     low = lax.broadcasted_iota(jnp.int32, (rows, 128), 1).astype(F32)
     squares = jnp.zeros((rows, 1), F32)
     parts = []
@@ -307,23 +346,49 @@
             kv_ref[:, (c - 1) * width : c * width] = part
 
 
-def embed_rows(ids, table, weight, gain):
-    rows, width = ids.shape[0], weight.shape[1] // 3
+def embed_rows(ids, items, micro, forward, rows, table, weight, gain):
+    width = weight.shape[1] // 3
     vm = pl.BlockSpec(memory_space=pltpu.VMEM)
     return pl.pallas_call(
-        functools.partial(embed_kernel, width),
+        functools.partial(embed_kernel, width, rows, micro, forward),
         out_shape=[
             jax.ShapeDtypeStruct((rows, D), BF16),
             jax.ShapeDtypeStruct((rows, D), BF16),
             jax.ShapeDtypeStruct((rows, 3 * width), BF16),
             jax.ShapeDtypeStruct((rows, 2 * width), BF16),
+            jax.ShapeDtypeStruct((rows, SLOTS), jnp.int32),
         ],
-        in_specs=[vm] * 4,
-        out_specs=[vm] * 4,
+        in_specs=[vm] * 5,
+        out_specs=[vm] * 5,
         cost_estimate=pl.CostEstimate(flops=2 * 10**9, bytes_accessed=6 * 10**6, transcendentals=1000),
         compiler_params=pltpu.CompilerParams(vmem_limit_bytes=32 * 2**20),
         name="embed_rows",
-    )(ids, table, weight, gain)
+    )(ids, items, table, weight, gain)
+
+
+def up_kernel(count, *refs):
+    hidden, weight, outs = refs[:count], refs[count], refs[count + 1 :]
+    for i in range(count):
+        for c in range(0, weight.shape[1], 256):
+            value, slope = gelu_pair(mm(hidden[i][...], weight[:, c : c + 256]))
+            outs[2 * i][:, c : c + 256] = value.astype(BF16)
+            outs[2 * i + 1][:, c : c + 256] = slope.astype(BF16)
+
+
+def up_rows(hidden, weight):
+    count = len(hidden)
+    vm = pl.BlockSpec(memory_space=pltpu.VMEM)
+    shape = jax.ShapeDtypeStruct((hidden[0].shape[0], weight.shape[1]), BF16)
+    out = pl.pallas_call(
+        functools.partial(up_kernel, count),
+        out_shape=[shape] * (2 * count),
+        in_specs=[vm] * (count + 1),
+        out_specs=[vm] * (2 * count),
+        cost_estimate=pl.CostEstimate(flops=4 * 10**9, bytes_accessed=10**7, transcendentals=10**6),
+        compiler_params=pltpu.CompilerParams(vmem_limit_bytes=32 * 2**20),
+        name="up_rows",
+    )(*hidden, weight)
+    return [(out[2 * i], out[2 * i + 1]) for i in range(count)]
 
 
 def gelu_pair(x):
@@ -337,7 +402,7 @@
 
 def byte_kernel(
     rows, tile, with_base,
-    pieces, start_ref, own_ref, *rest
+    pieces, micro, forward, slot_rows, start_ref, own_ref, *rest
 ):
     piece_refs, rest = rest[:pieces], rest[pieces:]
     ids_ref, mask_ref, count_ref, w_in, w_up, w_out, w_down, w_head, w_embed, w_bridge, gains_ref = rest[:11]
@@ -359,6 +424,10 @@
     causal = lax.broadcasted_iota(jnp.int32, (SLOTS, 256), 0) <= lane % SLOTS
     none = jnp.zeros((SLOTS, 256), F32)
     patches = rows // SLOTS
+    begin = chunk_begin(forward, slot_rows) + lax.axis_index(STACK) * patches
+    here = pl.ds(pl.multiple_of(begin, 128), patches)
+    ids = jnp.transpose(ids_ref[micro, :, here].astype(F32))
+    counts = jnp.transpose(mask_ref[micro, :, here].astype(F32))
     for j in range(SLOTS):
         cs = slice(j * GSLOT, (j + 1) * GSLOT)
         at = pl.ds(j, patches, stride=SLOTS)
@@ -367,9 +436,9 @@
             total = total + piece[:, cs].astype(F32)
         wide_rows[at, :] = total
         spread = functools.partial(jnp.broadcast_to, shape=(patches, 128))
-        own_ids[at, :] = spread(ids_ref[:, j : j + 1].astype(F32))
-        prev_ids[at, :] = spread(ids_ref[:, j - 1 : j].astype(F32)) if j else jnp.full((patches, 128), -1.0, F32)
-        weights[at, :] = spread(mask_ref[:, j : j + 1].astype(F32) / count_ref[0, 0])
+        own_ids[at, :] = spread(ids[:, j : j + 1])
+        prev_ids[at, :] = spread(ids[:, j - 1 : j]) if j else jnp.full((patches, 128), -1.0, F32)
+        weights[at, :] = spread(counts[:, j : j + 1] / count_ref[0, 0])
     inputs_ref[...] = wide_rows[...].astype(BF16)
 
     def one_hot(ids):
@@ -537,7 +606,7 @@
     put(g_bridge, (every, every), mm_tn(inputs_ref[...], sgrad[...]), 6)
 
 
-def byte_layer(start, own, pieces, ids, mask, count, weights, gains, base=None, tile=512):
+def byte_layer(start, own, pieces, ids, mask, micro, forward, slot_rows, count, weights, gains, base=None, tile=512):
     rows = start.shape[0] * SLOTS
     shapes = [(LD, 3 * LD), (LD, LFF), (LD, LD), (LFF, LD), (LD, VOCAB), (VOCAB, LD), (GSLOT, LD)]
     out_shape = [jax.ShapeDtypeStruct(s, BF16) for s in shapes] + [
@@ -548,7 +617,7 @@
     in_specs = [vm] * len(args)
     in_specs[4 + len(pieces)] = pl.BlockSpec(memory_space=pltpu.SMEM)
     return pl.pallas_call(
-        functools.partial(byte_kernel, rows, tile, base is not None, len(pieces)),
+        functools.partial(byte_kernel, rows, tile, base is not None, len(pieces), micro, forward, slot_rows),
         out_shape=out_shape,
         in_specs=in_specs,
         out_specs=[vm] * len(out_shape),
@@ -608,14 +677,14 @@
 
 
 def group_peers(slots, groups):
-    s, m, d = lax.axis_index("slot"), lax.axis_index("mp"), lax.axis_index("dp")
+    s, m, d = lax.axis_index(SLOT), lax.axis_index(STACK), lax.axis_index(CORE)
     across = [(other(s, j, slots), m, d) for j in range(1, slots)]
     beside = [(s, m, other(d, k, groups)) for k in range(1, groups)]
     return across, beside
 
 
 def stack_peers(stacks):
-    s, m, d = lax.axis_index("slot"), lax.axis_index("mp"), lax.axis_index("dp")
+    s, m, d = lax.axis_index(SLOT), lax.axis_index(STACK), lax.axis_index(CORE)
     return [(s, other(m, j, stacks), d) for j in range(1, stacks)]
 
 
@@ -626,7 +695,7 @@
     outs, gain_out, count_out = refs[count + 2 : 2 * count + 2], refs[2 * count + 2], refs[2 * count + 3]
     shards, rest = refs[2 * count + 4 : 3 * count + 4], refs[3 * count + 4 :]
     (tail_z, tail_s, tail_d, held_count, own_sem, xs, xr, cs, cr, zs, zr, ts, tr, ds, dr, ns, nr) = rest
-    s, m, d = lax.axis_index("slot"), lax.axis_index("mp"), lax.axis_index("dp")
+    s, m, d = lax.axis_index(SLOT), lax.axis_index(STACK), lax.axis_index(CORE)
     across, beside = group_peers(slots, groups)
     above = stack_peers(stacks)
     for w in range(count):
@@ -725,7 +794,7 @@
 
 
 def gather_weights(shards, columns, tail, counted):
-    sizes = tuple(lax.axis_size(axis) for axis in ("slot", "mp", "dp"))
+    sizes = tuple(lax.axis_size(axis) for axis in (SLOT, STACK, CORE))
     slots, stacks, groups = sizes
     count = len(shards)
     parts = slots * groups
@@ -774,7 +843,7 @@
     cs, cr, xs, xr = rest[3 * count : 3 * count + 4]
     if shared:
         from_z, own_c, from_c, zs, zr, ts, tr = rest[3 * count + 4 :]
-    s, m, d = lax.axis_index("slot"), lax.axis_index("mp"), lax.axis_index("dp")
+    s, m, d = lax.axis_index(SLOT), lax.axis_index(STACK), lax.axis_index(CORE)
     across, beside = group_peers(slots, groups)
     above = stack_peers(stacks)
     greet(across + beside + above if shared else across + beside)
@@ -848,7 +917,7 @@
 
 
 def scatter_grads(partials, columns, shared=False):
-    sizes = tuple(lax.axis_size(axis) for axis in ("slot", "mp", "dp"))
+    sizes = tuple(lax.axis_size(axis) for axis in (SLOT, STACK, CORE))
     slots, stacks, groups = sizes
     count = len(partials)
     parts = slots * groups
@@ -897,7 +966,7 @@
     greet(across + beside + above)
     total = value[...]
     for axis, peers, held, send, recv in (
-        ("mp", above, held_z, zs, zr), ("slot", across, held_s, xs, xr), ("dp", beside, held_d, cs, cr)
+        (STACK, above, held_z, zs, zr), (SLOT, across, held_s, xs, xr), (CORE, beside, held_d, cs, cr)
     ):
         index = lax.axis_index(axis)
         held[index] = total
@@ -916,7 +985,7 @@
 
 
 def total_of(value):
-    sizes = tuple(lax.axis_size(axis) for axis in ("slot", "mp", "dp"))
+    sizes = tuple(lax.axis_size(axis) for axis in (SLOT, STACK, CORE))
     slots, stacks, groups = sizes
     vm = pl.BlockSpec(memory_space=pltpu.VMEM)
     dma = pltpu.SemaphoreType.DMA
@@ -1062,12 +1131,12 @@
 
 
 def shift_chunks(value, distance, forward):
-    size = lax.axis_size("slot")
+    size = lax.axis_size(SLOT)
     if forward:
         pairs = [(i, i + distance) for i in range(size - distance)]
     else:
         pairs = [(i + distance, i) for i in range(size - distance)]
-    return lax.ppermute(value, "slot", pairs)
+    return lax.ppermute(value, SLOT, pairs)
 
 
 def update(weight, moment, average, gradient, factor, rate):
@@ -1084,20 +1153,13 @@
 
 def gather_pack(local_pack):
     share = local_pack.shape[0]
-    index = lax.axis_index(("slot", "mp", "dp"))
+    index = lax.axis_index((SLOT, STACK, CORE))
     offset = lax.rem(index * share, 128)
     rows = block_rows(share)
     block = lax.dynamic_update_slice_in_dim(
         jnp.zeros((rows * 128,), BF16), local_pack.astype(BF16), offset, 0
     )
-    return lax.all_gather(block.reshape(rows, 128), ("slot", "mp", "dp"), axis=0, tiled=True)
-
-
-def scatter_pack(blocks, share):
-    own = lax.psum_scatter(blocks, ("slot", "mp", "dp"), scatter_dimension=0, tiled=True)
-    index = lax.axis_index(("slot", "mp", "dp"))
-    offset = lax.rem(index * share, 128)
-    return lax.dynamic_slice_in_dim(own.reshape(-1), offset, share, 0).astype(F32)
+    return lax.all_gather(block.reshape(rows, 128), (SLOT, STACK, CORE), axis=0, tiled=True)
 
 
 def local(
@@ -1108,13 +1170,13 @@
     average_attend_in, average_expand_in, average_attend_out, average_expand_out,
     average_slot_table, average_local_pack,
 ):
-    slot_size, mp_size = lax.axis_size("slot"), lax.axis_size("mp")
+    slot_size, mp_size = lax.axis_size(SLOT), lax.axis_size(STACK)
     slot_index, mp_index, dp_index = (
-        lax.axis_index("slot"), lax.axis_index("mp"), lax.axis_index("dp"),
+        lax.axis_index(SLOT), lax.axis_index(STACK), lax.axis_index(CORE),
     )
     counted = jnp.full((8, 128), jnp.sum(loss_mask.astype(F32)))
     width = attend_in.shape[2]
-    piece = slot_table.shape[0] * VOCAB // lax.axis_size("dp")
+    piece = slot_table.shape[0] * VOCAB // lax.axis_size(CORE)
     table_shard = lax.dynamic_slice_in_dim(
         slot_table.reshape(-1, GSLOT), dp_index * piece, piece, 0
     )
@@ -1131,10 +1193,9 @@
             shards, (False, False, False), tail, counted
         )
         full_out, full_shrink = (
-            lax.all_gather(v.astype(BF16), ("slot", "dp"), axis=1, tiled=True) for v in late
+            lax.all_gather(v.astype(BF16), (SLOT, CORE), axis=1, tiled=True) for v in late
         )
-    local_pack_later, gains = lax.optimization_barrier((local_pack, gains))
-    pack_whole = gather_pack(local_pack_later)
+    pack_whole = gather_pack(local_pack)
     gains = gains.reshape(-1)
     mask_count = counted[0, 0]
     gain_global = gains[:D]
@@ -1145,107 +1206,95 @@
     local_rows = rows // mp_size
     vocab_ids = jnp.arange(VOCAB)
     reach = min(slot_size - 1, -(-(longest_item - 1) // rows))
+    ids_t, mask_t = jnp.transpose(byte_ids, (0, 2, 1)), jnp.transpose(loss_mask, (0, 2, 1))
     micros = []
     for micro in range(byte_ids.shape[0]):
         forward = micro % 2 == 0
-        chunk = slot_index if forward else slot_size - 1 - slot_index
-        group_ids = byte_ids[micro]
-        items = item_ids[micro, 0]
-        begin = chunk * rows
-        previous = jnp.concatenate([jnp.full((1, SLOTS), -1, jnp.int32), group_ids[:-1]], axis=0)
-        earlier_item = jnp.concatenate([items[:1], items[:-1]])
-        previous = jnp.where((items == earlier_item)[:, None], previous, -1)
-        own_previous = lax.dynamic_slice_in_dim(previous, begin, rows, 0)
-        own_items = lax.dynamic_slice_in_dim(items, begin, rows, 0)
-        first = jnp.sum((items[None, :] < own_items[:, None]).astype(jnp.int32), axis=1)
-        first = jnp.maximum(first - (chunk - reach) * rows, 0)
-        start_rows, hidden, projected, own_kv = embed_rows(
-            own_previous, table, full_in_flat, gain_global[None]
+        start_rows, hidden, projected, own_kv, own_previous = embed_rows(
+            ids_t, item_ids, micro, forward, rows, table, full_in_flat, gain_global[None]
         )
         earlier = [shift_chunks(own_kv, d, forward) for d in range(1, reach + 1)]
-        expanded = product(hidden, full_expand)
-        active = gelu_tanh(expanded).astype(BF16)
-        begin_local = begin + mp_index * local_rows
-        micros.append(dict(
-            forward=forward, group_ids=group_ids, begin_local=begin_local, start_rows=start_rows,
-            hidden=hidden, projected=projected, earlier=earlier,
-            expanded=expanded, active=active, low=first[::BLK] // BLK,
-            first=first.reshape(-1, 1, BLK), own_previous=own_previous, mask=loss_mask[micro],
+        micros.append(types.SimpleNamespace(
+            forward=forward, micro=micro, start_rows=start_rows, hidden=hidden, projected=projected,
+            earlier=earlier, own_previous=own_previous,
         ))
+    for m, pair in zip(micros, up_rows([m.hidden for m in micros], full_expand)):
+        m.active, m.slope = pair
     for m in micros:
-        m["attended"], m["lse"] = attention_fwd(m["low"], m["first"], m["projected"], m["earlier"])
-        m["own"], m["pieces"] = trade_rows(
-            product(m["attended"], full_out) + product(m["active"], full_shrink), "mp"
+        m.attended, m.lse = attention_fwd(
+            item_ids, m.micro, m.forward, m.projected, m.earlier
         )
-        m["own_start"] = lax.dynamic_slice_in_dim(
-            m["start_rows"], mp_index * local_rows, local_rows, 0
+        m.own, m.pieces = trade_rows(
+            product(m.attended, full_out) + product(m.active, full_shrink), STACK
+        )
+        m.own_start = lax.dynamic_slice_in_dim(
+            m.start_rows, mp_index * local_rows, local_rows, 0
         )
     base = None
     for m in micros:
-        ids = lax.dynamic_slice_in_dim(m["group_ids"], m["begin_local"], local_rows, 0)
-        mask = lax.dynamic_slice_in_dim(m["mask"], m["begin_local"], local_rows, 0)
         out = byte_layer(
-            m["own_start"], m["own"], m["pieces"], ids, mask, mask_count.reshape(1, 1),
-            unpacked[:7], local_gains, base,
+            m.own_start, m.own, m.pieces, ids_t, mask_t, m.micro, m.forward, rows,
+            mask_count.reshape(1, 1), unpacked[:7], local_gains, base,
         )
         base = out[:9]
-        m["own_back"] = out[9]
-        m["branch_pieces"] = share_rows(out[9], "mp")
+        m.own_back = out[9]
+        m.branch_pieces = share_rows(out[9], STACK)
     matrices, local_gain_grads, loss_sum = base[:7], base[7], base[8][0, 0]
+    local_blocks = pack(matrices, local_pack.shape[0])
     sums = None
     table_grad = None
     gain_global_grad = None
     for m in micros:
-        branch_grad, m["query_grad"], m["kv_grads"] = attention_bwd(
-            m["low"], m["first"], m["projected"], m["earlier"], m["attended"], m["lse"],
-            full_out, m["branch_pieces"],
+        branch_grad, m.query_grad, m.kv_grads = attention_bwd(
+            item_ids, m.micro, m.forward, m.projected, m.earlier, m.attended, m.lse,
+            full_out, m.branch_pieces,
         )
-        m["branch_grad"] = branch_grad
-        m["returned"] = [
-            shift_chunks(m["kv_grads"][d], d, not m["forward"]) for d in range(1, reach + 1)
+        m.branch_grad = branch_grad
+        m.returned = [
+            shift_chunks(m.kv_grads[d], d, not m.forward) for d in range(1, reach + 1)
         ]
-        m["expanded_grad"] = gelu_back(
-            m["expanded"], back_product(branch_grad, full_shrink)
+        m.expanded_grad = (
+            m.slope.astype(F32) * back_product(branch_grad, full_shrink)
         ).astype(BF16)
     for m in micros:
-        kv_total = m["kv_grads"][0].astype(F32)
-        for value in m["returned"]:
+        kv_total = m.kv_grads[0].astype(F32)
+        for value in m.returned:
             kv_total = kv_total + value.astype(F32)
-        m["projected_grad"] = jnp.concatenate([m["query_grad"], kv_total.astype(BF16)], axis=1)
-        m["partial"] = back_product(m["projected_grad"], full_in_flat) + back_product(
-            m["expanded_grad"], full_expand
+        m.projected_grad = jnp.concatenate([m.query_grad, kv_total.astype(BF16)], axis=1)
+        m.partial = back_product(m.projected_grad, full_in_flat) + back_product(
+            m.expanded_grad, full_expand
         )
-        m["back"] = trade_rows(m["partial"], "mp")
+        m.back = trade_rows(m.partial, STACK)
     sums = None
     for m in micros:
         terms = (
-            gram_product(m["hidden"], m["projected_grad"]),
-            gram_product(m["hidden"], m["expanded_grad"]),
-            gram_product(m["attended"], m["branch_grad"]),
-            gram_product(m["active"], m["branch_grad"]),
+            gram_product(m.hidden, m.projected_grad),
+            gram_product(m.hidden, m.expanded_grad),
+            gram_product(m.attended, m.branch_grad),
+            gram_product(m.active, m.branch_grad),
         )
         sums = terms if sums is None else tuple(a + b for a, b in zip(sums, terms))
     sums = tuple(s.astype(BF16) for s in sums)
     if wide:
-        sums, _ = lax.optimization_barrier((sums, [m["back"][0] for m in micros]))
+        sums, _ = lax.optimization_barrier((sums, [m.back[0] for m in micros]))
         own_in, own_expand, own_out, own_shrink = scatter_grads(sums, (False, False, True, True))
     else:
         own_in, own_expand = scatter_grads(sums[:2], (False, False))
         own_out, own_shrink = (
-            lax.psum_scatter(v, ("slot", "dp"), scatter_dimension=1, tiled=True).astype(F32)
+            lax.psum_scatter(v, (SLOT, CORE), scatter_dimension=1, tiled=True).astype(F32)
             for v in sums[2:]
         )
-    backs, own_in = lax.optimization_barrier(([m["back"] for m in micros], own_in))
+    backs, own_in = lax.optimization_barrier(([m.back for m in micros], own_in))
     table_grad = None
     for m, (hidden_grad, pieces) in zip(micros, backs):
         for value in pieces:
             hidden_grad = hidden_grad + value.astype(F32)
-        _, scaled, factor = norm_forward(m["own_start"].astype(F32), gain_global)
+        _, scaled, factor = norm_forward(m.own_start.astype(F32), gain_global)
         gain_term = jnp.sum(hidden_grad * scaled, axis=0)
         start_grad = (
-            m["own_back"].astype(F32) + norm_backward(scaled, factor, gain_global, hidden_grad)
+            m.own_back.astype(F32) + norm_backward(scaled, factor, gain_global, hidden_grad)
         ).astype(BF16)
-        own_lookup = lax.dynamic_slice_in_dim(m["own_previous"], mp_index * local_rows, local_rows, 0)
+        own_lookup = lax.dynamic_slice_in_dim(m.own_previous, mp_index * local_rows, local_rows, 0)
         own_lookup = (own_lookup[:, :, None] == vocab_ids).astype(BF16)
         table_term = jnp.einsum(
             "pjv,pjg->jvg", own_lookup, start_grad.reshape(local_rows, SLOTS, GSLOT),
@@ -1257,7 +1306,7 @@
             table_grad = table_grad + table_term
             gain_global_grad = gain_global_grad + gain_term
     gain_grads = jnp.concatenate([gain_global_grad, local_gain_grads.reshape(-1)])
-    parts = slot_size * lax.axis_size("dp")
+    parts = slot_size * lax.axis_size(CORE)
     small = jnp.concatenate(
         [
             table_grad.astype(BF16).reshape(parts, -1, GSLOT),
@@ -1265,21 +1314,30 @@
         ],
         axis=1,
     ).reshape(-1, GSLOT)
+    squares = jnp.float32(0.0)
+    for gradient in (own_in, own_expand, own_out, own_shrink):
+        squares = squares + jnp.sum(gradient * gradient)
+    small, squares = lax.optimization_barrier((small, squares))
     own_small = scatter_grads([small], (False,), True)[0]
-    own_in = own_in.reshape(attend_in.shape)
-    own_small = own_small.reshape(lax.axis_size("dp"), piece + 16, GSLOT)
+    own_small = own_small.reshape(lax.axis_size(CORE), piece + 16, GSLOT)
     own_table = own_small[:, :piece].reshape(slot_table.shape)
     gain_total = own_small[0, piece:].reshape(-1)
-    own_pack = scatter_pack(pack(matrices, local_pack.shape[0]), local_pack.shape[0])
     last = (slot_index == slot_size - 1) & (mp_index == mp_size - 1)
-    last = last & (dp_index == lax.axis_size("dp") - 1)
+    last = last & (dp_index == lax.axis_size(CORE) - 1)
+    owner = ((mp_index == 0) & (dp_index == 0)).astype(F32)
+    squares = squares + owner * jnp.sum(own_table * own_table)
+    squares = squares + jnp.where(last, jnp.sum(gain_total * gain_total), 0.0)
+    own_in = jnp.stack([own_in[:, i * width : (i + 1) * width] for i in range(3)])
+    own_block = lax.psum_scatter(local_blocks, (SLOT, STACK, CORE), scatter_dimension=0, tiled=True)
+    pack_share, tail_size = local_pack.shape[0], D + 2 * LD
+    offset = lax.rem(lax.axis_index((SLOT, STACK, CORE)) * pack_share, 128)
+    index = jnp.arange(own_block.shape[0])[:, None] * 128 + jnp.arange(128)[None, :] - offset
+    inside = (index >= 0) & (index < jnp.where(last, pack_share - tail_size, pack_share))
+    squares = squares + jnp.sum(jnp.where(inside, own_block.astype(F32) ** 2, 0.0))
+    own_pack = lax.dynamic_slice_in_dim(own_block.reshape(-1), offset, pack_share, 0).astype(F32)
     own_pack = jnp.concatenate(
-        [own_pack[: -gain_total.shape[0]], jnp.where(last, gain_total, own_pack[-gain_total.shape[0] :])]
+        [own_pack[:-tail_size], jnp.where(last, gain_total, own_pack[-tail_size:])]
     )
-    owner = ((mp_index == 0) & (dp_index == 0)).astype(F32)
-    squares = jnp.sum(own_pack * own_pack) + owner * jnp.sum(own_table * own_table)
-    for gradient in (own_in, own_expand, own_out, own_shrink):
-        squares = squares + jnp.sum(gradient * gradient)
     both = total_of(jnp.stack([jnp.full((8, 128), squares), jnp.full((8, 128), loss_sum)]))
     total_squares, loss_value = both[0, 0, 0], both[1, 0, 0]
     clip_norm = jnp.sqrt(total_squares)
@@ -1293,33 +1351,38 @@
         (slot_table, moment_slot_table, average_slot_table, own_table, rate_table),
         (local_pack, moment_local_pack, average_local_pack, own_pack, rate_dense),
     ):
-        results.extend(update(weight, moment, average, gradient, factor, rate))
+        if gradient is own_in:
+            weight, moment, average = (jnp.transpose(v, (1, 0, 2)) for v in (weight, moment, average))
+        changed = update(weight, moment, average, gradient, factor, rate)
+        if gradient is own_in:
+            changed = tuple(jnp.transpose(v, (1, 0, 2)) for v in changed)
+        results.extend(changed)
     return tuple(results)
 
 
 def solution(mesh):
     placed = (
-        P(None, "dp", None),
-        P(None, "dp", None),
-        P(None, "dp", None),
-        P(("slot", "dp"), None, "mp"),
-        P(("slot", "dp"), "mp"),
-        P("mp", ("slot", "dp")),
-        P("mp", ("slot", "dp")),
-        P("slot", None, None),
-        P(("slot", "mp", "dp")),
-        P(("slot", "dp"), None, "mp"),
-        P(("slot", "dp"), "mp"),
-        P("mp", ("slot", "dp")),
-        P("mp", ("slot", "dp")),
-        P("slot", None, None),
-        P(("slot", "mp", "dp")),
-        P(("slot", "dp"), None, "mp"),
-        P(("slot", "dp"), "mp"),
-        P("mp", ("slot", "dp")),
-        P("mp", ("slot", "dp")),
-        P("slot", None, None),
-        P(("slot", "mp", "dp")),
+        P(None, CORE, None),
+        P(None, CORE, None),
+        P(None, CORE, None),
+        P((SLOT, CORE), None, STACK),
+        P((SLOT, CORE), STACK),
+        P(STACK, (SLOT, CORE)),
+        P(STACK, (SLOT, CORE)),
+        P(SLOT, None, None),
+        P((SLOT, STACK, CORE)),
+        P((SLOT, CORE), None, STACK),
+        P((SLOT, CORE), STACK),
+        P(STACK, (SLOT, CORE)),
+        P(STACK, (SLOT, CORE)),
+        P(SLOT, None, None),
+        P((SLOT, STACK, CORE)),
+        P((SLOT, CORE), None, STACK),
+        P((SLOT, CORE), STACK),
+        P(STACK, (SLOT, CORE)),
+        P(STACK, (SLOT, CORE)),
+        P(SLOT, None, None),
+        P((SLOT, STACK, CORE)),
     )
     return jax.shard_map(
         local,
@@ -1329,24 +1392,24 @@
             P(),
             P(),
             P(),
-            P(("slot", "dp"), None, "mp"),
-            P(("slot", "dp"), None, "mp"),
-            P(("slot", "dp"), None, "mp"),
-            P(("slot", "dp"), "mp"),
-            P(("slot", "dp"), "mp"),
-            P(("slot", "dp"), "mp"),
-            P("mp", ("slot", "dp")),
-            P("mp", ("slot", "dp")),
-            P("mp", ("slot", "dp")),
-            P("mp", ("slot", "dp")),
-            P("mp", ("slot", "dp")),
-            P("mp", ("slot", "dp")),
-            P("slot", None, None),
-            P("slot", None, None),
-            P("slot", None, None),
-            P(("slot", "mp", "dp")),
-            P(("slot", "mp", "dp")),
-            P(("slot", "mp", "dp")),
+            P((SLOT, CORE), None, STACK),
+            P((SLOT, CORE), None, STACK),
+            P((SLOT, CORE), None, STACK),
+            P((SLOT, CORE), STACK),
+            P((SLOT, CORE), STACK),
+            P((SLOT, CORE), STACK),
+            P(STACK, (SLOT, CORE)),
+            P(STACK, (SLOT, CORE)),
+            P(STACK, (SLOT, CORE)),
+            P(STACK, (SLOT, CORE)),
+            P(STACK, (SLOT, CORE)),
+            P(STACK, (SLOT, CORE)),
+            P(SLOT, None, None),
+            P(SLOT, None, None),
+            P(SLOT, None, None),
+            P((SLOT, STACK, CORE)),
+            P((SLOT, STACK, CORE)),
+            P((SLOT, STACK, CORE)),
         ),
         check_vma=False,
     )

time: 501 us -> 479 us (0.956)
  local copies, waits for them, and re-layouts: 70.8 us -> 41.1 us
  Pallas kernels: 258 us -> 272 us
  waiting for transfers between devices: 19.9 us -> 30.8 us
  matrix products: 32.6 us -> 24.5 us
    unnamed x184 -> x146, local copies, waits for them, and re-layouts: 49.7 us -> 25.7 us
    ppermute x8, waiting for transfers between devices: 0.02 us -> 12.6 us  [shift_chunks(): return lax.ppermute(value, SLOT, pairs)]
    pallas_call x1, Pallas kernels: 40.7 us -> 46.6 us  [gather_weights(): pl.pallas_call(functools.partial(gather_kernel, sizes, columns, forwarded...]
    dot_general x6 -> x4, matrix products: 12.4 us -> 6.82 us  [product(): return jnp.dot(left, right, preferred_element_type=jnp.float32)]
    dynamic_slice x13 -> x4, local copies, waits for them, and re-layouts: 6.74 us -> 1.36 us  [local(): lax.dynamic_slice_in_dim(m.own_previous, mp_index * local_rows, local_row...]
    pallas_call x4 -> x5, Pallas kernels: 21.3 us -> 26.4 us  [the longest x2 14.9 us: attention_fwd(): pl.pallas_call(functools.partial(fwd_kernel, rows, width, count, micro, f...]
  transfers between devices with their start and end apart: 28 -> 28, of which waited for: 3 -> 4; matrix products, arithmetic and copies ran while one was open for 14% -> 10% of each run, Pallas kernels for 42% -> 55%
where the time goes in v3:
time: 479 us; the launch traced here: 475 us
  Pallas kernels  272 us (57%)
  starting transfers between devices  54 us (11%)
  local copies, waits for them, and re-layouts  41.1 us (9%)
  waiting for transfers between devices  30.8 us (6%)
  other arithmetic  28.4 us (6%)
  matrix products  24.5 us (5%)
  between operations  24.2 us (5%)
    pallas_call x2, Pallas kernels, byte_layer(): pl.pallas_call(functools.partial(byte_kernel, rows, tile, base is not Non...  91.3 us
    pallas_call x2, Pallas kernels, scatter_grads(): pl.pallas_call(functools.partial(scatter_kernel, sizes, columns, extents,...  61.7 us
    pallas_call x1, Pallas kernels, gather_weights(): pl.pallas_call(functools.partial(gather_kernel, sizes, columns, forwarded...  46.6 us
    ppermute x8, starting transfers between devices, shift_chunks(): return lax.ppermute(value, SLOT, pairs)  27 us
    ppermute x18, starting transfers between devices, swap(): return lax.ppermute(value, axis, pairs)  27 us
    unnamed x146, local copies, waits for them, and re-layouts  25.7 us
    pallas_call x2, Pallas kernels, attention_bwd(): pl.pallas_call(functools.partial(bwd_kernel, rows, width, count, len(piec...  18.7 us
    ppermute x18, waiting for transfers between devices, swap(): return lax.ppermute(value, axis, pairs)  18.2 us
  transfers between devices with their start and end apart: 28, of which 4 were waited for; matrix products, arithmetic and copies ran while one was open for 10% of the time, Pallas kernels for 55%

profile of v3, /device:TPU:0, one launch (start us, length us, event | category | flops | bytes accessed | tf_op | source)
XLA Modules:
  0.0 475.2 jit_solution(344933890639520166)
XLA Ops:
  15.3 46.6 %gather_weights.1 = (bf16[2048,128]{1,0:T(8,128)(2,1)S(1)}, bf16[1024,768]{1,0:T(8,128)(2,1)S(1)}, bf16[1024,1024]{1,0:T(8,128)(2,1)S(1)}, bf16[256,1024]{1,0:T(...) custom-call(f32[256,128]{1,0:T(8,128)S(1)} %constant_dynamic-slice_fusion.8.refs_0_, ...), custom_call_target="tpu_custom_call" | custom-call | flops 1000000 | bytes 120000000 | tf_op jit(solution)/shard_map/gather_weights/pallas_call | solution.py:809
  65.2 3.5 embed_rows.3
  73.4 3.6 embed_rows.2
  78.8 6.8 %collective-permute-start.1 = (bf16[512,512]{1,0:T(8,128)(2,1)}, bf16[512,512]{1,0:T(8,128)(2,1)}, u32[]{:S(2)}, u32[]{:S(2)}) collective-permute-start(bf16[512,512]{1,0:T(8,128)(2,1)} %get-tuple-element.108), channel_id=1, source_target_pairs={{0,16},{8,24},{1,17},{9,25},{2,18},{10,26},{3,19},{11,27},{4,20},{... | collective-permute-start | bytes 1572872 | tf_op jit(solution)/shard_map/ppermute | solution.py:1139
  85.6 5.6 %collective-permute-start = (bf16[512,512]{1,0:T(8,128)(2,1)}, bf16[512,512]{1,0:T(8,128)(2,1)}, u32[]{:S(2)}, u32[]{:S(2)}) collective-permute-start(bf16[512,512]{1,0:T(8,128)(2,1)} %get-tuple-element.108), channel_id=1, source_target_pairs={{0,8},{8,16},{16,24},{1,9},{9,17},{17,25},{2,10},{10,18},{18,26},{... | collective-permute-start | bytes 1572872 | tf_op jit(solution)/shard_map/ppermute | solution.py:1139
  97.3 4.3 up_rows.1
  101.7 2.6 fusion.43
  107.5 3.2 fusion.45
  110.7 5.4 %patch_attention.2 = (bf16[512,256]{1,0:T(8,128)(2,1)S(1)}, f32[4,1,512]{2,1,0:T(1,128)S(1)}) custom-call(s32[2,1,2048]{2,1,0:T(1,128)S(1)} %copy-done.41, bf16[512,768]{1,0:T(8,128)(2,1)S(1)} %copy-done.50, bf16[512,512]{1,0:T(8,128)(2,1)} %collective-permute-done.rest_0_, bf16[512,512]{1,0:T(8,128)(2,1)} %collective-permute-done.1.rest_1_), custom_call_target="tpu_custom_call" | custom-call | flops 6000000000 | bytes 20000000 | tf_op jit(solution)/shard_map/patch_attention/pallas_call | solution.py:266
  117.8 3.5 collective-permute-start.4
  122.2 9.5 %patch_attention.3 = (bf16[512,256]{1,0:T(8,128)(2,1)S(1)}, f32[4,1,512]{2,1,0:T(1,128)S(1)}) custom-call(s32[2,1,2048]{2,1,0:T(1,128)S(1)} %copy-done.41, bf16[512,768]{1,0:T(8,128)(2,1)S(1)} %copy-done.47, bf16[512,512]{1,0:T(8,128)(2,1)} %collective-permute-done.13.rest_0_, bf16[512,512]{1,0:T(8,128)(2,1)} %collective-permute-done.14.rest_1_), custom_call_target="tpu_custom_call" | custom-call | flops 6000000000 | bytes 20000000 | tf_op jit(solution)/shard_map/patch_attention/pallas_call | solution.py:266
  133.1 3.5 collective-permute-start.17
  138.3 7.9 %unpack.1 = (bf16[512,1536]{1,0:T(8,128)(2,1)S(1)}, bf16[512,2048]{1,0:T(8,128)(2,1)S(1)}, bf16[512,512]{1,0:T(8,128)(2,1)S(1)}, bf16[2048,512]{1,0:T(8,128)(2,1...) custom-call(bf16[27648,128]{1,0:T(8,128)(2,1)} %all-gather.2.cloned.1.call-done.blocks_ref), custom_call_target="tpu_custom_call" | custom-call | tf_op jit(solution)/shard_map/unpack/pallas_call | solution.py:1049
  152.4 3.4 collective-permute-done.3.rest_1_
  155.8 44.3 %byte_layer.2 = (bf16[512,1536]{1,0:T(8,128)(2,1)}, bf16[512,2048]{1,0:T(8,128)(2,1)}, bf16[512,512]{1,0:T(8,128)(2,1)}, bf16[2048,512]{1,0:T(8,128)(2,1)}, bf16...) custom-call(bf16[128,1024]{1,0:T(8,128)(2,1)} %get-tuple-element.209, ...), custom_call_target="tpu_custom_call" | custom-call | flops 43000000512 | bytes 150000000 | tf_op jit(solution)/shard_map/byte_layer/pallas_call | solution.py:619
  200.1 3.2 collective-permute-start.7
  204.5 47.0 %byte_layer.3 = (bf16[512,1536]{1,0:T(8,128)(2,1)}, bf16[512,2048]{1,0:T(8,128)(2,1)}, bf16[512,512]{1,0:T(8,128)(2,1)}, bf16[2048,512]{1,0:T(8,128)(2,1)}, bf16...) custom-call(bf16[128,1024]{1,0:T(8,128)(2,1)} %get-tuple-element.211, ...), custom_call_target="tpu_custom_call" | custom-call | flops 43000000512 | bytes 150000000 | tf_op jit(solution)/shard_map/byte_layer/pallas_call | solution.py:619
  251.4 3.3 collective-permute-start.20
  262.3 8.4 %pack.1 = bf16[27648,128]{1,0:T(8,128)(2,1)} custom-call(bf16[512,1536]{1,0:T(8,128)(2,1)S(1)} %copy-done.9, bf16[512,2048]{1,0:T(8,128)(2,1)S(1)} %copy-done.6, bf16[512,512]{1,0:T(8,128)(2,1)S(1)} %copy-done.18, bf16[2048,512]{1,0:T(8,128)(2,1)} %get-tuple-element.178.refs_3_, bf16[512,256]{1,0:T(8,128)(2,1)S(1)} %copy-done.23, ...), custom_call_target="tpu_custom_call" | custom-call | tf_op jit(solution)/shard_map/pack/pallas_call | solution.py:1090
  274.0 6.9 %patch_attention_back.2 = (bf16[512,1024]{1,0:T(8,128)(2,1)S(1)}, bf16[512,256]{1,0:T(8,128)(2,1)S(1)}, bf16[512,512]{1,0:T(8,128)(2,1)S(1)}, bf16[512,512]{1,0:T(8,128)(2,1)S(1)}, bf16[512,512]{1,0:T(8,128)(2,1)S(1)}) custom-call(s32[2,1,2048]{2,1,0:T(1,128)S(1)} %copy-done.41, bf16[512,768]{1,0:T(8,128)(2,1)S(1)} %copy-done.51, ...), custom_call_target="tpu_custom_call" | custom-call | flops 8000000000 | bytes 25000000 | tf_op jit(solution)/shard_map/patch_attention_back/pallas_call | solution.py:285
  283.6 11.8 %patch_attention_back.3 = (bf16[512,1024]{1,0:T(8,128)(2,1)S(1)}, bf16[512,256]{1,0:T(8,128)(2,1)S(1)}, bf16[512,512]{1,0:T(8,128)(2,1)S(1)}, bf16[512,512]{1,0:T(8,128)(2,1)S(1)}, bf16[512,512]{1,0:T(8,128)(2,1)S(1)}) custom-call(s32[2,1,2048]{2,1,0:T(1,128)S(1)} %copy-done.41, bf16[512,768]{1,0:T(8,128)(2,1)S(1)} %copy-done.48, ...), custom_call_target="tpu_custom_call" | custom-call | flops 8000000000 | bytes 25000000 | tf_op jit(solution)/shard_map/patch_attention_back/pallas_call | solution.py:285
  295.4 8.1 %collective-permute-start.21 = (bf16[512,512]{1,0:T(8,128)(2,1)S(1)}, bf16[512,512]{1,0:T(8,128)(2,1)S(1)}, u32[]{:S(2)}, u32[]{:S(2)}) collective-permute-start(bf16[512,512]{1,0:T(8,128)(2,1)S(1)} %get-tuple-element.150), channel_id=1, source_target_pairs={{0,8},{8,16},{16,24},{1,9},{9,17},{17,25},{2,10},{10,18},{18,26},{... | collective-permute-start | bytes 1572872 | tf_op jit(solution)/shard_map/ppermute | solution.py:1139
  313.5 2.8 add_convert_fusion.refs_3_
  318.0 12.6 %collective-permute-done.22 = bf16[512,512]{1,0:T(8,128)(2,1)S(1)} collective-permute-done((bf16[512,512]{1,0:T(8,128)(2,1)S(1)}, bf16[512,512]{1,0:T(8,128)(2,1)S(1)}, u32[]{:S(2)}, u32[]{:S(2)}) %collective-permute-start.22) | collective-permute-done | bytes 524320 | tf_op jit(solution)/shard_map/ppermute | solution.py:1139
  332.0 2.5 collective-permute-start.25
  337.8 2.5 collective-permute-start.12
  343.5 42.4 %scatter_grads.1 = (f32[128,768]{1,0:T(8,128)S(1)}, f32[128,1024]{1,0:T(8,128)S(1)}, f32[256,128]{1,0:T(8,128)S(1)}, f32[1024,128]{1,0:T(8,128)S(1)}) custom-call(bf16[1024,768]{1,0:T(8,128)(2,1)S(1)} %add_convert_fusion.2.refs_0_, bf16[1024,1024]{1,0:T(8,128)(2,1)S(1)} %add_convert_fusion.1.refs_1_, bf16[256,1024]{1,0:T(8,128)(2,1)S(1)} %fusion.refs_2_, ...), custom_call_target="tpu_custom_call" | custom-call | flops 1000000 | bytes 120000000 | tf_op jit(solution)/shard_map/scatter_grads/pallas_call | solution.py:933
  390.4 7.0 %collective-permute-done.11 = bf16[128,1024]{1,0:T(8,128)(2,1)} collective-permute-done((bf16[128,1024]{1,0:T(8,128)(2,1)S(1)}, bf16[128,1024]{1,0:T(8,128)(2,1)}, u32[]{:S(2)}, u32[]{:S(2)}) %collective-permute-start.11) | collective-permute-done | bytes 262176 | tf_op jit(solution)/shard_map/ppermute | solution.py:1111
  397.4 7.7 %collective-permute-done.10 = bf16[128,1024]{1,0:T(8,128)(2,1)S(1)} collective-permute-done((bf16[128,1024]{1,0:T(8,128)(2,1)S(1)}, bf16[128,1024]{1,0:T(8,128)(2,1)S(1)}, u32[]{:S(2)}, u32[]{:S(2)}) %collective-permute-start.10) | collective-permute-done | bytes 262176 | tf_op jit(solution)/shard_map/ppermute | solution.py:1111
  412.7 19.3 %scatter_small.1 = f32[544,128]{1,0:T(8,128)S(1)} custom-call(bf16[2176,128]{1,0:T(8,128)(2,1)S(1)} %bitcast.92), custom_call_target="tpu_custom_call" | custom-call | flops 1000000 | bytes 10000000 | tf_op jit(solution)/shard_map/scatter_small/pallas_call | solution.py:933
  440.3 11.3 %total_of.1 = f32[2,8,128]{2,1,0:T(8,128)} custom-call(f32[2,8,128]{2,1,0:T(8,128)} %stack.18.value), custom_call_target="tpu_custom_call" | custom-call | tf_op jit(solution)/shard_map/total_of/pallas_call | solution.py:992
  458.5 2.6 multiply_add_fusion.2
  (265 shorter events, 98.0 us)
Async XLA Ops:
  7.3 131.0 %all-gather.2.cloned.1.call-start = ((), (), s32[]{:S(2)}) async-start(), calls=%async_computation.1 | async-start | bytes 7299072 | tf_op jit(solution)/shard_map/all_gather | solution.py:1162
  11.3 424.0 %reduce-scatter.2.cloned.1.call-start = ((), (), s32[]{:S(2)}) async-start(), calls=%async_computation.2 | async-start | bytes 7299072 | tf_op jit(solution)/shard_map/reduce_scatter | solution.py:1331
  70.8 51.4 %collective-permute-start.14 = (bf16[512,512]{1,0:T(8,128)(2,1)}, bf16[512,512]{1,0:T(8,128)(2,1)}, u32[]{:S(2)}, u32[]{:S(2)}) collective-permute-start(bf16[512,512]{1,0:T(8,128)(2,1)} %get-tuple-element.133), channel_id=1, source_target_pairs={{16,0},{24,8},{17,1},{25,9},{18,2},{26,10},{19,3},{27,11},{20,4},{... | collective-permute-start | bytes 1572872 | tf_op jit(solution)/shard_map/ppermute | solution.py:1139
  72.0 50.1 %collective-permute-start.13 = (bf16[512,512]{1,0:T(8,128)(2,1)}, bf16[512,512]{1,0:T(8,128)(2,1)}, u32[]{:S(2)}, u32[]{:S(2)}) collective-permute-start(bf16[512,512]{1,0:T(8,128)(2,1)} %get-tuple-element.133), channel_id=1, source_target_pairs={{8,0},{16,8},{24,16},{9,1},{17,9},{25,17},{10,2},{18,10},{26,18},{... | collective-permute-start | bytes 1572872 | tf_op jit(solution)/shard_map/ppermute | solution.py:1139
  78.8 31.9 %collective-permute-start.1 = (bf16[512,512]{1,0:T(8,128)(2,1)}, bf16[512,512]{1,0:T(8,128)(2,1)}, u32[]{:S(2)}, u32[]{:S(2)}) collective-permute-start(bf16[512,512]{1,0:T(8,128)(2,1)} %get-tuple-element.108), channel_id=1, source_target_pairs={{0,16},{8,24},{1,17},{9,25},{2,18},{10,26},{3,19},{11,27},{4,20},{... | collective-permute-start | bytes 1572872 | tf_op jit(solution)/shard_map/ppermute | solution.py:1139
  85.6 25.1 %collective-permute-start = (bf16[512,512]{1,0:T(8,128)(2,1)}, bf16[512,512]{1,0:T(8,128)(2,1)}, u32[]{:S(2)}, u32[]{:S(2)}) collective-permute-start(bf16[512,512]{1,0:T(8,128)(2,1)} %get-tuple-element.108), channel_id=1, source_target_pairs={{0,8},{8,16},{16,24},{1,9},{9,17},{17,25},{2,10},{10,18},{18,26},{... | collective-permute-start | bytes 1572872 | tf_op jit(solution)/shard_map/ppermute | solution.py:1139
  117.8 33.7 %collective-permute-start.4 = (bf16[128,1024]{1,0:T(8,128)(2,1)}, bf16[128,1024]{1,0:T(8,128)(2,1)}, u32[]{:S(2)}, u32[]{:S(2)}) collective-permute-start(bf16[128,1024]{1,0:T(8,128)(2,1)} %get-tuple-element.218), channel_id=1, source_target_pairs={{0,6},{2,4},{4,2},{6,0},{1,7},{3,5},{5,3},{7,1},{8,14},{10,12},{12... | collective-permute-start | bytes 786440 | tf_op jit(solution)/shard_map/ppermute | solution.py:1111
  121.3 34.5 %collective-permute-start.3 = (bf16[128,1024]{1,0:T(8,128)(2,1)}, bf16[128,1024]{1,0:T(8,128)(2,1)}, u32[]{:S(2)}, u32[]{:S(2)}) collective-permute-start(bf16[128,1024]{1,0:T(8,128)(2,1)} %get-tuple-element.219), channel_id=1, source_target_pairs={{0,4},{2,6},{4,0},{6,2},{1,5},{3,7},{5,1},{7,3},{8,12},{10,14},{12... | collective-permute-start | bytes 786440 | tf_op jit(solution)/shard_map/ppermute | solution.py:1111
  121.3 34.5 %collective-permute-start.2 = (bf16[128,1024]{1,0:T(8,128)(2,1)S(1)}, bf16[128,1024]{1,0:T(8,128)(2,1)}, u32[]{:S(2)}, u32[]{:S(2)}) collective-permute-start(bf16[128,1024]{1,0:T(8,128)(2,1)S(1)} %get-tuple-element.220), channel_id=1, source_target_pairs={{0,2},{2,0},{4,6},{6,4},{1,3},{3,1},{5,7},{7,5},{8,10},{10,8},{12,... | collective-permute-start | bytes 786440 | tf_op jit(solution)/shard_map/ppermute | solution.py:1111
  133.1 70.2 %collective-permute-start.17 = (bf16[128,1024]{1,0:T(8,128)(2,1)}, bf16[128,1024]{1,0:T(8,128)(2,1)}, u32[]{:S(2)}, u32[]{:S(2)}) collective-permute-start(bf16[128,1024]{1,0:T(8,128)(2,1)} %get-tuple-element.221), channel_id=1, source_target_pairs={{0,6},{2,4},{4,2},{6,0},{1,7},{3,5},{5,3},{7,1},{8,14},{10,12},{12... | collective-permute-start | bytes 786440 | tf_op jit(solution)/shard_map/ppermute | solution.py:1111
  136.6 67.9 %collective-permute-start.16 = (bf16[128,1024]{1,0:T(8,128)(2,1)}, bf16[128,1024]{1,0:T(8,128)(2,1)}, u32[]{:S(2)}, u32[]{:S(2)}) collective-permute-start(bf16[128,1024]{1,0:T(8,128)(2,1)} %get-tuple-element.222), channel_id=1, source_target_pairs={{0,4},{2,6},{4,0},{6,2},{1,5},{3,7},{5,1},{7,3},{8,12},{10,14},{12... | collective-permute-start | bytes 786440 | tf_op jit(solution)/shard_map/ppermute | solution.py:1111
  151.4 53.0 %collective-permute-start.15 = (bf16[128,1024]{1,0:T(8,128)(2,1)}, bf16[128,1024]{1,0:T(8,128)(2,1)}, u32[]{:S(2)}, u32[]{:S(2)}) collective-permute-start(bf16[128,1024]{1,0:T(8,128)(2,1)} %get-tuple-element.223), channel_id=1, source_target_pairs={{0,2},{2,0},{4,6},{6,4},{1,3},{3,1},{5,7},{7,5},{8,10},{10,8},{12,... | collective-permute-start | bytes 786440 | tf_op jit(solution)/shard_map/ppermute | solution.py:1111
  200.1 70.6 %collective-permute-start.7 = (bf16[128,1024]{1,0:T(8,128)(2,1)}, bf16[128,1024]{1,0:T(8,128)(2,1)}, u32[]{:S(2)}, u32[]{:S(2)}) collective-permute-start(bf16[128,1024]{1,0:T(8,128)(2,1)} %get-tuple-element.124.rest_5_), channel_id=1, source_target_pairs={{0,6},{2,4},{4,2},{6,0},{1,7},{3,5},{5,3},{7,1},{8,14},{10,12},{12... | collective-permute-start | bytes 786440 | tf_op jit(solution)/shard_map/ppermute | solution.py:1111
  203.3 68.7 %collective-permute-start.6 = (bf16[128,1024]{1,0:T(8,128)(2,1)}, bf16[128,1024]{1,0:T(8,128)(2,1)}, u32[]{:S(2)}, u32[]{:S(2)}) collective-permute-start(bf16[128,1024]{1,0:T(8,128)(2,1)} %get-tuple-element.124.rest_5_), channel_id=1, source_target_pairs={{0,4},{2,6},{4,0},{6,2},{1,5},{3,7},{5,1},{7,3},{8,12},{10,14},{12... | collective-permute-start | bytes 786440 | tf_op jit(solution)/shard_map/ppermute | solution.py:1111
  203.3 68.7 %collective-permute-start.5 = (bf16[128,1024]{1,0:T(8,128)(2,1)}, bf16[128,1024]{1,0:T(8,128)(2,1)}, u32[]{:S(2)}, u32[]{:S(2)}) collective-permute-start(bf16[128,1024]{1,0:T(8,128)(2,1)} %get-tuple-element.124.rest_5_), channel_id=1, source_target_pairs={{0,2},{2,0},{4,6},{6,4},{1,3},{3,1},{5,7},{7,5},{8,10},{10,8},{12,... | collective-permute-start | bytes 786440 | tf_op jit(solution)/shard_map/ppermute | solution.py:1111
  251.4 32.1 %collective-permute-start.20 = (bf16[128,1024]{1,0:T(8,128)(2,1)}, bf16[128,1024]{1,0:T(8,128)(2,1)}, u32[]{:S(2)}, u32[]{:S(2)}) collective-permute-start(bf16[128,1024]{1,0:T(8,128)(2,1)} %get-tuple-element.147.rest_5_), channel_id=1, source_target_pairs={{0,6},{2,4},{4,2},{6,0},{1,7},{3,5},{5,3},{7,1},{8,14},{10,12},{12... | collective-permute-start | bytes 786440 | tf_op jit(solution)/shard_map/ppermute | solution.py:1111
  254.7 28.9 %collective-permute-start.19 = (bf16[128,1024]{1,0:T(8,128)(2,1)}, bf16[128,1024]{1,0:T(8,128)(2,1)}, u32[]{:S(2)}, u32[]{:S(2)}) collective-permute-start(bf16[128,1024]{1,0:T(8,128)(2,1)} %get-tuple-element.147.rest_5_), channel_id=1, source_target_pairs={{0,4},{2,6},{4,0},{6,2},{1,5},{3,7},{5,1},{7,3},{8,12},{10,14},{12... | collective-permute-start | bytes 786440 | tf_op jit(solution)/shard_map/ppermute | solution.py:1111
  270.7 12.9 %collective-permute-start.18 = (bf16[128,1024]{1,0:T(8,128)(2,1)}, bf16[128,1024]{1,0:T(8,128)(2,1)S(1)}, u32[]{:S(2)}, u32[]{:S(2)}) collective-permute-start(bf16[128,1024]{1,0:T(8,128)(2,1)} %get-tuple-element.147.rest_5_), channel_id=1, source_target_pairs={{0,2},{2,0},{4,6},{6,4},{1,3},{3,1},{5,7},{7,5},{8,10},{10,8},{12,... | collective-permute-start | bytes 786440 | tf_op jit(solution)/shard_map/ppermute | solution.py:1111
  281.0 55.5 %collective-permute-start.8 = (bf16[512,512]{1,0:T(8,128)(2,1)S(1)}, bf16[512,512]{1,0:T(8,128)(2,1)S(1)}, u32[]{:S(2)}, u32[]{:S(2)}) collective-permute-start(bf16[512,512]{1,0:T(8,128)(2,1)S(1)} %get-tuple-element.128), channel_id=1, source_target_pairs={{8,0},{16,8},{24,16},{9,1},{17,9},{25,17},{10,2},{18,10},{26,18},{... | collective-permute-start | bytes 1572872 | tf_op jit(solution)/shard_map/ppermute | solution.py:1139
  282.3 54.2 %collective-permute-start.9 = (bf16[512,512]{1,0:T(8,128)(2,1)S(1)}, bf16[512,512]{1,0:T(8,128)(2,1)S(1)}, u32[]{:S(2)}, u32[]{:S(2)}) collective-permute-start(bf16[512,512]{1,0:T(8,128)(2,1)S(1)} %get-tuple-element.129), channel_id=1, source_target_pairs={{16,0},{24,8},{17,1},{25,9},{18,2},{26,10},{19,3},{27,11},{20,4},{... | collective-permute-start | bytes 1572872 | tf_op jit(solution)/shard_map/ppermute | solution.py:1139
  295.4 22.6 %collective-permute-start.21 = (bf16[512,512]{1,0:T(8,128)(2,1)S(1)}, bf16[512,512]{1,0:T(8,128)(2,1)S(1)}, u32[]{:S(2)}, u32[]{:S(2)}) collective-permute-start(bf16[512,512]{1,0:T(8,128)(2,1)S(1)} %get-tuple-element.150), channel_id=1, source_target_pairs={{0,8},{8,16},{16,24},{1,9},{9,17},{17,25},{2,10},{10,18},{18,26},{... | collective-permute-start | bytes 1572872 | tf_op jit(solution)/shard_map/ppermute | solution.py:1139
  303.5 27.1 %collective-permute-start.22 = (bf16[512,512]{1,0:T(8,128)(2,1)S(1)}, bf16[512,512]{1,0:T(8,128)(2,1)S(1)}, u32[]{:S(2)}, u32[]{:S(2)}) collective-permute-start(bf16[512,512]{1,0:T(8,128)(2,1)S(1)} %get-tuple-element.151), channel_id=1, source_target_pairs={{0,16},{8,24},{1,17},{9,25},{2,18},{10,26},{3,19},{11,27},{4,20},{... | collective-permute-start | bytes 1572872 | tf_op jit(solution)/shard_map/ppermute | solution.py:1139
  332.0 54.6 %collective-permute-start.25 = (bf16[128,1024]{1,0:T(8,128)(2,1)S(1)}, bf16[128,1024]{1,0:T(8,128)(2,1)S(1)}, u32[]{:S(2)}, u32[]{:S(2)}) collective-permute-start(bf16[128,1024]{1,0:T(8,128)(2,1)S(1)} %get-tuple-element.212), channel_id=1, source_target_pairs={{0,6},{2,4},{4,2},{6,0},{1,7},{3,5},{5,3},{7,1},{8,14},{10,12},{12... | collective-permute-start | bytes 786440 | tf_op jit(solution)/shard_map/ppermute | solution.py:1111
  334.5 55.9 %collective-permute-start.24 = (bf16[128,1024]{1,0:T(8,128)(2,1)S(1)}, bf16[128,1024]{1,0:T(8,128)(2,1)}, u32[]{:S(2)}, u32[]{:S(2)}) collective-permute-start(bf16[128,1024]{1,0:T(8,128)(2,1)S(1)} %get-tuple-element.213), channel_id=1, source_target_pairs={{0,4},{2,6},{4,0},{6,2},{1,5},{3,7},{5,1},{7,3},{8,12},{10,14},{12... | collective-permute-start | bytes 786440 | tf_op jit(solution)/shard_map/ppermute | solution.py:1111
  334.8 55.6 %collective-permute-start.23 = (bf16[128,1024]{1,0:T(8,128)(2,1)S(1)}, bf16[128,1024]{1,0:T(8,128)(2,1)}, u32[]{:S(2)}, u32[]{:S(2)}) collective-permute-start(bf16[128,1024]{1,0:T(8,128)(2,1)S(1)} %get-tuple-element.214), channel_id=1, source_target_pairs={{0,2},{2,0},{4,6},{6,4},{1,3},{3,1},{5,7},{7,5},{8,10},{10,8},{12,... | collective-permute-start | bytes 786440 | tf_op jit(solution)/shard_map/ppermute | solution.py:1111
  337.8 52.6 %collective-permute-start.12 = (bf16[128,1024]{1,0:T(8,128)(2,1)S(1)}, bf16[128,1024]{1,0:T(8,128)(2,1)}, u32[]{:S(2)}, u32[]{:S(2)}) collective-permute-start(bf16[128,1024]{1,0:T(8,128)(2,1)S(1)} %get-tuple-element.215), channel_id=1, source_target_pairs={{0,6},{2,4},{4,2},{6,0},{1,7},{3,5},{5,3},{7,1},{8,14},{10,12},{12... | collective-permute-start | bytes 786440 | tf_op jit(solution)/shard_map/ppermute | solution.py:1111
  340.3 57.1 %collective-permute-start.11 = (bf16[128,1024]{1,0:T(8,128)(2,1)S(1)}, bf16[128,1024]{1,0:T(8,128)(2,1)}, u32[]{:S(2)}, u32[]{:S(2)}) collective-permute-start(bf16[128,1024]{1,0:T(8,128)(2,1)S(1)} %get-tuple-element.216), channel_id=1, source_target_pairs={{0,4},{2,6},{4,0},{6,2},{1,5},{3,7},{5,1},{7,3},{8,12},{10,14},{12... | collective-permute-start | bytes 786440 | tf_op jit(solution)/shard_map/ppermute | solution.py:1111
  343.5 65.6 %copy-start.53 = (bf16[128,1024]{1,0:T(8,128)(2,1)S(1)}, bf16[128,1024]{1,0:T(8,128)(2,1)}, u32[]{:S(2)}) copy-start(bf16[128,1024]{1,0:T(8,128)(2,1)} %get-tuple-element.209.start_ref) | copy-start | bytes 786436
  343.5 65.6 %copy-start.67 = (f32[1024]{0:T(1024)S(1)}, f32[1024]{0:T(1024)}, u32[]{:S(2)}) copy-start(f32[1024]{0:T(1024)} %get-tuple-element.230) | copy-start | bytes 12292
  343.5 65.6 %copy-start.71 = (f32[128]{0:T(128)S(1)}, f32[128]{0:T(128)}, u32[]{:S(2)}) copy-start(f32[128]{0:T(128)} %add_rsqrt_fusion) | copy-start | bytes 1540
  343.5 65.7 %copy-start.72 = (f32[128]{0:T(128)S(1)}, f32[128]{0:T(128)}, u32[]{:S(2)}) copy-start(f32[128]{0:T(128)} %add_rsqrt_fusion.1) | copy-start | bytes 1540
  386.6 18.5 %collective-permute-start.10 = (bf16[128,1024]{1,0:T(8,128)(2,1)S(1)}, bf16[128,1024]{1,0:T(8,128)(2,1)S(1)}, u32[]{:S(2)}, u32[]{:S(2)}) collective-permute-start(bf16[128,1024]{1,0:T(8,128)(2,1)S(1)} %get-tuple-element.217), channel_id=1, source_target_pairs={{0,2},{2,0},{4,6},{6,4},{1,3},{3,1},{5,7},{7,5},{8,10},{10,8},{12,... | collective-permute-start | bytes 786440 | tf_op jit(solution)/shard_map/ppermute | solution.py:1111
  (69 other events, 485.4 us)
Sparse Core Ops, SparseCore 0:
  11.7 88.2 all-gather.1
  270.8 152.8 reduce-scatter.1
